TPU v7x, 32 devices: a whole 2x2x4 slice. The times are simulated.
32 devices in a mesh: groups: 2 (over y), row: 16 (over z, x, core).
Axes of the slice: x: 2, y: 2, z: 4, core: 2. Of those that a mesh axis runs over, the one named last changes fastest.
Arguments:
- homolog_activation: float32 [32, 512, 256], P('groups', 'row'), parts along dimension 0, may hold values from -6 to 6
- homolog_entry_valid: int32 [32, 512], P('groups', 'row'), parts along dimension 0, may hold values 0 or 1
- amino_valid_flags: int32 [1024], P(('groups', 'row')), parts along dimension 0, may hold values 0 or 1
- first_factor_weights: float32 [256, 32], replicated, may hold values from -0.375 to 0.375
- second_factor_weights: float32 [256, 32], replicated, may hold values from -0.375 to 0.375
- final_linear_weights: float32 [1024, 128], replicated, may hold values from -0.1875 to 0.1875
- couple_delta_deriv: float32 [1024, 512, 128], P(('groups', 'row')), parts along dimension 0, may hold values from -6 to 6
Outputs:
- alignment_grad: float32 [32, 512, 256], P('groups', 'row'), parts along dimension 0
- left_weight_grad: float32 [512, 32], P('groups'), parts along dimension 0
- right_weight_grad: float32 [512, 32], P('groups'), parts along dimension 0
- out_weight_grad: float32 [2048, 128], P('groups'), parts along dimension 0
There are 2 independent parts, one for each index of `groups`. A program takes and returns all parts, laid end to end along the dimension named above; an argument that names none is the same for every part. Nothing has to cross between parts.
All inputs are finite; a program needn't handle non-finite values. No bound on the sum of `homolog_entry_valid` or of `amino_valid_flags` on one device may be relied on, other than what follows from the above.
Results may differ from a plain program's by a relative error of at most 0.0003.
Values sent between devices are 32-bit elements; how exact they have to be, the bound alone decides.
No kernel may reach another device: no remote copies, remote signals or barrier semaphores. Data moves between devices by JAX's collectives and lax.ppermute only.
A program may use at most 128 MiB of HBM per device.

v0:
```python
import jax
import jax.numpy as jnp
from jax import lax
from jax.sharding import PartitionSpec as P

SPLIT_PIECES = lax.Precision.HIGHEST


def local(
    homolog_activation,
    homolog_entry_valid,
    amino_valid_flags,
    first_factor_weights,
    second_factor_weights,
    final_linear_weights,
    couple_delta_deriv,
):
    rows = couple_delta_deriv.shape[0]
    total = couple_delta_deriv.shape[1]
    homolog_number_here = homolog_activation.shape[0]
    width = first_factor_weights.shape[1]
    pair_width = final_linear_weights.shape[1]
    keep_mask = homolog_entry_valid.astype(jnp.float32).T
    present = amino_valid_flags.astype(jnp.float32)
    homolog_slice_here = jnp.transpose(homolog_activation, (1, 0, 2))
    first_factor_embed = (
        jnp.einsum("plg,gz->plz", homolog_slice_here, first_factor_weights, precision=SPLIT_PIECES)
        * keep_mask[:, :, None]
    )
    second_factor_embed = (
        jnp.einsum("plg,gz->plz", homolog_slice_here, second_factor_weights, precision=SPLIT_PIECES)
        * keep_mask[:, :, None]
    )
    right_flat, keep_all, present_all = (
        lax.all_gather(
            second_factor_embed.reshape(rows, homolog_number_here * width),
            "row",
            axis=0,
            tiled=True,
        ),
        lax.all_gather(keep_mask, "row", axis=0, tiled=True),
        lax.all_gather(present, "row", axis=0, tiled=True),
    )
    right_all = right_flat.reshape(total, homolog_number_here, width)
    count = jnp.dot(
        keep_mask, keep_all.T, precision=SPLIT_PIECES, preferred_element_type=jnp.float32
    )
    factor = present[:, None] * present_all[None, :] / jnp.maximum(count, 1.0)
    scaled = couple_delta_deriv * factor[:, :, None]
    w_three = final_linear_weights.reshape(width, width, pair_width)
    block = min(256, total)
    right_pieces = []
    for begin in range(0, total, block):
        piece = scaled[:, begin : begin + block]
        feats = jnp.einsum("rjk,abk->rjab", piece, w_three, precision=SPLIT_PIECES)
        right_pieces.append(
            jnp.einsum("rjab,rsa->jsb", feats, first_factor_embed, precision=SPLIT_PIECES)
        )
    carried = jnp.einsum("rjk,jsc->rsck", scaled, right_all, precision=SPLIT_PIECES)
    output_grad = jnp.einsum("rsa,rsck->ack", first_factor_embed, carried, precision=SPLIT_PIECES)
    first_factor_embed_deriv = jnp.einsum("rsck,ack->rsa", carried, w_three, precision=SPLIT_PIECES)
    right_terms = jnp.concatenate(right_pieces, axis=0)
    summed = lax.psum(right_terms, "row")
    second_factor_embed_deriv = lax.dynamic_slice_in_dim(
        summed, lax.axis_index("row") * rows, rows, 0
    )
    first_factor_embed_deriv = first_factor_embed_deriv * keep_mask[:, :, None]
    second_factor_embed_deriv = second_factor_embed_deriv * keep_mask[:, :, None]
    alignment_grad = jnp.einsum(
        "gyo,fo->ygf", first_factor_embed_deriv, first_factor_weights, precision=SPLIT_PIECES
    ) + jnp.einsum(
        "gyo,fo->ygf", second_factor_embed_deriv, second_factor_weights, precision=SPLIT_PIECES
    )
    first_operand_array = jnp.einsum(
        "dxb,dxo->bo", homolog_slice_here, first_factor_embed_deriv, precision=SPLIT_PIECES
    )
    second_operand_array = jnp.einsum(
        "dxb,dxo->bo", homolog_slice_here, second_factor_embed_deriv, precision=SPLIT_PIECES
    )
    output_grad_total, left_grad_total, right_grad_total = lax.psum(
        (output_grad.reshape(width * width, pair_width), first_operand_array, second_operand_array),
        "row",
    )
    return (alignment_grad, left_grad_total, right_grad_total, output_grad_total)


def solution(mesh):
    in_specs = (
        P("groups", "row", None),
        P("groups", "row"),
        P(("groups", "row")),
        P(),
        P(),
        P(),
        P(("groups", "row"), None, None),
    )
    out_specs = (P("groups", "row", None), P("groups", None), P("groups", None), P("groups", None))
    return jax.shard_map(local, mesh=mesh, in_specs=in_specs, out_specs=out_specs, check_vma=False)
```

profile of v0, /device:TPU:0, one launch (start us, length us, event | category | flops | bytes accessed | tf_op | source)
XLA Modules:
  0.0 451.3 jit_solution(17768828914577271759)
XLA Ops:
  7.2 0.7 convert_bitcast_fusion
  8.0 1.8 convolution_multiply_fusion.1
  9.8 0.8 reshape.24
  10.7 23.4 %all-gather = f32[16,32,16]{1,2,0:T(8,128)S(1)} all-gather(f32[1,32,16]{1,2,0:T(8,128)S(1)} %get-tuple-element.24), channel_id=1, replica_groups=mesh['groups'=2,'row'=16] {'row'}, dimensions={0}, use_global_device_ids=true | all-gather | bytes 34816 | tf_op jit(solution)/shard_map/all_gather | solution.py:41
  34.9 1.2 dynamic-slice
  36.8 0.8 convert_dynamic-update-slice_fusion
  37.6 29.9 %all-reduce = f32[512]{0:T(512)S(1)} all-reduce(f32[512]{0:T(512)S(1)} %convert_dynamic-update-slice_fusion), channel_id=1, replica_groups=mesh['groups'=2,'row'=16] {'row'}, use_global_device_ids=true, to_apply=%add | all-reduce | flops 512 | bytes 4096
  67.5 1.0 fusion.22
  68.5 5.3 %broadcast_multiply_fusion = f32[32,512,128]{2,1,0:T(8,128)S(1)} fusion(f32[32,512,128]{2,1,0:T(8,128)} %param.13, f32[32,512]{1,0:T(8,128)S(1)} %fusion.22), kind=kLoop, calls=%fused_computation.11 | loop fusion | flops 2097152 | bytes 16842752 | tf_op jit(solution)/shard_map/mul | solution.py:49
  73.8 30.6 %fusion.7 = f32[32,256,32,32]{1,2,0,3:T(8,128)} fusion(f32[32,512,128]{2,1,0:T(8,128)S(1)} %broadcast_multiply_fusion, f32[32,32,128,1]{2,1,0,3:T(8,128)S(1)} %bitcast.87), kind=kOutput, calls=%fused_computation.9 | convolution fusion | flops 12884901888 | bytes 38273024 | tf_op jit(solution)/shard_map/rjk,abk->rjab/dot_general | solution.py:55
  104.4 31.1 %fusion.6 = f32[32,256,32,32]{1,2,0,3:T(8,128)} fusion(f32[32,512,128]{2,1,0:T(8,128)S(1)} %broadcast_multiply_fusion, f32[32,32,128,1]{2,1,0,3:T(8,128)S(1)} %bitcast.88), kind=kOutput, calls=%fused_computation.7 | convolution fusion | flops 12884901888 | bytes 38273024 | tf_op jit(solution)/shard_map/rjk,abk->rjab/dot_general | solution.py:55
  135.5 0.8 fusion.18
  136.3 29.3 %convolution_bitcast_fusion.1 = f32[16,256,32]{1,0,2:T(8,128)} fusion(f32[32,16,32,1]{2,1,0,3:T(8,128)S(1)} %fusion.18, f32[32,256,32,32]{1,2,0,3:T(8,128)} %fusion.7), kind=kOutput, calls=%fused_computation.14 | convolution fusion | flops 1610612736 | bytes 34144256 | tf_op jit(solution)/shard_map/rjab,rsa->jsb/dot_general | solution.py:57
  165.6 2.4 copy.68
  168.1 29.5 %convolution_bitcast_fusion = f32[16,256,32]{1,0,2:T(8,128)} fusion(f32[32,16,32,1]{2,1,0,3:T(8,128)S(1)} %fusion.18, f32[32,256,32,32]{1,2,0,3:T(8,128)} %fusion.6), kind=kOutput, calls=%fused_computation.13 | convolution fusion | flops 1610612736 | bytes 34144256 | tf_op jit(solution)/shard_map/rjab,rsa->jsb/dot_general | solution.py:57
  197.6 3.6 copy.70
  201.2 3.8 pad_maximum_fusion
  205.0 1.6 copy.62
  206.6 16.1 %fusion.8 = f32[32,16,32,128]{3,2,0,1:T(8,128)S(1)} fusion(f32[512,16,32,1]{0,2,3,1:T(8,128)S(1)} %bitcast.91, f32[32,512,128]{2,1,0:T(8,128)} %copy-done.2), kind=kOutput, calls=%fused_computation.12 | convolution fusion | flops 12884901888 | bytes 17825792 | tf_op jit(solution)/shard_map/rjk,jsc->rsck/dot_general | solution.py:59
  222.7 3.2 copy-done.1
  225.9 9.4 %fusion.11 = f32[32,32,128]{2,0,1:T(8,128)S(1)} fusion(f32[32,16,32,1]{2,1,0,3:T(8,128)S(1)} %fusion.18, f32[32,16,32,128]{3,2,0,1:T(8,128)S(1)} %fusion.8), kind=kOutput, calls=%fused_computation.15 | convolution fusion | flops 805306368 | bytes 8978432 | tf_op jit(solution)/shard_map/rsa,rsck->ack/dot_general | solution.py:60
  235.4 1.1 copy.74
  236.5 14.4 %fusion.19 = f32[32,16,32]{2,1,0:T(8,128)S(1)} fusion(f32[32,16,32,128]{3,2,0,1:T(8,128)} %copy-done.1, f32[32,32,128]{2,1,0:T(8,128)S(1)} %bitcast.89, f32[32,16]{1,0:T(8,128)S(1)} %copy.61), kind=kOutput, calls=%fused_computation.22 | convolution fusion | flops 805322752 | bytes 8980480 | tf_op jit(solution)/shard_map/rsck,ack->rsa/dot_general | solution.py:61
  250.9 1.4 convolution_bitcast_fusion.3
  252.9 98.3 %all-reduce.8.cloned.1.call-done = (f32[512,16,32]{2,1,0:T(8,128)}, f32[1024,128]{1,0:T(8,128)}) async-done(((f32[512,16,32]{2,1,0:T(8,128)}, f32[1024,128]{1,0:T(8,128)}), (f32[512,16,32]{2,1,0:T(8,128)}, f32[1024,128]{1,0:T(8,128)})) %all-reduce.8.cloned.1.call-update) | async-done | bytes 1572880 | tf_op jit(solution)/shard_map/psum | solution.py:63
  351.2 2.4 convolution_bitcast_fusion.2
  353.6 1.6 fusion.14
  355.2 1.1 copy.75
  356.3 83.5 %all-reduce.6.cloned.1.call-done = (f32[256,32]{0,1:T(8,128)}, f32[256,32]{0,1:T(8,128)}) async-done(((f32[256,32]{0,1:T(8,128)}, f32[256,32]{0,1:T(8,128)}), (f32[256,32]{0,1:T(8,128)}, f32[256,32]{0,1:T(8,128)})) %all-reduce.6.cloned.1.call-update) | async-done | bytes 65552 | tf_op jit(solution)/shard_map/psum | solution.py:80
  439.9 1.4 copy.115
  441.2 1.4 copy.116
  442.6 1.9 copy.117
  (24 shorter events, 1.6 us)
Async XLA Ops:
  7.2 128.3 %copy-start = (f32[256,32]{0,1:T(8,128)S(1)}, f32[256,32]{0,1:T(8,128)}, u32[]{:S(2)}) copy-start(f32[256,32]{0,1:T(8,128)} %param.10) | copy-start | bytes 98308
  7.2 197.8 %all-gather.3.cloned.1.call-start = ((), (), s32[]{:S(2)}) async-start(), calls=%async_computation | async-start | bytes 1114112 | tf_op jit(solution)/shard_map/all_gather | solution.py:35
  10.6 340.6 %all-reduce.8.cloned.1.call-start = ((), (), s32[]{:S(2)}) async-start(), calls=%async_computation.2 | async-start | bytes 9437184 | tf_op jit(solution)/shard_map/psum | solution.py:63
  68.5 5.3 %copy-start.4 = (f32[1024,128]{1,0:T(8,128)S(1)}, f32[1024,128]{1,0:T(8,128)}, u32[]{:S(2)}) copy-start(f32[1024,128]{1,0:T(8,128)} %param.12) | copy-start | bytes 1572868
  73.8 30.7 %copy-start.2 = (f32[32,512,128]{2,1,0:T(8,128)}, f32[32,512,128]{2,1,0:T(8,128)S(1)}, u32[]{:S(2)}) copy-start(f32[32,512,128]{2,1,0:T(8,128)S(1)} %broadcast_multiply_fusion) | copy-start | bytes 25165828
  104.4 31.1 %copy-start.3 = (f32[16,32,256]{2,1,0:T(8,128)S(1)}, f32[16,32,256]{2,1,0:T(8,128)}, u32[]{:S(2)}) copy-start(f32[16,32,256]{2,1,0:T(8,128)} %param.7) | copy-start | bytes 1572868
  222.7 3.2 copy-start.1
  236.5 117.2 %copy-start.5 = (f32[256,32]{0,1:T(8,128)S(1)}, f32[256,32]{0,1:T(8,128)}, u32[]{:S(2)}) copy-start(f32[256,32]{0,1:T(8,128)} %param.11) | copy-start | bytes 98308
  236.5 203.4 %all-reduce.6.cloned.1.call-start = ((), (), s32[]{:S(2)}) async-start(), calls=%async_computation.1 | async-start | bytes 131072 | tf_op jit(solution)/shard_map/psum | solution.py:80
Sparse Core Ops, SparseCore 0:
  10.8 40.6 all-gather.2
  236.6 114.5 all-reduce.7
  355.3 84.5 all-reduce.5
where the time goes:
time: 460 us; the launch traced here: 451 us
  waiting for transfers between devices  182 us (40%)
  matrix products  170 us (37%)
  blocking collectives  53.4 us (12%)
  local copies, waits for them, and re-layouts  19.9 us (4%)
  between operations  14.8 us (3%)
  other arithmetic  11.2 us (2%)
    psum x1, waiting for transfers between devices, local(): summed = lax.psum(right_terms, 'row')  98.3 us
    psum x1, waiting for transfers between devices, local(): lax.psum((output_grad.reshape(width * width, pair_width), first_operand_a...  83.5 us
    dot_general x2, matrix products, local(): feats = jnp.einsum('rjk,abk->rjab', piece, w_three, precision=SPLIT_PIECES)  61.7 us
    dot_general x2, matrix products, local(): jnp.einsum('rjab,rsa->jsb', feats, first_factor_embed, precision=SPLIT_PI...  58.8 us
    unnamed x1, blocking collectives  29.9 us
    all_gather x1, blocking collectives, local(): lax.all_gather(keep_mask, 'row', axis=0, tiled=True)  23.4 us
    dot_general x1, matrix products, local(): jnp.einsum('rjk,jsc->rsck', scaled, right_all, precision=SPLIT_PIECES)  16.1 us
    dot_general x1, matrix products, local(): jnp.einsum('rsck,ack->rsa', carried, w_three, precision=SPLIT_PIECES)  14.4 us
  transfers between devices with their start and end apart: 3, of which 2 were waited for; matrix products, arithmetic and copies ran while one was open for 35% of the time, Pallas kernels for 0%

commit v1 on v0

v1 whole, which is shorter than its diff:
```python
import functools

import jax
import jax.numpy as jnp
from jax import lax
from jax.experimental import pallas as pl
from jax.experimental.pallas import tpu as pltpu
from jax.sharding import PartitionSpec as P

EXACT = lax.Precision.HIGHEST

F32, BF16 = jnp.float32, jnp.bfloat16
NT = (((1,), (1,)), ((), ()))
NN = (((1,), (0,)), ((), ()))
TN = (((0,), (0,)), ((), ()))

def split(x):
    hi = x.astype(BF16)
    return hi, (x - hi.astype(F32)).astype(BF16)

def split_outside(x):
    hi = lax.reduce_precision(x, 8, 7)
    return hi.astype(BF16), (x - hi).astype(BF16)


def dot(a, b, dims=NN):
    return lax.dot_general(a, b, dims, preferred_element_type=F32)

def params(mib, sem=None):
    return pltpu.CompilerParams(vmem_limit_bytes=mib << 20)

def t_kernel(lcat_ref, wcat_ref, thi_ref, tlo_ref, *, ib, s, w, k):
    t = dot(lcat_ref[...], wcat_ref[...])
    hi, lo = split(t)
    for i in range(ib):
        for b in range(w):
            thi_ref[b*s:(b+1)*s, i*k:(i+1)*k] = hi[i*s:(i+1)*s, b*k:(b+1)*k]
            tlo_ref[b*s:(b+1)*s, i*k:(i+1)*k] = lo[i*s:(i+1)*s, b*k:(b+1)*k]

def t_call(lcat, wcat, r, s, w, k, ib):
    return pl.pallas_call(
        functools.partial(t_kernel, ib=ib, s=s, w=w, k=k),
        grid=(r // ib,),
        in_specs=[pl.BlockSpec((ib*s, lcat.shape[1]), lambda g: (g, 0)),
                  pl.BlockSpec(wcat.shape, lambda g: (0, 0))],
        out_specs=[pl.BlockSpec((w*s, ib*k), lambda g: (0, g))]*2,
        out_shape=[jax.ShapeDtypeStruct((w*s, r*k), BF16)]*2,
        compiler_params=params(48), name="t_call")(lcat, wcat)

def g_block(me, d_ref, f_ref, offs, r, i, o):
    src = pl.multiple_of((me ^ offs[o]) * r, r)
    return d_ref[i, pl.ds(src, r), :] * f_ref[0, o*r:(o+1)*r, i:i+1]

def b_kernel(me_ref, d_ref, f_ref, thi_ref, tlo_ref, out_ref, ghi, glo, *, ib, offs, r, k, part, parts, chunk):
    me = me_ref[0]
    n = len(offs)
    per = n // parts
    @pl.when(pl.program_id(0) == 0)
    def _():
        out_ref[...] = jnp.zeros_like(out_ref)
    cb = chunk // r
    for c in range(per // cb):
        for q in range(cb):
            o = c*cb + q
            for i in range(ib):
                hi, lo = split(g_block(me, d_ref, f_ref, offs, r, i, part*per + o))
                ghi[o*r:(o+1)*r, i*k:(i+1)*k] = hi
                glo[o*r:(o+1)*r, i*k:(i+1)*k] = lo
        sl = slice(c*chunk, (c+1)*chunk)
        out_ref[sl] += (dot(ghi[sl], thi_ref[...], NT) + dot(ghi[sl], tlo_ref[...], NT) + dot(glo[sl], thi_ref[...], NT))

def b_call(me, d, ft, thi, tlo, offs, rb, ib, part, parts, chunk):
    r, total, k = d.shape
    ws = thi.shape[0]
    rows = total // parts
    return pl.pallas_call(
        functools.partial(b_kernel, ib=ib, offs=offs, r=rb, k=k, part=part, parts=parts, chunk=chunk),
        grid=(r // ib,),
        in_specs=[pl.BlockSpec(memory_space=pltpu.SMEM),
                  pl.BlockSpec((ib, total, k), lambda g: (g, 0, 0)),
                  pl.BlockSpec((1, total, ib), lambda g: (g, 0, 0)),
                  pl.BlockSpec((ws, ib*k), lambda g: (0, g)),
                  pl.BlockSpec((ws, ib*k), lambda g: (0, g))],
        out_specs=pl.BlockSpec((rows, ws), lambda g: (0, 0)),
        out_shape=jax.ShapeDtypeStruct((rows, ws), F32),
        scratch_shapes=[pltpu.VMEM((rows, ib*k), BF16)]*2,
        compiler_params=params(48), name=f"b_call{part}")(me, d, ft, thi, tlo)

def c_kernel(me_ref, d_ref, f_ref, rg_ref, whi_ref, wlo_ref, lt_ref, lg_ref, ow_ref, rhi, rlo, ghi, glo, xhi, xlo, *, ib, offs, r, s, w, k, chunk):
    me = me_ref[0]
    n = len(offs)
    @pl.when(pl.program_id(0) == 0)
    def _():
        ow_ref[...] = jnp.zeros_like(ow_ref)
        hi, lo = split(rg_ref[...].T)
        rhi[...] = hi
        rlo[...] = lo
    ci = chunk // k
    for c in range(ib // ci):
        for i in range(c*ci, (c+1)*ci):
            for o in range(n):
                hi, lo = split(g_block(me, d_ref, f_ref, offs, r, i, o))
                ghi[o*r:(o+1)*r, i*k:(i+1)*k] = hi
                glo[o*r:(o+1)*r, i*k:(i+1)*k] = lo
        sl = slice(c*chunk, (c+1)*chunk)
        c1 = dot(rhi[...], ghi[:, sl]) + dot(rhi[...], glo[:, sl]) + dot(rlo[...], ghi[:, sl])
        hi, lo = split(c1)
        for i in range(c*ci, (c+1)*ci):
            ii = i - c*ci
            for b in range(w):
                xhi[i*s:(i+1)*s, b*k:(b+1)*k] = hi[b*s:(b+1)*s, ii*k:(ii+1)*k]
                xlo[i*s:(i+1)*s, b*k:(b+1)*k] = lo[b*s:(b+1)*s, ii*k:(ii+1)*k]
    lg_ref[...] = dot(xhi[...], whi_ref[...], NT) + dot(xhi[...], wlo_ref[...], NT) + dot(xlo[...], whi_ref[...], NT)
    lhi, llo = split(lt_ref[0])
    ow_ref[...] += dot(lhi, xhi[...]) + dot(llo, xhi[...]) + dot(lhi, xlo[...])

def c_call(me, d, ft, rg, whi, wlo, lt, offs, rb, ib, s, chunk):
    r, total, k = d.shape
    w = whi.shape[0]
    ws = w*s
    return pl.pallas_call(
        functools.partial(c_kernel, ib=ib, offs=offs, r=rb, s=s, w=w, k=k, chunk=chunk),
        grid=(r // ib,),
        in_specs=[pl.BlockSpec(memory_space=pltpu.SMEM),
                  pl.BlockSpec((ib, total, k), lambda g: (g, 0, 0)),
                  pl.BlockSpec((1, total, ib), lambda g: (g, 0, 0)),
                  pl.BlockSpec((total, ws), lambda g: (0, 0)),
                  pl.BlockSpec((w, w*k), lambda g: (0, 0)),
                  pl.BlockSpec((w, w*k), lambda g: (0, 0)),
                  pl.BlockSpec((1, w, ib*s), lambda g: (g, 0, 0))],
        out_specs=[pl.BlockSpec((ib*s, w), lambda g: (g, 0)), pl.BlockSpec((w, w*k), lambda g: (0, 0))],
        out_shape=[jax.ShapeDtypeStruct((r*s, w), F32), jax.ShapeDtypeStruct((w, w*k), F32)],
        scratch_shapes=[pltpu.VMEM((ws, total), BF16)]*2 + [pltpu.VMEM((total, ib*k), BF16)]*2 + [pltpu.VMEM((ib*s, w*k), BF16)]*2,
        compiler_params=params(56), name="c_call")(me, d, ft, rg, whi, wlo, lt)


def swap(x, bit, n):
    return lax.ppermute(x, "row", [(i, i ^ bit) for i in range(n)])


def gather_relative(x, bits, n):
    for bit in bits:
        x = jnp.concatenate([x, swap(x, bit, n)], axis=0)
    return x


def relative_order(bits):
    offs = [0]
    for bit in bits:
        offs = offs + [o ^ bit for o in offs]
    return tuple(offs)


def local(n, activation, valid, flags, w1, w2, wf, delta):
    s, r, m = activation.shape
    total, k = delta.shape[1:]
    w = w1.shape[1]
    ib = min(8, r)
    groups = r // ib
    me = lax.axis_index("row").astype(jnp.int32)
    bits = [1 << e for e in reversed(range(n.bit_length() - 1))]
    offs = relative_order(bits)

    keep = valid.astype(F32)
    present = flags.astype(F32)
    masks = gather_relative(jnp.concatenate([keep.reshape(-1), present])[None], bits, n)
    keep_rel = masks[:, : s * r].reshape(n, s, r)
    present_rel = masks[:, s * r :].reshape(total)
    count = lax.dot_general(
        keep_rel.astype(BF16), keep.astype(BF16), (((1,), (0,)), ((), ())), preferred_element_type=F32
    ).reshape(total, r)
    ft = present_rel[:, None] * present[None, :] / jnp.maximum(count, 1.0)
    ft = ft.reshape(total, groups, ib).transpose(1, 0, 2)

    both = jnp.einsum("sim,mc->isc", activation, jnp.concatenate([w1, w2], axis=1), precision=EXACT)
    both = both * keep.T[:, :, None]
    left, right = both[:, :, :w], both[:, :, w:]
    right_own = right.transpose(0, 2, 1).reshape(1, r, w * s)
    right_rel = gather_relative(right_own, bits, n).reshape(total, w * s)

    wcat = wf.reshape(w, w * k)
    whi, wlo = split_outside(wcat)
    lflat = left.reshape(r * s, w)
    lhi, llo = split_outside(lflat)
    thi, tlo = t_call(
        jnp.concatenate([lhi, llo, lhi], axis=1), jnp.concatenate([whi, whi, wlo], axis=0), r, s, w, k, ib
    )

    if r % 16 == 0:
        where, rb, blocks = me.reshape(1), r, offs
    else:
        order = me ^ jnp.array(offs, jnp.int32)
        delta = jnp.take(delta.reshape(r, n, r, k), order, axis=1).reshape(r, total, k)
        rb = 128
        where, blocks = jnp.zeros((1,), jnp.int32), tuple(range(total // rb))

    far = b_call(where, delta, ft, thi, tlo, blocks, rb, ib, 1, 2, 256)
    near = b_call(where, delta, ft, thi, tlo, blocks, rb, ib, 0, 2, 256)

    quarter = w // 4
    places = (0, 2, 1, 3)
    turn = (me & 3) ^ jnp.array(places, jnp.int32)
    lt = jnp.take(lflat.T.reshape(4, quarter, r * s), turn, axis=0).reshape(w, groups, ib * s).transpose(1, 0, 2)
    left_grad, ow = c_call(where, delta, ft, right_rel, whi, wlo, lt, blocks, rb, ib, s, 256)

    grad = near + swap(far, 1, n)
    for bit in reversed(bits[:-1]):
        half = grad.shape[0] // 2
        grad = grad[:half] + swap(grad[half:], bit, n)
    half = w // 2
    ow = ow[:half] + swap(ow[half:], 1, n)
    ow = ow[:quarter] + swap(ow[quarter:], 2, n)
    for bit in reversed(bits[:-2]):
        ow = ow + swap(ow, bit, n)
    ow = jnp.concatenate([ow, swap(ow, 2, n)], axis=0)
    ow = jnp.concatenate([ow, swap(ow, 1, n)], axis=0)
    back = jnp.array(places, jnp.int32)[(me & 3) ^ jnp.arange(4, dtype=jnp.int32)]
    out_grad = jnp.take(ow.reshape(4, quarter, w * k), back, axis=0).reshape(w * w, k)

    right_grad = grad.reshape(r, w, s).transpose(2, 0, 1) * keep[:, :, None]
    left_grad = left_grad.reshape(r, s, w).transpose(1, 0, 2) * keep[:, :, None]
    grads = jnp.concatenate([left_grad, right_grad], axis=2)
    alignment = jnp.einsum("sic,mc->sim", grads, jnp.concatenate([w1, w2], axis=1), precision=EXACT)
    small = jnp.einsum("sim,sic->cm", activation, grads, precision=EXACT)
    for bit in reversed(bits):
        small = small + swap(small, bit, n)
    return alignment, small[:w].T, small[w:].T, out_grad


def solution(mesh):
    in_specs = (
        P("groups", "row", None),
        P("groups", "row"),
        P(("groups", "row")),
        P(),
        P(),
        P(),
        P(("groups", "row"), None, None),
    )
    out_specs = (P("groups", "row", None), P("groups", None), P("groups", None), P("groups", None))
    body = functools.partial(local, mesh.shape["row"])
    return jax.shard_map(body, mesh=mesh, in_specs=in_specs, out_specs=out_specs, check_vma=False)
```

time: 460 us -> 126 us (0.27); the launches traced: 451 us -> 126 us
  matrix products: 170 us -> 3.64 us
  waiting for transfers between devices: 182 us -> 42 us
  blocking collectives: 53.4 us -> 0 us
  Pallas kernels: 0 us -> 38.9 us
  starting transfers between devices: 0.12 us -> 21.7 us
  between operations: 14.8 us -> 1.2 us
  other arithmetic: 11.2 us -> 4.24 us
  local copies, waits for them, and re-layouts: 19.9 us -> 14.4 us
    psum x2 -> x0, waiting for transfers between devices: 182 us -> none  [the longest x1 98.3 us: local(): summed = lax.psum(right_terms, 'row')]
    dot_general x14 -> x4, matrix products: 170 us -> 3.64 us  [the longest x1 1.42 us: local(): jnp.einsum('sic,mc->sim', grads, jnp.concatenate([w1, w2], axis=1), preci...]
    ppermute x0 -> x22, waiting for transfers between devices: none -> 42 us  [swap(): return lax.ppermute(x, 'row', [(i, i ^ bit) for i in range(n)])]
    pallas_call x0 -> x4, Pallas kernels: none -> 38.9 us  [the longest x1 19.3 us: c_call(): pl.pallas_call(functools.partial(c_kernel, ib=ib, offs=offs, r=rb, s=s, w...]
    unnamed x1 -> x0, blocking collectives: 29.9 us -> none
    all_gather x1 -> x0, blocking collectives: 23.4 us -> none  [local(): lax.all_gather(keep_mask, 'row', axis=0, tiled=True)]
    ppermute x0 -> x22, starting transfers between devices: none -> 21.7 us  [swap(): return lax.ppermute(x, 'row', [(i, i ^ bit) for i in range(n)])]
    dot_general x3 -> x2, local copies, waits for them, and re-layouts: 7.12 us -> 0.14 us  [local(): lax.dot_general(keep_rel.astype(BF16), keep.astype(BF16), (((1,), (0,)),...]
  transfers between devices with their start and end apart: 3 -> 22, of which waited for: 2 -> 11; matrix products, arithmetic and copies ran while one was open for 35% -> 9% of each run, Pallas kernels for 0% -> 31%
where the time goes in v1:
time: 126 us
  waiting for transfers between devices  42 us (33%)
  Pallas kernels  38.9 us (31%)
  starting transfers between devices  21.7 us (17%)
  local copies, waits for them, and re-layouts  14.4 us (11%)
  other arithmetic  4.24 us (3%)
  matrix products  3.64 us (3%)
    ppermute x22, waiting for transfers between devices, swap(): return lax.ppermute(x, 'row', [(i, i ^ bit) for i in range(n)])  42 us
    ppermute x22, starting transfers between devices, swap(): return lax.ppermute(x, 'row', [(i, i ^ bit) for i in range(n)])  21.7 us
    pallas_call x1, Pallas kernels, c_call(): pl.pallas_call(functools.partial(c_kernel, ib=ib, offs=offs, r=rb, s=s, w...  19.3 us
    pallas_call x2, Pallas kernels, b_call(): pl.pallas_call(functools.partial(b_kernel, ib=ib, offs=offs, r=rb, k=k, p...  15.5 us
    unnamed x34, local copies, waits for them, and re-layouts  7.87 us
    pallas_call x1, Pallas kernels, t_call(): pl.pallas_call(functools.partial(t_kernel, ib=ib, s=s, w=w, k=k), grid=(r...  4.13 us
  transfers between devices with their start and end apart: 22, of which 11 were waited for; matrix products, arithmetic and copies ran while one was open for 9% of the time, Pallas kernels for 31%

profile of v1, /device:TPU:0, one launch (start us, length us, event | category | flops | bytes accessed | tf_op | source)
XLA Modules:
  0.0 126.1 jit_solution(17377035586967325561)
XLA Ops:
  0.7 0.7 convert_element_type.26
  1.4 0.7 convert_bitcast_fusion
  2.2 4.1 %collective-permute-start = (f32[1,544]{1,0:T(1,128)S(1)}, f32[1,544]{1,0:T(1,128)S(1)}, u32[]{:S(2)}, u32[]{:S(2)}) collective-permute-start(f32[1,544]{1,0:T(1,128)S(1)} %broadcast_in_dim.34), channel_id=1, source_target_pairs={{0,8},{1,9},{2,10},{3,11},{4,12},{5,13},{6,14},{7,15},{8,0},{9,1},... | collective-permute-start | bytes 6536 | tf_op jit(solution)/shard_map/ppermute | solution.py:138
  6.3 1.3 %fusion = f32[32,16,64]{2,0,1:T(8,128)S(1)} fusion(f32[16,32,256]{2,1,0:T(8,128)S(1)} %copy-done, f32[32,16]{0,1:T(8,128)S(1)} %get-tuple-element.24, f32[256,32]{0,1:T(8,128)} %param.13, f32[256,32]{0,1:T(8,128)} %param.12), kind=kOutput, calls=%fused_computation.4 | convolution fusion | flops 100712448 | bytes 722944 | tf_op jit(solution)/shard_map/sim,mc->isc/dot_general | solution.py:175
  8.5 2.0 %collective-permute-start.1 = (f32[2,544]{1,0:T(2,128)S(1)}, f32[2,544]{1,0:T(2,128)S(1)}, u32[]{:S(2)}, u32[]{:S(2)}) collective-permute-start(f32[2,544]{1,0:T(2,128)S(1)} %pad_maximum_fusion.11), channel_id=1, source_target_pairs={{0,4},{1,5},{2,6},{3,7},{4,0},{5,1},{6,2},{7,3},{8,12},{9,13},{10,... | collective-permute-start | bytes 13064 | tf_op jit(solution)/shard_map/ppermute | solution.py:138
  10.5 3.2 %collective-permute-done.1 = f32[2,544]{1,0:T(2,128)S(1)} collective-permute-done((f32[2,544]{1,0:T(2,128)S(1)}, f32[2,544]{1,0:T(2,128)S(1)}, u32[]{:S(2)}, u32[]{:S(2)}) %collective-permute-start.1) | collective-permute-done | bytes 4384 | tf_op jit(solution)/shard_map/ppermute | solution.py:138
  13.8 1.6 %collective-permute-start.2 = (f32[4,544]{1,0:T(4,128)S(1)}, f32[4,544]{1,0:T(4,128)S(1)}, u32[]{:S(2)}, u32[]{:S(2)}) collective-permute-start(f32[4,544]{1,0:T(4,128)S(1)} %pad_maximum_fusion.10), channel_id=1, source_target_pairs={{0,2},{1,3},{2,0},{3,1},{4,6},{5,7},{6,4},{7,5},{8,10},{9,11},{10,... | collective-permute-start | bytes 26120 | tf_op jit(solution)/shard_map/ppermute | solution.py:138
  15.4 2.1 %collective-permute-done.2 = f32[4,544]{1,0:T(4,128)S(1)} collective-permute-done((f32[4,544]{1,0:T(4,128)S(1)}, f32[4,544]{1,0:T(4,128)S(1)}, u32[]{:S(2)}, u32[]{:S(2)}) %collective-permute-start.2) | collective-permute-done | bytes 8736 | tf_op jit(solution)/shard_map/ppermute | solution.py:138
  17.9 4.1 %t_call.1 = (bf16[512,4096]{1,0:T(8,128)(2,1)S(1)}, bf16[512,4096]{1,0:T(8,128)(2,1)}) custom-call(bf16[512,96]{1,0:T(8,128)(2,1)S(1)} %pad_maximum_fusion.6.lcat_ref, bf16[96,4096]{1,0:T(8,128)(2,1)S(1)} %pad_maximum_fusion.wcat_ref), custom_call_target="tpu_custom_call" | custom-call | tf_op jit(solution)/shard_map/t_call/pallas_call | solution.py:41
  22.0 2.0 %copy-done.1 = bf16[512,4096]{1,0:T(8,128)(2,1)} copy-done((bf16[512,4096]{1,0:T(8,128)(2,1)}, bf16[512,4096]{1,0:T(8,128)(2,1)S(1)}, u32[]{:S(2)}) %copy-start.1) | copy-done | bytes 4194328
  25.0 2.6 %copy-done.2 = bf16[512,4096]{1,0:T(8,128)(2,1)S(1)} copy-done((bf16[512,4096]{1,0:T(8,128)(2,1)S(1)}, bf16[512,4096]{1,0:T(8,128)(2,1)}, u32[]{:S(2)}) %copy-start.2) | copy-done | bytes 4194328
  27.6 7.7 %b_call1.1 = f32[256,512]{1,0:T(8,128)S(1)} custom-call(s32[1]{0:T(128)} %bitcast.me_ref, f32[32,512,128]{2,1,0:T(8,128)} %d_ref.5, f32[4,512,8]{2,1,0:T(8,128)S(1)} %bitcast.52, bf16[512,4096]{1,0:T(8,128)(2,1)S(1)} %copy-done.2, bf16[512,4096]{1,0:T(8,128)(2,1)} %get-tuple-element.10.tlo_ref), custom_call_target="tpu_custom_call" | custom-call | tf_op jit(solution)/shard_map/b_call1/pallas_call | solution.py:76
  36.0 2.5 %collective-permute-start.5 = (f32[2,32,512]{2,1,0:T(8,128)S(1)}, f32[2,32,512]{2,1,0:T(8,128)S(1)}, u32[]{:S(2)}, u32[]{:S(2)}) collective-permute-start(f32[2,32,512]{2,1,0:T(8,128)S(1)} %pad_maximum_fusion.5), channel_id=1, source_target_pairs={{0,4},{1,5},{2,6},{3,7},{4,0},{5,1},{6,2},{7,3},{8,12},{9,13},{10,... | collective-permute-start | bytes 393224 | tf_op jit(solution)/shard_map/ppermute | solution.py:138
  39.4 2.8 %collective-permute-done.5 = f32[2,32,512]{2,1,0:T(8,128)S(1)} collective-permute-done((f32[2,32,512]{2,1,0:T(8,128)S(1)}, f32[2,32,512]{2,1,0:T(8,128)S(1)}, u32[]{:S(2)}, u32[]{:S(2)}) %collective-permute-start.5) | collective-permute-done | bytes 131104 | tf_op jit(solution)/shard_map/ppermute | solution.py:138
  42.2 1.6 %collective-permute-start.6 = (f32[4,32,512]{2,1,0:T(8,128)S(1)}, f32[4,32,512]{2,1,0:T(8,128)S(1)}, u32[]{:S(2)}, u32[]{:S(2)}) collective-permute-start(f32[4,32,512]{2,1,0:T(8,128)S(1)} %pad_maximum_fusion.2), channel_id=1, source_target_pairs={{0,2},{1,3},{2,0},{3,1},{4,6},{5,7},{6,4},{7,5},{8,10},{9,11},{10,... | collective-permute-start | bytes 786440 | tf_op jit(solution)/shard_map/ppermute | solution.py:138
  44.5 2.2 %copy-done.3 = bf16[512,4096]{1,0:T(8,128)(2,1)S(1)} copy-done((bf16[512,4096]{1,0:T(8,128)(2,1)S(1)}, bf16[512,4096]{1,0:T(8,128)(2,1)}, u32[]{:S(2)}) %copy-start.3) | copy-done | bytes 4194328
  46.7 7.7 %b_call0.1 = f32[256,512]{1,0:T(8,128)S(1)} custom-call(s32[1]{0:T(128)} %bitcast.me_ref, f32[32,512,128]{2,1,0:T(8,128)} %d_ref.5, f32[4,512,8]{2,1,0:T(8,128)S(1)} %bitcast.53, bf16[512,4096]{1,0:T(8,128)(2,1)S(1)} %copy-done.3, bf16[512,4096]{1,0:T(8,128)(2,1)} %get-tuple-element.10.tlo_ref), custom_call_target="tpu_custom_call" | custom-call | tf_op jit(solution)/shard_map/b_call0/pallas_call | solution.py:76
  54.5 1.1 add.66
  56.3 6.8 %collective-permute-done.9 = f32[128,512]{1,0:T(8,128)S(1)} collective-permute-done((f32[128,512]{1,0:T(8,128)S(1)}, f32[128,512]{1,0:T(8,128)S(1)}, u32[]{:S(2)}, u32[]{:S(2)}) %collective-permute-start.9) | collective-permute-done | bytes 262176 | tf_op jit(solution)/shard_map/ppermute | solution.py:138
  63.2 1.5 %collective-permute-start.10 = (f32[64,512]{1,0:T(8,128)S(1)}, f32[64,512]{1,0:T(8,128)S(1)}, u32[]{:S(2)}, u32[]{:S(2)}) collective-permute-start(f32[64,512]{1,0:T(8,128)S(1)} %slice.78), channel_id=1, source_target_pairs={{0,4},{1,5},{2,6},{3,7},{4,0},{5,1},{6,2},{7,3},{8,12},{9,13},{10,... | collective-permute-start | bytes 393224 | tf_op jit(solution)/shard_map/ppermute | solution.py:138
  64.7 3.5 %collective-permute-done.10 = f32[64,512]{1,0:T(8,128)S(1)} collective-permute-done((f32[64,512]{1,0:T(8,128)S(1)}, f32[64,512]{1,0:T(8,128)S(1)}, u32[]{:S(2)}, u32[]{:S(2)}) %collective-permute-start.10) | collective-permute-done | bytes 131104 | tf_op jit(solution)/shard_map/ppermute | solution.py:138
  68.2 4.3 %collective-permute-start.11 = (f32[32,512]{1,0:T(8,128)S(1)}, f32[32,512]{1,0:T(8,128)S(1)}, u32[]{:S(2)}, u32[]{:S(2)}) collective-permute-start(f32[32,512]{1,0:T(8,128)S(1)} %slice.80), channel_id=1, source_target_pairs={{0,8},{1,9},{2,10},{3,11},{4,12},{5,13},{6,14},{7,15},{8,0},{9,1},... | collective-permute-start | bytes 196616 | tf_op jit(solution)/shard_map/ppermute | solution.py:138
  72.6 1.0 copy-done.8
  73.6 19.3 %c_call.1 = (f32[512,32]{1,0:T(8,128)}, f32[32,4096]{1,0:T(8,128)}) custom-call(s32[1]{0:T(128)} %bitcast.me_ref, f32[32,512,128]{2,1,0:T(8,128)} %d_ref.5, f32[4,512,8]{2,1,0:T(8,128)} %bitcast.54, f32[512,512]{1,0:T(8,128)} %bitcast.56, bf16[32,4096]{1,0:T(8,128)(2,1)} %copy-done.6, bf16[32,4096]{1,0:T(8,128)(2,1)} %copy-done.7, f32[4,32,128]{2,1,0:T(8,128)} %fusion.4.lt_ref), custom_call_target="tpu_custom_call" | custom-call | tf_op jit(solution)/shard_map/c_call/pallas_call | solution.py:121
  93.0 1.0 slice.62
  96.5 4.8 %collective-permute-done.17 = f32[8,4096]{1,0:T(8,128)S(1)} collective-permute-done((f32[8,4096]{1,0:T(8,128)S(1)}, f32[8,4096]{1,0:T(8,128)S(1)}, u32[]{:S(2)}, u32[]{:S(2)}) %collective-permute-start.17) | collective-permute-done | bytes 131104 | tf_op jit(solution)/shard_map/ppermute | solution.py:138
  102.2 4.2 %collective-permute-done.18 = f32[8,4096]{1,0:T(8,128)S(1)} collective-permute-done((f32[8,4096]{1,0:T(8,128)S(1)}, f32[8,4096]{1,0:T(8,128)S(1)}, u32[]{:S(2)}, u32[]{:S(2)}) %collective-permute-start.18) | collective-permute-done | bytes 131104 | tf_op jit(solution)/shard_map/ppermute | solution.py:138
  107.1 6.3 %collective-permute-done.19 = f32[8,4096]{1,0:T(8,128)S(1)} collective-permute-done((f32[8,4096]{1,0:T(8,128)S(1)}, f32[8,4096]{1,0:T(8,128)S(1)}, u32[]{:S(2)}, u32[]{:S(2)}) %collective-permute-start.19) | collective-permute-done | bytes 131104 | tf_op jit(solution)/shard_map/ppermute | solution.py:138
  114.2 4.2 %collective-permute-done.14 = f32[64,256]{1,0:T(8,128)S(1)} collective-permute-done((f32[64,256]{1,0:T(8,128)S(1)}, f32[64,256]{1,0:T(8,128)S(1)}, u32[]{:S(2)}, u32[]{:S(2)}) %collective-permute-start.14) | collective-permute-done | bytes 65568 | tf_op jit(solution)/shard_map/ppermute | solution.py:138
  119.0 1.4 %fusion.3 = f32[16,32,256]{2,1,0:T(8,128)} fusion(f32[16,32,32]{2,1,0:T(8,128)S(1)} %get-tuple-element.23, f32[16,32,32]{2,1,0:T(8,128)S(1)} %get-tuple-element.22, f32[256,32]{0,1:T(8,128)S(1)} %copy-done.12, f32[256,32]{0,1:T(8,128)S(1)} %copy-done.13), kind=kOutput, calls=%fused_computation.29 | convolution fusion | flops 100712448 | bytes 720896 | tf_op jit(solution)/shard_map/sic,mc->sim/dot_general | solution.py:223
  120.4 3.4 %collective-permute-done.15 = f32[64,256]{1,0:T(8,128)S(1)} collective-permute-done((f32[64,256]{1,0:T(8,128)S(1)}, f32[64,256]{1,0:T(8,128)S(1)}, u32[]{:S(2)}, u32[]{:S(2)}) %collective-permute-start.15) | collective-permute-done | bytes 65568 | tf_op jit(solution)/shard_map/ppermute | solution.py:138
  125.2 0.9 select_n.49
  (123 shorter events, 11.9 us)
Async XLA Ops:
  0.6 5.7 %copy-start = (f32[16,32,256]{2,1,0:T(8,128)S(1)}, f32[16,32,256]{2,1,0:T(8,128)}, u32[]{:S(2)}) copy-start(f32[16,32,256]{2,1,0:T(8,128)} %param.9) | copy-start | bytes 1572868
  0.6 7.4 %copy-start.10 = (f32[1024,128]{1,0:T(8,128)S(1)}, f32[1024,128]{1,0:T(8,128)}, u32[]{:S(2)}) copy-start(f32[1024,128]{1,0:T(8,128)} %param.14) | copy-start | bytes 1572868
  2.2 6.3 %collective-permute-start = (f32[1,544]{1,0:T(1,128)S(1)}, f32[1,544]{1,0:T(1,128)S(1)}, u32[]{:S(2)}, u32[]{:S(2)}) collective-permute-start(f32[1,544]{1,0:T(1,128)S(1)} %broadcast_in_dim.34), channel_id=1, source_target_pairs={{0,8},{1,9},{2,10},{3,11},{4,12},{5,13},{6,14},{7,15},{8,0},{9,1},... | collective-permute-start | bytes 6536 | tf_op jit(solution)/shard_map/ppermute | solution.py:138
  8.0 27.9 %collective-permute-start.4 = (f32[1,32,512]{1,2,0:T(8,128)S(1)}, f32[1,32,512]{1,2,0:T(8,128)S(1)}, u32[]{:S(2)}, u32[]{:S(2)}) collective-permute-start(f32[1,32,512]{1,2,0:T(8,128)S(1)} %bitcast.57), channel_id=1, source_target_pairs={{0,8},{1,9},{2,10},{3,11},{4,12},{5,13},{6,14},{7,15},{8,0},{9,1},... | collective-permute-start | bytes 196616 | tf_op jit(solution)/shard_map/ppermute | solution.py:138
  8.2 7.2 %copy-start.5 = (s32[4]{0:T(128)S(1)}, s32[4]{0:T(128)}, u32[]{:S(2)}) copy-start(s32[4]{0:T(128)} %constant.39.clone) | copy-start | bytes 52
  8.2 9.6 %copy-start.6 = (bf16[32,4096]{1,0:T(8,128)(2,1)}, bf16[32,4096]{1,0:T(8,128)(2,1)S(1)}, u32[]{:S(2)}) copy-start(bf16[32,4096]{1,0:T(8,128)(2,1)S(1)} %get-tuple-element.14.whi_ref) | copy-start | bytes 786436
  8.3 9.6 %copy-start.7 = (bf16[32,4096]{1,0:T(8,128)(2,1)}, bf16[32,4096]{1,0:T(8,128)(2,1)S(1)}, u32[]{:S(2)}) copy-start(bf16[32,4096]{1,0:T(8,128)(2,1)S(1)} %get-tuple-element.15.wlo_ref) | copy-start | bytes 786436
  8.3 16.1 %copy-start.14 = (s32[16,32]{1,0:T(8,128)S(1)}, s32[16,32]{1,0:T(8,128)}, u32[]{:S(2)}) copy-start(s32[16,32]{1,0:T(8,128)} %param.10) | copy-start | bytes 6148
  8.5 5.2 %collective-permute-start.1 = (f32[2,544]{1,0:T(2,128)S(1)}, f32[2,544]{1,0:T(2,128)S(1)}, u32[]{:S(2)}, u32[]{:S(2)}) collective-permute-start(f32[2,544]{1,0:T(2,128)S(1)} %pad_maximum_fusion.11), channel_id=1, source_target_pairs={{0,4},{1,5},{2,6},{3,7},{4,0},{5,1},{6,2},{7,3},{8,12},{9,13},{10,... | collective-permute-start | bytes 13064 | tf_op jit(solution)/shard_map/ppermute | solution.py:138
  13.8 3.7 %collective-permute-start.2 = (f32[4,544]{1,0:T(4,128)S(1)}, f32[4,544]{1,0:T(4,128)S(1)}, u32[]{:S(2)}, u32[]{:S(2)}) collective-permute-start(f32[4,544]{1,0:T(4,128)S(1)} %pad_maximum_fusion.10), channel_id=1, source_target_pairs={{0,2},{1,3},{2,0},{3,1},{4,6},{5,7},{6,4},{7,5},{8,10},{9,11},{10,... | collective-permute-start | bytes 26120 | tf_op jit(solution)/shard_map/ppermute | solution.py:138
  17.5 6.5 %collective-permute-start.3 = (f32[8,544]{1,0:T(8,128)S(1)}, f32[8,544]{1,0:T(8,128)S(1)}, u32[]{:S(2)}, u32[]{:S(2)}) collective-permute-start(f32[8,544]{1,0:T(8,128)S(1)} %pad_maximum_fusion.9), channel_id=1, source_target_pairs={{0,1},{1,0},{2,3},{3,2},{4,5},{5,4},{6,7},{7,6},{8,9},{9,8},{10,11... | collective-permute-start | bytes 52232 | tf_op jit(solution)/shard_map/ppermute | solution.py:138
  25.0 19.5 %copy-start.4 = (f32[512,4,8]{2,0,1:T(8,128)}, f32[512,4,8]{2,0,1:T(8,128)S(1)}, u32[]{:S(2)}) copy-start(f32[512,4,8]{2,0,1:T(8,128)S(1)} %copy.36) | copy-start | bytes 196612
  35.3 19.2 %collective-permute-start.8 = (f32[256,512]{1,0:T(8,128)S(1)}, f32[256,512]{1,0:T(8,128)}, u32[]{:S(2)}, u32[]{:S(2)}) collective-permute-start(f32[256,512]{1,0:T(8,128)S(1)} %b_call1.1), channel_id=1, source_target_pairs={{0,1},{1,0},{2,3},{3,2},{4,5},{5,4},{6,7},{7,6},{8,9},{9,8},{10,11... | collective-permute-start | bytes 1572872 | tf_op jit(solution)/shard_map/ppermute | solution.py:138
  36.0 6.2 %collective-permute-start.5 = (f32[2,32,512]{2,1,0:T(8,128)S(1)}, f32[2,32,512]{2,1,0:T(8,128)S(1)}, u32[]{:S(2)}, u32[]{:S(2)}) collective-permute-start(f32[2,32,512]{2,1,0:T(8,128)S(1)} %pad_maximum_fusion.5), channel_id=1, source_target_pairs={{0,4},{1,5},{2,6},{3,7},{4,0},{5,1},{6,2},{7,3},{8,12},{9,13},{10,... | collective-permute-start | bytes 393224 | tf_op jit(solution)/shard_map/ppermute | solution.py:138
  42.2 14.0 %collective-permute-start.6 = (f32[4,32,512]{2,1,0:T(8,128)S(1)}, f32[4,32,512]{2,1,0:T(8,128)S(1)}, u32[]{:S(2)}, u32[]{:S(2)}) collective-permute-start(f32[4,32,512]{2,1,0:T(8,128)S(1)} %pad_maximum_fusion.2), channel_id=1, source_target_pairs={{0,2},{1,3},{2,0},{3,1},{4,6},{5,7},{6,4},{7,5},{8,10},{9,11},{10,... | collective-permute-start | bytes 786440 | tf_op jit(solution)/shard_map/ppermute | solution.py:138
  55.6 7.5 %collective-permute-start.9 = (f32[128,512]{1,0:T(8,128)S(1)}, f32[128,512]{1,0:T(8,128)S(1)}, u32[]{:S(2)}, u32[]{:S(2)}) collective-permute-start(f32[128,512]{1,0:T(8,128)S(1)} %slice.76), channel_id=1, source_target_pairs={{0,2},{1,3},{2,0},{3,1},{4,6},{5,7},{6,4},{7,5},{8,10},{9,11},{10,... | collective-permute-start | bytes 786440 | tf_op jit(solution)/shard_map/ppermute | solution.py:138
  56.2 16.3 %collective-permute-start.7 = (f32[8,32,512]{2,1,0:T(8,128)S(1)}, f32[8,32,512]{2,1,0:T(8,128)S(1)}, u32[]{:S(2)}, u32[]{:S(2)}) collective-permute-start(f32[8,32,512]{2,1,0:T(8,128)S(1)} %pad_maximum_fusion.1), channel_id=1, source_target_pairs={{0,1},{1,0},{2,3},{3,2},{4,5},{5,4},{6,7},{7,6},{8,9},{9,8},{10,11... | collective-permute-start | bytes 1572872 | tf_op jit(solution)/shard_map/ppermute | solution.py:138
  63.2 5.0 %collective-permute-start.10 = (f32[64,512]{1,0:T(8,128)S(1)}, f32[64,512]{1,0:T(8,128)S(1)}, u32[]{:S(2)}, u32[]{:S(2)}) collective-permute-start(f32[64,512]{1,0:T(8,128)S(1)} %slice.78), channel_id=1, source_target_pairs={{0,4},{1,5},{2,6},{3,7},{4,0},{5,1},{6,2},{7,3},{8,12},{9,13},{10,... | collective-permute-start | bytes 393224 | tf_op jit(solution)/shard_map/ppermute | solution.py:138
  68.2 26.5 %collective-permute-start.11 = (f32[32,512]{1,0:T(8,128)S(1)}, f32[32,512]{1,0:T(8,128)S(1)}, u32[]{:S(2)}, u32[]{:S(2)}) collective-permute-start(f32[32,512]{1,0:T(8,128)S(1)} %slice.80), channel_id=1, source_target_pairs={{0,8},{1,9},{2,10},{3,11},{4,12},{5,13},{6,14},{7,15},{8,0},{9,1},... | collective-permute-start | bytes 196616 | tf_op jit(solution)/shard_map/ppermute | solution.py:138
  93.0 3.3 %copy-start.11 = (f32[512,32]{1,0:T(8,128)S(1)}, f32[512,32]{1,0:T(8,128)}, u32[]{:S(2)}) copy-start(f32[512,32]{1,0:T(8,128)} %get-tuple-element.8) | copy-start | bytes 196612
  94.0 1.6 %collective-permute-start.16 = (f32[16,4096]{1,0:T(8,128)S(1)}, f32[16,4096]{1,0:T(8,128)S(1)}, u32[]{:S(2)}, u32[]{:S(2)}) collective-permute-start(f32[16,4096]{1,0:T(8,128)S(1)} %slice.62), channel_id=1, source_target_pairs={{0,1},{1,0},{2,3},{3,2},{4,5},{5,4},{6,7},{7,6},{8,9},{9,8},{10,11... | collective-permute-start | bytes 786440 | tf_op jit(solution)/shard_map/ppermute | solution.py:138
  95.7 5.6 %collective-permute-start.17 = (f32[8,4096]{1,0:T(8,128)S(1)}, f32[8,4096]{1,0:T(8,128)S(1)}, u32[]{:S(2)}, u32[]{:S(2)}) collective-permute-start(f32[8,4096]{1,0:T(8,128)S(1)} %slice.84), channel_id=1, source_target_pairs={{0,2},{1,3},{2,0},{3,1},{4,6},{5,7},{6,4},{7,5},{8,10},{9,11},{10,... | collective-permute-start | bytes 393224 | tf_op jit(solution)/shard_map/ppermute | solution.py:138
  101.3 17.7 %copy-start.12 = (f32[256,32]{0,1:T(8,128)S(1)}, f32[256,32]{0,1:T(8,128)}, u32[]{:S(2)}) copy-start(f32[256,32]{0,1:T(8,128)} %param.13) | copy-start | bytes 98308
  101.3 17.7 %copy-start.13 = (f32[256,32]{0,1:T(8,128)S(1)}, f32[256,32]{0,1:T(8,128)}, u32[]{:S(2)}) copy-start(f32[256,32]{0,1:T(8,128)} %param.12) | copy-start | bytes 98308
  101.3 5.0 %collective-permute-start.18 = (f32[8,4096]{1,0:T(8,128)S(1)}, f32[8,4096]{1,0:T(8,128)S(1)}, u32[]{:S(2)}, u32[]{:S(2)}) collective-permute-start(f32[8,4096]{1,0:T(8,128)S(1)} %slice_add_fusion.2), channel_id=1, source_target_pairs={{0,4},{1,5},{2,6},{3,7},{4,0},{5,1},{6,2},{7,3},{8,12},{9,13},{10,... | collective-permute-start | bytes 393224 | tf_op jit(solution)/shard_map/ppermute | solution.py:138
  102.1 4.4 %collective-permute-start.12 = (f32[64,256]{1,0:T(8,128)S(1)}, f32[64,256]{1,0:T(8,128)S(1)}, u32[]{:S(2)}, u32[]{:S(2)}) collective-permute-start(f32[64,256]{1,0:T(8,128)S(1)} %convolution_bitcast_fusion.1), channel_id=1, source_target_pairs={{0,1},{1,0},{2,3},{3,2},{4,5},{5,4},{6,7},{7,6},{8,9},{9,8},{10,11... | collective-permute-start | bytes 196616 | tf_op jit(solution)/shard_map/ppermute | solution.py:138
  106.4 7.1 %collective-permute-start.19 = (f32[8,4096]{1,0:T(8,128)S(1)}, f32[8,4096]{1,0:T(8,128)S(1)}, u32[]{:S(2)}, u32[]{:S(2)}) collective-permute-start(f32[8,4096]{1,0:T(8,128)S(1)} %add.78), channel_id=1, source_target_pairs={{0,8},{1,9},{2,10},{3,11},{4,12},{5,13},{6,14},{7,15},{8,0},{9,1},... | collective-permute-start | bytes 393224 | tf_op jit(solution)/shard_map/ppermute | solution.py:138
  106.5 7.6 %collective-permute-start.13 = (f32[64,256]{1,0:T(8,128)S(1)}, f32[64,256]{1,0:T(8,128)S(1)}, u32[]{:S(2)}, u32[]{:S(2)}) collective-permute-start(f32[64,256]{1,0:T(8,128)S(1)} %add.70), channel_id=1, source_target_pairs={{0,2},{1,3},{2,0},{3,1},{4,6},{5,7},{6,4},{7,5},{8,10},{9,11},{10,... | collective-permute-start | bytes 196616 | tf_op jit(solution)/shard_map/ppermute | solution.py:138
  113.4 5.4 %collective-permute-start.20 = (f32[8,4096]{1,0:T(8,128)S(1)}, f32[8,4096]{1,0:T(8,128)S(1)}, u32[]{:S(2)}, u32[]{:S(2)}) collective-permute-start(f32[8,4096]{1,0:T(8,128)S(1)} %add.79), channel_id=1, source_target_pairs={{0,2},{1,3},{2,0},{3,1},{4,6},{5,7},{6,4},{7,5},{8,10},{9,11},{10,... | collective-permute-start | bytes 393224 | tf_op jit(solution)/shard_map/ppermute | solution.py:138
  114.1 4.3 %collective-permute-start.14 = (f32[64,256]{1,0:T(8,128)S(1)}, f32[64,256]{1,0:T(8,128)S(1)}, u32[]{:S(2)}, u32[]{:S(2)}) collective-permute-start(f32[64,256]{1,0:T(8,128)S(1)} %add.71), channel_id=1, source_target_pairs={{0,4},{1,5},{2,6},{3,7},{4,0},{5,1},{6,2},{7,3},{8,12},{9,13},{10,... | collective-permute-start | bytes 196616 | tf_op jit(solution)/shard_map/ppermute | solution.py:138
  118.4 5.4 %collective-permute-start.15 = (f32[64,256]{1,0:T(8,128)S(1)}, f32[64,256]{1,0:T(8,128)S(1)}, u32[]{:S(2)}, u32[]{:S(2)}) collective-permute-start(f32[64,256]{1,0:T(8,128)S(1)} %add.72), channel_id=1, source_target_pairs={{0,8},{1,9},{2,10},{3,11},{4,12},{5,13},{6,14},{7,15},{8,0},{9,1},... | collective-permute-start | bytes 196616 | tf_op jit(solution)/shard_map/ppermute | solution.py:138
  118.9 5.6 %collective-permute-start.21 = (f32[16,4096]{1,0:T(8,128)S(1)}, f32[16,4096]{1,0:T(8,128)S(1)}, u32[]{:S(2)}, u32[]{:S(2)}) collective-permute-start(f32[16,4096]{1,0:T(8,128)S(1)} %pad_maximum_fusion.4), channel_id=1, source_target_pairs={{0,1},{1,0},{2,3},{3,2},{4,5},{5,4},{6,7},{7,6},{8,9},{9,8},{10,11... | collective-permute-start | bytes 786440 | tf_op jit(solution)/shard_map/ppermute | solution.py:138
  (5 other events, 10.4 us)

commit v2 on v1

v2 whole, which is shorter than its diff:
```python
import functools

import jax
import jax.numpy as jnp
from jax import lax
from jax.experimental import pallas as pl
from jax.experimental.pallas import tpu as pltpu
from jax.sharding import PartitionSpec as P

EXACT = lax.Precision.HIGHEST
F32, BF16 = jnp.float32, jnp.bfloat16
NT = (((1,), (1,)), ((), ()))
NN = (((1,), (0,)), ((), ()))
VM = pl.BlockSpec(memory_space=pltpu.VMEM)
SM = pl.BlockSpec(memory_space=pltpu.SMEM)
ANY = pl.BlockSpec(memory_space=pl.ANY)


def split(x):
    hi = x.astype(BF16)
    return hi, (x - hi.astype(F32)).astype(BF16)


def split_outside(x):
    hi = lax.reduce_precision(x, 8, 7)
    return hi.astype(BF16), (x - hi).astype(BF16)


def dot(a, b, dims=NN):
    return lax.dot_general(a, b, dims, preferred_element_type=F32)


def call(kernel, name, cost_us, mib, **kw):
    return pl.pallas_call(
        kernel,
        compiler_params=pltpu.CompilerParams(vmem_limit_bytes=mib << 20),
        cost_estimate=pl.CostEstimate(flops=int(cost_us * 1e9), bytes_accessed=0, transcendentals=0),
        name=name,
        **kw,
    )


def t_kernel(lcat_ref, wcat_ref, d_ref, thi_ref, tlo_ref, dv_ref, sem, *, ib, s, w, k, r):
    copy = pltpu.make_async_copy(d_ref, dv_ref, sem)
    copy.start()
    for g in range(r // ib):
        hi, lo = split(dot(lcat_ref[g * ib * s : (g + 1) * ib * s, :], wcat_ref[...]))
        for i in range(ib):
            q = g * ib + i
            for b in range(w):
                rows, lanes = slice(i * s, (i + 1) * s), slice(b * k, (b + 1) * k)
                thi_ref[b * s : (b + 1) * s, q * k : (q + 1) * k] = hi[rows, lanes]
                tlo_ref[b * s : (b + 1) * s, q * k : (q + 1) * k] = lo[rows, lanes]
    copy.wait()


def t_call(lcat, wcat, d, s, w, ib):
    r, total, k = d.shape
    return call(
        functools.partial(t_kernel, ib=ib, s=s, w=w, k=k, r=r),
        "left_by_weights",
        3.4,
        40,
        in_specs=[VM, VM, ANY],
        out_specs=[VM] * 3,
        out_shape=[pltpu.VMEM((w * s, r * k), BF16)] * 2 + [pltpu.VMEM(d.shape, F32)],
        scratch_shapes=[pltpu.SemaphoreType.DMA],
    )(lcat, wcat, d)


def b_kernel(me_ref, d_ref, f_ref, thi_ref, tlo_ref, out_ref, ghi, glo, *, ib, offs, rb, k, part, parts, steps):
    me = me_ref[0]
    per = len(offs) // parts
    rows = per * rb

    def prep(g):
        for o in range(per):
            at = part * per + o
            src = pl.multiple_of((me ^ offs[at]) * rb, rb)
            for i in range(ib):
                q = g * ib + i
                x = d_ref[q, pl.ds(src, rb), :] * f_ref[g, at * rb : (at + 1) * rb, i : i + 1]
                hi, lo = split(x)
                ghi[o * rb : (o + 1) * rb, q * k : (q + 1) * k] = hi
                glo[o * rb : (o + 1) * rb, q * k : (q + 1) * k] = lo

    prep(0)
    for g in range(steps):
        if g + 1 < steps:
            prep(g + 1)
        lanes = slice(g * ib * k, (g + 1) * ib * k)
        hi, lo = ghi[:, lanes], glo[:, lanes]
        x = dot(jnp.concatenate([hi, lo], axis=0), thi_ref[:, lanes], NT)
        x = x[:rows] + x[rows:] + dot(hi, tlo_ref[:, lanes], NT)
        out_ref[...] = x if g == 0 else out_ref[...] + x


def b_call(me, d, ft, thi, tlo, offs, rb, ib, part, parts):
    r, total, k = d.shape
    ws = thi.shape[0]
    rows = total // parts
    return call(
        functools.partial(b_kernel, ib=ib, offs=offs, rb=rb, k=k, part=part, parts=parts, steps=r // ib),
        f"right_grad_{part}",
        3.5,
        8,
        in_specs=[SM, VM, VM, VM, VM],
        out_specs=[VM] * 3,
        out_shape=[pltpu.VMEM((rows, ws), F32)] + [pltpu.VMEM((rows, r * k), BF16)] * 2,
    )(me, d, ft, thi, tlo)


def c_kernel(*refs, ib, s, k, steps, blocks, part, parts):
    g_refs = refs[: 2 * blocks]
    rg_ref, w_ref, lt_ref, lg_ref, ow_ref, rr, xhi, xlo, acc = refs[2 * blocks :]
    ws = rg_ref.shape[1] // parts
    wk = w_ref.shape[1] // parts
    w = lt_ref.shape[0] // 2
    rows = g_refs[0].shape[0]
    hi, lo = split(rg_ref[:, part * ws : (part + 1) * ws].T)
    rr[:ws] = hi
    rr[ws:] = lo

    def first(g):
        lanes = slice(g * ib * k, (g + 1) * ib * k)
        c1 = 0.0
        for p in range(blocks):
            js = slice(p * rows, (p + 1) * rows)
            x = dot(rr[:, js], g_refs[2 * p][:, lanes])
            c1 = c1 + x[:ws] + x[ws:] + dot(rr[:ws, js], g_refs[2 * p + 1][:, lanes])
        hi, lo = split(c1)
        for i in range(ib):
            q = g * ib + i
            for b in range(ws // s):
                xhi[q * s : (q + 1) * s, b * k : (b + 1) * k] = hi[b * s : (b + 1) * s, i * k : (i + 1) * k]
                xlo[q * s : (q + 1) * s, b * k : (b + 1) * k] = lo[b * s : (b + 1) * s, i * k : (i + 1) * k]

    def second(q0, q1):
        at = slice(q0 * ib * s, q1 * ib * s)
        xh, xl = xhi[at], xlo[at]
        mine = slice(part * wk, (part + 1) * wk)
        x = dot(xh, w_ref[:, mine], NT)
        lg_ref[at] = x[:, :w] + x[:, w:] + dot(xl, w_ref[:w, mine], NT)
        x = dot(lt_ref[:, at], xh)
        x = x[:w] + x[w:] + dot(lt_ref[:w, at], xl)
        x = x if q0 == 0 else acc[...] + x
        if q1 < steps:
            acc[...] = x
        else:
            for b in range(ws // s):
                ow_ref[:, b, :] = x[:, b * k : (b + 1) * k]

    span = min(2, steps)
    for g in range(steps):
        first(g)
        if g >= span and g % span == 0:
            second(g - span, g)
    second(steps - span, steps)


def c_call(gs, rg, w2, lt2, ib, s, k, part, parts):
    blocks = len(gs) // 2
    total, ws = rg.shape
    ws = ws // parts
    w = lt2.shape[0] // 2
    r = gs[0].shape[1] // k
    wk = w2.shape[1] // parts
    return call(
        functools.partial(c_kernel, ib=ib, s=s, k=k, steps=r // ib, blocks=blocks, part=part, parts=parts),
        f"left_and_weight_grad_{part}",
        5.6,
        20,
        in_specs=[VM] * (2 * blocks + 3),
        out_specs=[VM] * 2,
        out_shape=[pltpu.VMEM((r * s, w), F32), pltpu.VMEM((w, ws // s, k), F32)],
        scratch_shapes=[pltpu.VMEM((2 * ws, total), BF16)]
        + [pltpu.VMEM((r * s, wk), BF16)] * 2
        + [pltpu.VMEM((w, wk), F32)],
    )(*gs, rg, w2, lt2)


def swap(x, bit, n):
    return lax.ppermute(x, "row", [(i, i ^ bit) for i in range(n)])


def gather_relative(x, bits, n):
    for bit in bits:
        x = jnp.concatenate([x, swap(x, bit, n)], axis=0)
    return x


def relative_order(bits):
    offs = [0]
    for bit in bits:
        offs = offs + [o ^ bit for o in offs]
    return tuple(offs)


def pick(x, index):
    return x.at[index].get(mode="promise_in_bounds")


def after(x, *others):
    return lax.optimization_barrier((x, *others))[0]


def local(n, activation, valid, flags, w1, w2, wf, delta):
    s, r, m = activation.shape
    total, k = delta.shape[1:]
    w = w1.shape[1]
    ib = min(8, r)
    groups = r // ib
    parts = 2
    me = lax.axis_index("row").astype(jnp.int32)
    bits = [1 << e for e in reversed(range(n.bit_length() - 1))]
    offs = relative_order(bits)

    keep = valid.astype(F32)
    present = flags.astype(F32)
    both = jnp.einsum("sim,mc->isc", activation, jnp.concatenate([w1, w2], axis=1), precision=EXACT)
    both = both * keep.T[:, :, None]
    left, right = both[:, :, :w], both[:, :, w:]
    right_own = right.transpose(0, 2, 1).reshape(1, r, w * s)

    masks = jnp.concatenate([valid.reshape(-1), flags])[None]
    right_rel = right_own
    for step, bit in enumerate(bits):
        masks = jnp.concatenate([masks, swap(masks, bit, n)], axis=0)
        if step < len(bits) - 2:
            right_rel = jnp.concatenate([right_rel, swap(right_rel, bit, n)], axis=0)
    keep_rel = masks[:, : s * r].reshape(n, s, r)
    present_rel = masks[:, s * r :].reshape(total).astype(F32)
    count = lax.dot_general(
        keep_rel.astype(BF16), keep.astype(BF16), (((1,), (0,)), ((), ())), preferred_element_type=F32
    ).reshape(total, r)
    ft = present_rel[:, None] * present[None, :] / jnp.maximum(count, 1.0)
    ft = ft.reshape(total, groups, ib).transpose(1, 0, 2)
    early = right_rel
    right_rel = jnp.concatenate([right_rel, swap(right_rel, 2, n)], axis=0)

    whi, wlo = split_outside(wf.reshape(w, w * k))
    lflat = left.reshape(r * s, w)
    lhi, llo = split_outside(lflat)

    if r % 16 == 0:
        where, rb, blocks = me.reshape(1), r, offs
    else:
        order = me ^ jnp.array(offs, jnp.int32)
        delta = jnp.take(delta.reshape(r, n, r, k), order, axis=1).reshape(r, total, k)
        rb = total // 4
        where, blocks = jnp.zeros((1,), jnp.int32), tuple(range(4))

    thi, tlo, delta = t_call(
        after(jnp.concatenate([lhi, llo, lhi], axis=1), ft, early), jnp.concatenate([whi, whi, wlo], axis=0), delta, s, w, ib
    )
    right_rel_half = right_rel
    right_rel = jnp.concatenate([right_rel, swap(right_rel, 1, n)], axis=0).reshape(total, w * s)
    far, fhi, flo = b_call(where, delta, ft, thi, tlo, blocks, rb, ib, 1, 2)
    near, nhi, nlo = b_call(where, delta, ft, thi, tlo, blocks, rb, ib, 0, 2)

    quarter = w // 4
    places = (0, 2, 1, 3)
    turn = (me & 3) ^ jnp.array(places, jnp.int32)
    lt = pick(lflat.T.reshape(4, quarter, r * s), turn).reshape(w, r * s)
    lt2 = jnp.concatenate(split_outside(lt), axis=0)
    wboth = jnp.concatenate([whi, wlo], axis=0)

    left_grad = 0.0
    ows = []
    for part in range(parts):
        lg, ow = c_call((nhi, nlo, fhi, flo), right_rel, wboth, lt2, ib, s, k, part, parts)
        left_grad = left_grad + lg
        half = w // 2
        ow = ow[:half] + swap(ow[half:], 1, n)
        lt2 = after(lt2, ow)
        ow = ow[:quarter] + swap(ow[quarter:], 2, n)
        for bit in reversed(bits[:-2]):
            ow = ow + swap(ow, bit, n)
        ow = jnp.concatenate([ow, swap(ow, 2, n)], axis=0)
        ow = jnp.concatenate([ow, swap(ow, 1, n)], axis=0)
        ows.append(ow)

    grad = after(near + swap(far, 1, n), right_rel_half)
    for bit in reversed(bits[:-1]):
        half = grad.shape[0] // 2
        grad = grad[:half] + swap(grad[half:], bit, n)

    right_grad = grad.reshape(r, w, s).transpose(2, 0, 1) * keep[:, :, None]
    left_grad = left_grad.reshape(r, s, w).transpose(1, 0, 2) * keep[:, :, None]
    grads = jnp.concatenate([left_grad, right_grad], axis=2)
    alignment = jnp.einsum("sic,mc->sim", grads, jnp.concatenate([w1, w2], axis=1), precision=EXACT)
    small = jnp.einsum("sim,sic->cm", activation, grads, precision=EXACT)
    for bit in reversed(bits):
        small = small + swap(small, bit, n)

    back = pick(jnp.array(places, jnp.int32), (me & 3) ^ jnp.arange(4, dtype=jnp.int32))
    out_grad = jnp.concatenate(ows, axis=1).reshape(4, quarter, w, k)
    out_grad = pick(out_grad, back).reshape(w * w, k)
    return alignment, small[:w].T, small[w:].T, out_grad


def solution(mesh):
    in_specs = (
        P("groups", "row", None),
        P("groups", "row"),
        P(("groups", "row")),
        P(),
        P(),
        P(),
        P(("groups", "row"), None, None),
    )
    out_specs = (P("groups", "row", None), P("groups", None), P("groups", None), P("groups", None))
    body = functools.partial(local, mesh.shape["row"])
    return jax.shard_map(body, mesh=mesh, in_specs=in_specs, out_specs=out_specs, check_vma=False)
```

time: 126 us -> 98.2 us (0.78)
  Pallas kernels: 38.9 us -> 23.1 us
  waiting for transfers between devices: 42 us -> 27.7 us
  local copies, waits for them, and re-layouts: 14.4 us -> 7.9 us
  starting transfers between devices: 21.7 us -> 28.2 us
    pallas_call x4 -> x5, Pallas kernels: 38.9 us -> 23.1 us  [the longest x2 11.4 us: c_call(): call(functools.partial(c_kernel, ib=ib, s=s, k=k, steps=r // ib, blocks=b...]
    ppermute x22 -> x28, waiting for transfers between devices: 42 us -> 27.7 us  [swap(): return lax.ppermute(x, 'row', [(i, i ^ bit) for i in range(n)])]
    unnamed x34 -> x24, local copies, waits for them, and re-layouts: 7.87 us -> 0.1 us
    ppermute x22 -> x28, starting transfers between devices: 21.7 us -> 28.2 us  [swap(): return lax.ppermute(x, 'row', [(i, i ^ bit) for i in range(n)])]
    concatenate x7 -> x10, other arithmetic: 0.12 us -> 1.57 us  [the longest x2 0.74 us: local(): right_rel = jnp.concatenate([right_rel, swap(right_rel, bit, n)], axis=0)]
    transpose x2 -> x0, other arithmetic: 1.39 us -> none  [the longest x1 0.7 us: local(): both = both * keep.T[:, :, None]]
    gather x4 -> x3, local copies, waits for them, and re-layouts: 1.8 us -> 2.58 us  [pick(): return x.at[index].get(mode='promise_in_bounds')]
  transfers between devices with their start and end apart: 22 -> 28, of which waited for: 11 -> 15; matrix products, arithmetic and copies ran while one was open for 9% -> 13% of each run, Pallas kernels for 31% -> 15%
where the time goes in v2:
time: 98.2 us; the launch traced here: 97.8 us
  starting transfers between devices  28.2 us (29%)
  waiting for transfers between devices  27.7 us (28%)
  Pallas kernels  23.1 us (24%)
  local copies, waits for them, and re-layouts  7.9 us (8%)
  other arithmetic  5.31 us (5%)
  matrix products  4.27 us (4%)
  between operations  1.3 us (1%)
    ppermute x28, starting transfers between devices, swap(): return lax.ppermute(x, 'row', [(i, i ^ bit) for i in range(n)])  28.2 us
    ppermute x28, waiting for transfers between devices, swap(): return lax.ppermute(x, 'row', [(i, i ^ bit) for i in range(n)])  27.7 us
    pallas_call x2, Pallas kernels, c_call(): call(functools.partial(c_kernel, ib=ib, s=s, k=k, steps=r // ib, blocks=b...  11.4 us
    pallas_call x2, Pallas kernels, b_call(): call(functools.partial(b_kernel, ib=ib, offs=offs, rb=rb, k=k, part=part,...  7.15 us
    pallas_call x1, Pallas kernels, t_call(): call(functools.partial(t_kernel, ib=ib, s=s, w=w, k=k, r=r), 'left_by_wei...  4.6 us
    gather x3, local copies, waits for them, and re-layouts, pick(): return x.at[index].get(mode='promise_in_bounds')  2.58 us
  transfers between devices with their start and end apart: 28, of which 15 were waited for; matrix products, arithmetic and copies ran while one was open for 13% of the time, Pallas kernels for 15%

profile of v2, /device:TPU:0, one launch (start us, length us, event | category | flops | bytes accessed | tf_op | source)
XLA Modules:
  0.0 97.8 jit_solution(8070552047453750211)
XLA Ops:
  2.2 4.1 %collective-permute-start = (s32[1,544]{1,0:T(1,128)S(1)}, s32[1,544]{1,0:T(1,128)S(1)}, u32[]{:S(2)}, u32[]{:S(2)}) collective-permute-start(s32[1,544]{1,0:T(1,128)S(1)} %broadcast_in_dim.4), channel_id=1, source_target_pairs={{0,8},{1,9},{2,10},{3,11},{4,12},{5,13},{6,14},{7,15},{8,0},{9,1},... | collective-permute-start | bytes 6536 | tf_op jit(solution)/shard_map/ppermute | solution.py:183
  7.0 1.3 %fusion = f32[32,16,64]{2,0,1:T(8,128)S(1)} fusion(f32[16,32,256]{2,1,0:T(8,128)S(1)} %copy-done, f32[32,16]{0,1:T(8,128)S(1)} %get-tuple-element.49, f32[256,32]{0,1:T(8,128)} %param.13, f32[256,32]{0,1:T(8,128)} %param.12), kind=kOutput, calls=%fused_computation.4 | convolution fusion | flops 100712448 | bytes 722944 | tf_op jit(solution)/shard_map/sim,mc->isc/dot_general | solution.py:220
  10.9 1.9 %collective-permute-start.1 = (s32[2,544]{1,0:T(2,128)S(1)}, s32[2,544]{1,0:T(2,128)S(1)}, u32[]{:S(2)}, u32[]{:S(2)}) collective-permute-start(s32[2,544]{1,0:T(2,128)S(1)} %pad_add_fusion.2), channel_id=1, source_target_pairs={{0,4},{1,5},{2,6},{3,7},{4,0},{5,1},{6,2},{7,3},{8,12},{9,13},{10,... | collective-permute-start | bytes 13064 | tf_op jit(solution)/shard_map/ppermute | solution.py:183
  13.5 1.1 %collective-permute-done.1 = s32[2,544]{1,0:T(2,128)S(1)} collective-permute-done((s32[2,544]{1,0:T(2,128)S(1)}, s32[2,544]{1,0:T(2,128)S(1)}, u32[]{:S(2)}, u32[]{:S(2)}) %collective-permute-start.1) | collective-permute-done | bytes 4384 | tf_op jit(solution)/shard_map/ppermute | solution.py:183
  14.6 1.9 %collective-permute-start.2 = (s32[4,544]{1,0:T(4,128)S(1)}, s32[4,544]{1,0:T(4,128)S(1)}, u32[]{:S(2)}, u32[]{:S(2)}) collective-permute-start(s32[4,544]{1,0:T(4,128)S(1)} %pad_add_fusion.1), channel_id=1, source_target_pairs={{0,2},{1,3},{2,0},{3,1},{4,6},{5,7},{6,4},{7,5},{8,10},{9,11},{10,... | collective-permute-start | bytes 26120 | tf_op jit(solution)/shard_map/ppermute | solution.py:183
  19.7 3.4 %collective-permute-done.4 = f32[1,32,512]{1,2,0:T(8,128)} collective-permute-done((f32[1,32,512]{1,2,0:T(8,128)S(1)}, f32[1,32,512]{1,2,0:T(8,128)}, u32[]{:S(2)}, u32[]{:S(2)}) %collective-permute-start.4) | collective-permute-done | bytes 65568 | tf_op jit(solution)/shard_map/ppermute | solution.py:183
  25.4 1.2 %copy.35 = f32[512,4,8]{2,0,1:T(8,128)S(1)} copy(f32[512,4,8]{0,2,1:T(8,128)} %fusion.2) | data formatting | bytes 131072 | tf_op jit(solution)/shard_map/reshape | solution.py:237
  26.6 2.6 %collective-permute-done.5 = f32[2,32,512]{2,1,0:T(8,128)S(1)} collective-permute-done((f32[2,32,512]{2,1,0:T(8,128)S(1)}, f32[2,32,512]{2,1,0:T(8,128)S(1)}, u32[]{:S(2)}, u32[]{:S(2)}) %collective-permute-start.5) | collective-permute-done | bytes 131104 | tf_op jit(solution)/shard_map/ppermute | solution.py:183
  29.9 4.6 %left_by_weights.1 = (bf16[512,4096]{1,0:T(8,128)(2,1)S(1)}, bf16[512,4096]{1,0:T(8,128)(2,1)S(1)}, f32[32,512,128]{2,1,0:T(8,128)S(1)}) custom-call(bf16[512,96]{1,0:T(8,128)(2,1)} %pad_maximum_fusion.5.lcat_ref, bf16[96,4096]{1,0:T(8,128)(2,1)} %pad_maximum_fusion.wcat_ref, f32[32,512,128]{2,1,0:T(8,128)} %d_ref.1), custom_call_target="tpu_custom_call" | custom-call | flops 3400000000 | tf_op jit(solution)/shard_map/left_by_weights/pallas_call | solution.py:59
  34.6 3.5 %right_grad_1.1 = (f32[256,512]{1,0:T(8,128)S(1)}, bf16[256,4096]{1,0:T(8,128)(2,1)S(1)}, bf16[256,4096]{1,0:T(8,128)(2,1)S(1)}) custom-call(s32[1]{0:T(128)} %bitcast.me_ref, f32[32,512,128]{2,1,0:T(8,128)S(1)} %get-tuple-element.21.d_ref, f32[4,512,8]{2,1,0:T(8,128)S(1)} %bitcast.53, bf16[512,4096]{1,0:T(8,128)(2,1)S(1)} %get-tuple-element.22.thi_ref, ...), custom_call_target="tpu_custom_call" | custom-call | flops 3500000000 | tf_op jit(solution)/shard_map/right_grad_1/pallas_call | solution.py:102
  38.2 1.6 %collective-permute-start.6 = (f32[4,32,512]{2,1,0:T(8,128)S(1)}, f32[4,32,512]{2,1,0:T(8,128)S(1)}, u32[]{:S(2)}, u32[]{:S(2)}) collective-permute-start(f32[4,32,512]{2,1,0:T(8,128)S(1)} %copy-done.3), channel_id=1, source_target_pairs={{0,2},{1,3},{2,0},{3,1},{4,6},{5,7},{6,4},{7,5},{8,10},{9,11},{10,... | collective-permute-start | bytes 786440 | tf_op jit(solution)/shard_map/ppermute | solution.py:183
  39.8 3.6 %right_grad_0.1 = (f32[256,512]{1,0:T(8,128)S(1)}, bf16[256,4096]{1,0:T(8,128)(2,1)S(1)}, bf16[256,4096]{1,0:T(8,128)(2,1)S(1)}) custom-call(s32[1]{0:T(128)} %bitcast.me_ref, f32[32,512,128]{2,1,0:T(8,128)S(1)} %get-tuple-element.21.d_ref, f32[4,512,8]{2,1,0:T(8,128)S(1)} %bitcast.54, bf16[512,4096]{1,0:T(8,128)(2,1)S(1)} %get-tuple-element.22.thi_ref, ...), custom_call_target="tpu_custom_call" | custom-call | flops 3500000000 | tf_op jit(solution)/shard_map/right_grad_0/pallas_call | solution.py:102
  43.4 3.5 %collective-permute-done.6 = f32[4,32,512]{2,1,0:T(8,128)S(1)} collective-permute-done((f32[4,32,512]{2,1,0:T(8,128)S(1)}, f32[4,32,512]{2,1,0:T(8,128)S(1)}, u32[]{:S(2)}, u32[]{:S(2)}) %collective-permute-start.6) | collective-permute-done | bytes 262176 | tf_op jit(solution)/shard_map/ppermute | solution.py:183
  47.2 1.6 %collective-permute-start.10 = (f32[128,512]{1,0:T(8,128)S(1)}, f32[128,512]{1,0:T(8,128)S(1)}, u32[]{:S(2)}, u32[]{:S(2)}) collective-permute-start(f32[128,512]{1,0:T(8,128)S(1)} %slice.68), channel_id=1, source_target_pairs={{0,2},{1,3},{2,0},{3,1},{4,6},{5,7},{6,4},{7,5},{8,10},{9,11},{10,... | collective-permute-start | bytes 786440 | tf_op jit(solution)/shard_map/ppermute | solution.py:183
  48.8 7.2 %collective-permute-done.10 = f32[128,512]{1,0:T(8,128)S(1)} collective-permute-done((f32[128,512]{1,0:T(8,128)S(1)}, f32[128,512]{1,0:T(8,128)S(1)}, u32[]{:S(2)}, u32[]{:S(2)}) %collective-permute-start.10) | collective-permute-done | bytes 262176 | tf_op jit(solution)/shard_map/ppermute | solution.py:183
  56.2 5.8 %left_and_weight_grad_0.1 = (f32[512,32]{1,0:T(8,128)S(1)}, f32[32,16,128]{2,1,0:T(8,128)S(1)}) custom-call(bf16[256,4096]{1,0:T(8,128)(2,1)S(1)} %get-tuple-element.24.refs_0_, bf16[256,4096]{1,0:T(8,128)(2,1)S(1)} %get-tuple-element.25.refs_1_, bf16[256,4096]{1,0:T(8,128)(2,1)S(1)} %get-tuple-element.26.refs_2_, ...), custom_call_target="tpu_custom_call" | custom-call | flops 5600000000 | tf_op jit(solution)/shard_map/left_and_weight_grad_0/pallas_call | solution.py:168
  62.1 2.3 %collective-permute-start.12 = (f32[32,512]{1,0:T(8,128)S(1)}, f32[32,512]{1,0:T(8,128)S(1)}, u32[]{:S(2)}, u32[]{:S(2)}) collective-permute-start(f32[32,512]{1,0:T(8,128)S(1)} %slice.94), channel_id=1, source_target_pairs={{0,8},{1,9},{2,10},{3,11},{4,12},{5,13},{6,14},{7,15},{8,0},{9,1},... | collective-permute-start | bytes 196616 | tf_op jit(solution)/shard_map/ppermute | solution.py:183
  64.4 1.6 %collective-permute-start.17 = (f32[8,16,128]{2,1,0:T(8,128)S(1)}, f32[8,16,128]{2,1,0:T(8,128)S(1)}, u32[]{:S(2)}, u32[]{:S(2)}) collective-permute-start(f32[8,16,128]{2,1,0:T(8,128)S(1)} %slice.98), channel_id=1, source_target_pairs={{0,2},{1,3},{2,0},{3,1},{4,6},{5,7},{6,4},{7,5},{8,10},{9,11},{10,... | collective-permute-start | bytes 196616 | tf_op jit(solution)/shard_map/ppermute | solution.py:183
  66.0 5.6 %left_and_weight_grad_1.1 = (f32[512,32]{1,0:T(8,128)S(1)}, f32[32,16,128]{2,1,0:T(8,128)S(1)}) custom-call(bf16[256,4096]{1,0:T(8,128)(2,1)S(1)} %get-tuple-element.24.refs_0_, bf16[256,4096]{1,0:T(8,128)(2,1)S(1)} %get-tuple-element.25.refs_1_, bf16[256,4096]{1,0:T(8,128)(2,1)S(1)} %get-tuple-element.26.refs_2_, ...), custom_call_target="tpu_custom_call" | custom-call | flops 5600000000 | tf_op jit(solution)/shard_map/left_and_weight_grad_1/pallas_call | solution.py:168
  73.5 1.5 %collective-permute-start.18 = (f32[8,16,128]{2,1,0:T(8,128)S(1)}, f32[8,16,128]{2,1,0:T(8,128)S(1)}, u32[]{:S(2)}, u32[]{:S(2)}) collective-permute-start(f32[8,16,128]{2,1,0:T(8,128)S(1)} %slice_add_fusion.5), channel_id=1, source_target_pairs={{0,4},{1,5},{2,6},{3,7},{4,0},{5,1},{6,2},{7,3},{8,12},{9,13},{10,... | collective-permute-start | bytes 196616 | tf_op jit(solution)/shard_map/ppermute | solution.py:183
  75.7 1.6 %collective-permute-start.14 = (f32[64,256]{1,0:T(8,128)S(1)}, f32[64,256]{1,0:T(8,128)S(1)}, u32[]{:S(2)}, u32[]{:S(2)}) collective-permute-start(f32[64,256]{1,0:T(8,128)S(1)} %add.81), channel_id=1, source_target_pairs={{0,2},{1,3},{2,0},{3,1},{4,6},{5,7},{6,4},{7,5},{8,10},{9,11},{10,... | collective-permute-start | bytes 196616 | tf_op jit(solution)/shard_map/ppermute | solution.py:183
  77.8 1.3 %collective-permute-start.19 = (f32[8,16,128]{2,1,0:T(8,128)S(1)}, f32[8,16,128]{2,1,0:T(8,128)S(1)}, u32[]{:S(2)}, u32[]{:S(2)}) collective-permute-start(f32[8,16,128]{2,1,0:T(8,128)S(1)} %add.86), channel_id=1, source_target_pairs={{0,8},{1,9},{2,10},{3,11},{4,12},{5,13},{6,14},{7,15},{8,0},{9,1},... | collective-permute-start | bytes 196616 | tf_op jit(solution)/shard_map/ppermute | solution.py:183
  79.6 1.1 %collective-permute-start.24 = (f32[8,16,128]{2,1,0:T(8,128)S(1)}, f32[8,16,128]{2,1,0:T(8,128)S(1)}, u32[]{:S(2)}, u32[]{:S(2)}) collective-permute-start(f32[8,16,128]{2,1,0:T(8,128)S(1)} %slice_add_fusion.4), channel_id=1, source_target_pairs={{0,4},{1,5},{2,6},{3,7},{4,0},{5,1},{6,2},{7,3},{8,12},{9,13},{10,... | collective-permute-start | bytes 196616 | tf_op jit(solution)/shard_map/ppermute | solution.py:183
  80.7 1.1 %collective-permute-start.15 = (f32[64,256]{1,0:T(8,128)S(1)}, f32[64,256]{1,0:T(8,128)S(1)}, u32[]{:S(2)}, u32[]{:S(2)}) collective-permute-start(f32[64,256]{1,0:T(8,128)S(1)} %add.82), channel_id=1, source_target_pairs={{0,4},{1,5},{2,6},{3,7},{4,0},{5,1},{6,2},{7,3},{8,12},{9,13},{10,... | collective-permute-start | bytes 196616 | tf_op jit(solution)/shard_map/ppermute | solution.py:183
  81.8 1.4 %collective-permute-done.19 = f32[8,16,128]{2,1,0:T(8,128)S(1)} collective-permute-done((f32[8,16,128]{2,1,0:T(8,128)S(1)}, f32[8,16,128]{2,1,0:T(8,128)S(1)}, u32[]{:S(2)}, u32[]{:S(2)}) %collective-permute-start.19) | collective-permute-done | bytes 65568 | tf_op jit(solution)/shard_map/ppermute | solution.py:183
  83.9 1.6 %collective-permute-start.25 = (f32[8,16,128]{2,1,0:T(8,128)S(1)}, f32[8,16,128]{2,1,0:T(8,128)S(1)}, u32[]{:S(2)}, u32[]{:S(2)}) collective-permute-start(f32[8,16,128]{2,1,0:T(8,128)S(1)} %add.90), channel_id=1, source_target_pairs={{0,8},{1,9},{2,10},{3,11},{4,12},{5,13},{6,14},{7,15},{8,0},{9,1},... | collective-permute-start | bytes 196616 | tf_op jit(solution)/shard_map/ppermute | solution.py:183
  85.6 1.4 %fusion.5 = f32[16,32,256]{2,1,0:T(8,128)} fusion(f32[16,32,32]{2,1,0:T(8,128)S(1)} %get-tuple-element.47, f32[16,32,32]{2,1,0:T(8,128)S(1)} %get-tuple-element.46, f32[256,32]{0,1:T(8,128)S(1)} %copy-done.6, f32[256,32]{0,1:T(8,128)S(1)} %copy-done.7), kind=kOutput, calls=%fused_computation.34 | convolution fusion | flops 100712448 | bytes 720896 | tf_op jit(solution)/shard_map/sic,mc->sim/dot_general | solution.py:291
  87.0 1.4 %collective-permute-start.16 = (f32[64,256]{1,0:T(8,128)S(1)}, f32[64,256]{1,0:T(8,128)S(1)}, u32[]{:S(2)}, u32[]{:S(2)}) collective-permute-start(f32[64,256]{1,0:T(8,128)S(1)} %add.83), channel_id=1, source_target_pairs={{0,8},{1,9},{2,10},{3,11},{4,12},{5,13},{6,14},{7,15},{8,0},{9,1},... | collective-permute-start | bytes 196616 | tf_op jit(solution)/shard_map/ppermute | solution.py:183
  88.4 2.1 %collective-permute-done.25 = f32[8,16,128]{2,1,0:T(8,128)S(1)} collective-permute-done((f32[8,16,128]{2,1,0:T(8,128)S(1)}, f32[8,16,128]{2,1,0:T(8,128)S(1)}, u32[]{:S(2)}, u32[]{:S(2)}) %collective-permute-start.25) | collective-permute-done | bytes 65568 | tf_op jit(solution)/shard_map/ppermute | solution.py:183
  90.6 1.4 %collective-permute-start.26 = (f32[8,16,128]{2,1,0:T(8,128)S(1)}, f32[8,16,128]{2,1,0:T(8,128)S(1)}, u32[]{:S(2)}, u32[]{:S(2)}) collective-permute-start(f32[8,16,128]{2,1,0:T(8,128)S(1)} %add.91), channel_id=1, source_target_pairs={{0,2},{1,3},{2,0},{3,1},{4,6},{5,7},{6,4},{7,5},{8,10},{9,11},{10,... | collective-permute-start | bytes 196616 | tf_op jit(solution)/shard_map/ppermute | solution.py:183
  92.3 2.7 %collective-permute-done.26 = f32[8,16,128]{2,1,0:T(8,128)S(1)} collective-permute-done((f32[8,16,128]{2,1,0:T(8,128)S(1)}, f32[8,16,128]{2,1,0:T(8,128)S(1)}, u32[]{:S(2)}, u32[]{:S(2)}) %collective-permute-start.26) | collective-permute-done | bytes 65568 | tf_op jit(solution)/shard_map/ppermute | solution.py:183
  96.4 1.4 %gather_fusion.2 = f32[4,8,32,128]{3,2,1,0:T(8,128)} fusion(f32[4,8,32,128]{3,2,1,0:T(8,128)S(1)} %bitcast.58, s32[1024]{0:T(1024)S(1)} %pad_clamp_fusion), kind=kCustom, calls=%fused_computation.2 | custom fusion | bytes 1048592 | tf_op jit(solution)/shard_map/gather | solution.py:200
  (130 shorter events, 18.2 us)
Async XLA Ops:
  2.2 8.7 %collective-permute-start = (s32[1,544]{1,0:T(1,128)S(1)}, s32[1,544]{1,0:T(1,128)S(1)}, u32[]{:S(2)}, u32[]{:S(2)}) collective-permute-start(s32[1,544]{1,0:T(1,128)S(1)} %broadcast_in_dim.4), channel_id=1, source_target_pairs={{0,8},{1,9},{2,10},{3,11},{4,12},{5,13},{6,14},{7,15},{8,0},{9,1},... | collective-permute-start | bytes 6536 | tf_op jit(solution)/shard_map/ppermute | solution.py:183
  8.6 14.4 %collective-permute-start.4 = (f32[1,32,512]{1,2,0:T(8,128)S(1)}, f32[1,32,512]{1,2,0:T(8,128)}, u32[]{:S(2)}, u32[]{:S(2)}) collective-permute-start(f32[1,32,512]{1,2,0:T(8,128)S(1)} %bitcast.59), channel_id=1, source_target_pairs={{0,8},{1,9},{2,10},{3,11},{4,12},{5,13},{6,14},{7,15},{8,0},{9,1},... | collective-permute-start | bytes 196616 | tf_op jit(solution)/shard_map/ppermute | solution.py:183
  9.9 8.6 %copy-start.9 = (s32[32]{0:T(128)S(1)}, s32[32]{0:T(128)}, u32[]{:S(2)}) copy-start(s32[32]{0:T(128)} %param.11) | copy-start | bytes 388
  9.9 14.6 %copy-start.8 = (s32[16,32]{1,0:T(8,128)S(1)}, s32[16,32]{1,0:T(8,128)}, u32[]{:S(2)}) copy-start(s32[16,32]{1,0:T(8,128)} %param.10) | copy-start | bytes 6148
  10.9 3.7 %collective-permute-start.1 = (s32[2,544]{1,0:T(2,128)S(1)}, s32[2,544]{1,0:T(2,128)S(1)}, u32[]{:S(2)}, u32[]{:S(2)}) collective-permute-start(s32[2,544]{1,0:T(2,128)S(1)} %pad_add_fusion.2), channel_id=1, source_target_pairs={{0,4},{1,5},{2,6},{3,7},{4,0},{5,1},{6,2},{7,3},{8,12},{9,13},{10,... | collective-permute-start | bytes 13064 | tf_op jit(solution)/shard_map/ppermute | solution.py:183
  14.6 3.7 %collective-permute-start.2 = (s32[4,544]{1,0:T(4,128)S(1)}, s32[4,544]{1,0:T(4,128)S(1)}, u32[]{:S(2)}, u32[]{:S(2)}) collective-permute-start(s32[4,544]{1,0:T(4,128)S(1)} %pad_add_fusion.1), channel_id=1, source_target_pairs={{0,2},{1,3},{2,0},{3,1},{4,6},{5,7},{6,4},{7,5},{8,10},{9,11},{10,... | collective-permute-start | bytes 26120 | tf_op jit(solution)/shard_map/ppermute | solution.py:183
  18.4 1.3 %collective-permute-start.3 = (s32[8,544]{1,0:T(8,128)S(1)}, s32[8,544]{1,0:T(8,128)S(1)}, u32[]{:S(2)}, u32[]{:S(2)}) collective-permute-start(s32[8,544]{1,0:T(8,128)S(1)} %pad_add_fusion), channel_id=1, source_target_pairs={{0,1},{1,0},{2,3},{3,2},{4,5},{5,4},{6,7},{7,6},{8,9},{9,8},{10,11... | collective-permute-start | bytes 52232 | tf_op jit(solution)/shard_map/ppermute | solution.py:183
  24.2 5.0 %collective-permute-start.5 = (f32[2,32,512]{2,1,0:T(8,128)S(1)}, f32[2,32,512]{2,1,0:T(8,128)S(1)}, u32[]{:S(2)}, u32[]{:S(2)}) collective-permute-start(f32[2,32,512]{2,1,0:T(8,128)S(1)} %pad_maximum_fusion.6), channel_id=1, source_target_pairs={{0,4},{1,5},{2,6},{3,7},{4,0},{5,1},{6,2},{7,3},{8,12},{9,13},{10,... | collective-permute-start | bytes 393224 | tf_op jit(solution)/shard_map/ppermute | solution.py:183
  38.1 9.0 %collective-permute-start.9 = (f32[256,512]{1,0:T(8,128)S(1)}, f32[256,512]{1,0:T(8,128)S(1)}, u32[]{:S(2)}, u32[]{:S(2)}) collective-permute-start(f32[256,512]{1,0:T(8,128)S(1)} %get-tuple-element.33), channel_id=1, source_target_pairs={{0,1},{1,0},{2,3},{3,2},{4,5},{5,4},{6,7},{7,6},{8,9},{9,8},{10,11... | collective-permute-start | bytes 1572872 | tf_op jit(solution)/shard_map/ppermute | solution.py:183
  38.2 8.8 %collective-permute-start.6 = (f32[4,32,512]{2,1,0:T(8,128)S(1)}, f32[4,32,512]{2,1,0:T(8,128)S(1)}, u32[]{:S(2)}, u32[]{:S(2)}) collective-permute-start(f32[4,32,512]{2,1,0:T(8,128)S(1)} %copy-done.3), channel_id=1, source_target_pairs={{0,2},{1,3},{2,0},{3,1},{4,6},{5,7},{6,4},{7,5},{8,10},{9,11},{10,... | collective-permute-start | bytes 786440 | tf_op jit(solution)/shard_map/ppermute | solution.py:183
  47.0 9.1 %collective-permute-start.7 = (f32[8,32,512]{2,1,0:T(8,128)S(1)}, f32[8,32,512]{2,1,0:T(8,128)S(1)}, u32[]{:S(2)}, u32[]{:S(2)}) collective-permute-start(f32[8,32,512]{2,1,0:T(8,128)S(1)} %pad_maximum_fusion.1), channel_id=1, source_target_pairs={{0,1},{1,0},{2,3},{3,2},{4,5},{5,4},{6,7},{7,6},{8,9},{9,8},{10,11... | collective-permute-start | bytes 1572872 | tf_op jit(solution)/shard_map/ppermute | solution.py:183
  47.2 8.8 %collective-permute-start.10 = (f32[128,512]{1,0:T(8,128)S(1)}, f32[128,512]{1,0:T(8,128)S(1)}, u32[]{:S(2)}, u32[]{:S(2)}) collective-permute-start(f32[128,512]{1,0:T(8,128)S(1)} %slice.68), channel_id=1, source_target_pairs={{0,2},{1,3},{2,0},{3,1},{4,6},{5,7},{6,4},{7,5},{8,10},{9,11},{10,... | collective-permute-start | bytes 786440 | tf_op jit(solution)/shard_map/ppermute | solution.py:183
  56.0 6.0 %collective-permute-start.11 = (f32[64,512]{1,0:T(8,128)S(1)}, f32[64,512]{1,0:T(8,128)S(1)}, u32[]{:S(2)}, u32[]{:S(2)}) collective-permute-start(f32[64,512]{1,0:T(8,128)S(1)} %slice.92), channel_id=1, source_target_pairs={{0,4},{1,5},{2,6},{3,7},{4,0},{5,1},{6,2},{7,3},{8,12},{9,13},{10,... | collective-permute-start | bytes 393224 | tf_op jit(solution)/shard_map/ppermute | solution.py:183
  62.0 2.4 %collective-permute-start.8 = (f32[16,16,128]{2,1,0:T(8,128)S(1)}, f32[16,16,128]{2,1,0:T(8,128)S(1)}, u32[]{:S(2)}, u32[]{:S(2)}) collective-permute-start(f32[16,16,128]{2,1,0:T(8,128)S(1)} %slice.66), channel_id=1, source_target_pairs={{0,1},{1,0},{2,3},{3,2},{4,5},{5,4},{6,7},{7,6},{8,9},{9,8},{10,11... | collective-permute-start | bytes 393224 | tf_op jit(solution)/shard_map/ppermute | solution.py:183
  62.1 9.6 %collective-permute-start.12 = (f32[32,512]{1,0:T(8,128)S(1)}, f32[32,512]{1,0:T(8,128)S(1)}, u32[]{:S(2)}, u32[]{:S(2)}) collective-permute-start(f32[32,512]{1,0:T(8,128)S(1)} %slice.94), channel_id=1, source_target_pairs={{0,8},{1,9},{2,10},{3,11},{4,12},{5,13},{6,14},{7,15},{8,0},{9,1},... | collective-permute-start | bytes 196616 | tf_op jit(solution)/shard_map/ppermute | solution.py:183
  64.4 9.1 %collective-permute-start.17 = (f32[8,16,128]{2,1,0:T(8,128)S(1)}, f32[8,16,128]{2,1,0:T(8,128)S(1)}, u32[]{:S(2)}, u32[]{:S(2)}) collective-permute-start(f32[8,16,128]{2,1,0:T(8,128)S(1)} %slice.98), channel_id=1, source_target_pairs={{0,2},{1,3},{2,0},{3,1},{4,6},{5,7},{6,4},{7,5},{8,10},{9,11},{10,... | collective-permute-start | bytes 196616 | tf_op jit(solution)/shard_map/ppermute | solution.py:183
  71.6 3.4 %collective-permute-start.22 = (f32[16,16,128]{2,1,0:T(8,128)S(1)}, f32[16,16,128]{2,1,0:T(8,128)S(1)}, u32[]{:S(2)}, u32[]{:S(2)}) collective-permute-start(f32[16,16,128]{2,1,0:T(8,128)S(1)} %slice.78), channel_id=1, source_target_pairs={{0,1},{1,0},{2,3},{3,2},{4,5},{5,4},{6,7},{7,6},{8,9},{9,8},{10,11... | collective-permute-start | bytes 393224 | tf_op jit(solution)/shard_map/ppermute | solution.py:183
  72.1 13.5 %copy-start.6 = (f32[256,32]{0,1:T(8,128)S(1)}, f32[256,32]{0,1:T(8,128)}, u32[]{:S(2)}) copy-start(f32[256,32]{0,1:T(8,128)} %param.13) | copy-start | bytes 98308
  72.1 13.5 %copy-start.7 = (f32[256,32]{0,1:T(8,128)S(1)}, f32[256,32]{0,1:T(8,128)}, u32[]{:S(2)}) copy-start(f32[256,32]{0,1:T(8,128)} %param.12) | copy-start | bytes 98308
  72.9 2.7 %collective-permute-start.13 = (f32[64,256]{1,0:T(8,128)S(1)}, f32[64,256]{1,0:T(8,128)S(1)}, u32[]{:S(2)}, u32[]{:S(2)}) collective-permute-start(f32[64,256]{1,0:T(8,128)S(1)} %convolution_bitcast_fusion.1), channel_id=1, source_target_pairs={{0,1},{1,0},{2,3},{3,2},{4,5},{5,4},{6,7},{7,6},{8,9},{9,8},{10,11... | collective-permute-start | bytes 196616 | tf_op jit(solution)/shard_map/ppermute | solution.py:183
  73.5 4.3 %collective-permute-start.18 = (f32[8,16,128]{2,1,0:T(8,128)S(1)}, f32[8,16,128]{2,1,0:T(8,128)S(1)}, u32[]{:S(2)}, u32[]{:S(2)}) collective-permute-start(f32[8,16,128]{2,1,0:T(8,128)S(1)} %slice_add_fusion.5), channel_id=1, source_target_pairs={{0,4},{1,5},{2,6},{3,7},{4,0},{5,1},{6,2},{7,3},{8,12},{9,13},{10,... | collective-permute-start | bytes 196616 | tf_op jit(solution)/shard_map/ppermute | solution.py:183
  75.1 4.5 %collective-permute-start.23 = (f32[8,16,128]{2,1,0:T(8,128)S(1)}, f32[8,16,128]{2,1,0:T(8,128)S(1)}, u32[]{:S(2)}, u32[]{:S(2)}) collective-permute-start(f32[8,16,128]{2,1,0:T(8,128)S(1)} %slice.100), channel_id=1, source_target_pairs={{0,2},{1,3},{2,0},{3,1},{4,6},{5,7},{6,4},{7,5},{8,10},{9,11},{10,... | collective-permute-start | bytes 196616 | tf_op jit(solution)/shard_map/ppermute | solution.py:183
  75.7 5.0 %collective-permute-start.14 = (f32[64,256]{1,0:T(8,128)S(1)}, f32[64,256]{1,0:T(8,128)S(1)}, u32[]{:S(2)}, u32[]{:S(2)}) collective-permute-start(f32[64,256]{1,0:T(8,128)S(1)} %add.81), channel_id=1, source_target_pairs={{0,2},{1,3},{2,0},{3,1},{4,6},{5,7},{6,4},{7,5},{8,10},{9,11},{10,... | collective-permute-start | bytes 196616 | tf_op jit(solution)/shard_map/ppermute | solution.py:183
  77.8 5.3 %collective-permute-start.19 = (f32[8,16,128]{2,1,0:T(8,128)S(1)}, f32[8,16,128]{2,1,0:T(8,128)S(1)}, u32[]{:S(2)}, u32[]{:S(2)}) collective-permute-start(f32[8,16,128]{2,1,0:T(8,128)S(1)} %add.86), channel_id=1, source_target_pairs={{0,8},{1,9},{2,10},{3,11},{4,12},{5,13},{6,14},{7,15},{8,0},{9,1},... | collective-permute-start | bytes 196616 | tf_op jit(solution)/shard_map/ppermute | solution.py:183
  79.6 4.3 %collective-permute-start.24 = (f32[8,16,128]{2,1,0:T(8,128)S(1)}, f32[8,16,128]{2,1,0:T(8,128)S(1)}, u32[]{:S(2)}, u32[]{:S(2)}) collective-permute-start(f32[8,16,128]{2,1,0:T(8,128)S(1)} %slice_add_fusion.4), channel_id=1, source_target_pairs={{0,4},{1,5},{2,6},{3,7},{4,0},{5,1},{6,2},{7,3},{8,12},{9,13},{10,... | collective-permute-start | bytes 196616 | tf_op jit(solution)/shard_map/ppermute | solution.py:183
  80.7 6.3 %collective-permute-start.15 = (f32[64,256]{1,0:T(8,128)S(1)}, f32[64,256]{1,0:T(8,128)S(1)}, u32[]{:S(2)}, u32[]{:S(2)}) collective-permute-start(f32[64,256]{1,0:T(8,128)S(1)} %add.82), channel_id=1, source_target_pairs={{0,4},{1,5},{2,6},{3,7},{4,0},{5,1},{6,2},{7,3},{8,12},{9,13},{10,... | collective-permute-start | bytes 196616 | tf_op jit(solution)/shard_map/ppermute | solution.py:183
  83.2 8.8 %collective-permute-start.20 = (f32[8,16,128]{2,1,0:T(8,128)S(1)}, f32[8,16,128]{2,1,0:T(8,128)S(1)}, u32[]{:S(2)}, u32[]{:S(2)}) collective-permute-start(f32[8,16,128]{2,1,0:T(8,128)S(1)} %add.87), channel_id=1, source_target_pairs={{0,2},{1,3},{2,0},{3,1},{4,6},{5,7},{6,4},{7,5},{8,10},{9,11},{10,... | collective-permute-start | bytes 196616 | tf_op jit(solution)/shard_map/ppermute | solution.py:183
  83.9 6.6 %collective-permute-start.25 = (f32[8,16,128]{2,1,0:T(8,128)S(1)}, f32[8,16,128]{2,1,0:T(8,128)S(1)}, u32[]{:S(2)}, u32[]{:S(2)}) collective-permute-start(f32[8,16,128]{2,1,0:T(8,128)S(1)} %add.90), channel_id=1, source_target_pairs={{0,8},{1,9},{2,10},{3,11},{4,12},{5,13},{6,14},{7,15},{8,0},{9,1},... | collective-permute-start | bytes 196616 | tf_op jit(solution)/shard_map/ppermute | solution.py:183
  87.0 5.2 %collective-permute-start.16 = (f32[64,256]{1,0:T(8,128)S(1)}, f32[64,256]{1,0:T(8,128)S(1)}, u32[]{:S(2)}, u32[]{:S(2)}) collective-permute-start(f32[64,256]{1,0:T(8,128)S(1)} %add.83), channel_id=1, source_target_pairs={{0,8},{1,9},{2,10},{3,11},{4,12},{5,13},{6,14},{7,15},{8,0},{9,1},... | collective-permute-start | bytes 196616 | tf_op jit(solution)/shard_map/ppermute | solution.py:183
  90.6 4.3 %collective-permute-start.26 = (f32[8,16,128]{2,1,0:T(8,128)S(1)}, f32[8,16,128]{2,1,0:T(8,128)S(1)}, u32[]{:S(2)}, u32[]{:S(2)}) collective-permute-start(f32[8,16,128]{2,1,0:T(8,128)S(1)} %add.91), channel_id=1, source_target_pairs={{0,2},{1,3},{2,0},{3,1},{4,6},{5,7},{6,4},{7,5},{8,10},{9,11},{10,... | collective-permute-start | bytes 196616 | tf_op jit(solution)/shard_map/ppermute | solution.py:183
  92.0 3.6 %collective-permute-start.21 = (f32[16,16,128]{2,1,0:T(8,128)S(1)}, f32[16,16,128]{2,1,0:T(8,128)S(1)}, u32[]{:S(2)}, u32[]{:S(2)}) collective-permute-start(f32[16,16,128]{2,1,0:T(8,128)S(1)} %pad_maximum_fusion.7), channel_id=1, source_target_pairs={{0,1},{1,0},{2,3},{3,2},{4,5},{5,4},{6,7},{7,6},{8,9},{9,8},{10,11... | collective-permute-start | bytes 393224 | tf_op jit(solution)/shard_map/ppermute | solution.py:183
  94.9 1.4 %collective-permute-start.27 = (f32[16,16,128]{2,1,0:T(8,128)S(1)}, f32[16,16,128]{2,1,0:T(8,128)S(1)}, u32[]{:S(2)}, u32[]{:S(2)}) collective-permute-start(f32[16,16,128]{2,1,0:T(8,128)S(1)} %pad_maximum_fusion.8), channel_id=1, source_target_pairs={{0,1},{1,0},{2,3},{3,2},{4,5},{5,4},{6,7},{7,6},{8,9},{9,8},{10,11... | collective-permute-start | bytes 393224 | tf_op jit(solution)/shard_map/ppermute | solution.py:183
  (6 other events, 26.7 us)

commit v3 on v2

v3 whole, which is shorter than its diff:
```python
import functools

import jax
import jax.numpy as jnp
from jax import lax
from jax.experimental import pallas as pl
from jax.experimental.pallas import tpu as pltpu
from jax.sharding import PartitionSpec as P

EXACT = lax.Precision.HIGHEST
F32, BF16 = jnp.float32, jnp.bfloat16
NT = (((1,), (1,)), ((), ()))
NN = (((1,), (0,)), ((), ()))
PLACES = (0, 2, 1, 3)
GAP = 32
VM = pl.BlockSpec(memory_space=pltpu.VMEM)
SM = pl.BlockSpec(memory_space=pltpu.SMEM)
ANY = pl.BlockSpec(memory_space=pl.ANY)


def split(x):
    hi = x.astype(BF16)
    return hi, (x - hi.astype(F32)).astype(BF16)


def split_outside(x):
    hi = lax.reduce_precision(x, 8, 7)
    return hi.astype(BF16), (x - hi).astype(BF16)


def dot(a, b, dims=NN):
    return lax.dot_general(a, b, dims, preferred_element_type=F32)


def weights(w_ref, w, first=0, size=None):
    return jnp.concatenate([w_ref[pl.ds(b, w, stride=w), :] for b in range(first, first + (size or w))], axis=1)


def residues(l_ref, r, s, first, size):
    return jnp.concatenate([l_ref[pl.ds(i, s, stride=r), :] for i in range(first, first + size)], axis=0)


def call(kernel, name, cost_us, mib, **kw):
    return pl.pallas_call(
        kernel,
        compiler_params=pltpu.CompilerParams(vmem_limit_bytes=mib << 20),
        cost_estimate=pl.CostEstimate(flops=int(cost_us * 1e9), bytes_accessed=0, transcendentals=0),
        name=name,
        **kw,
    )


def b_kernel(
    me_ref, d_ref, m_ref, own_ref, l_ref, w_ref, oa_ref, ob_ref, ahi, alo, bhi, blo, thi_ref, tlo_ref, dv_ref, f_ref, wcat, sem, *, ib, offs, rb, s
):
    r, total, k = d_ref.shape
    w = l_ref.shape[1]
    steps = r // ib
    per = len(offs) // 2
    copy = pltpu.make_async_copy(d_ref, dv_ref, sem)
    copy.start()
    me = me_ref[0]

    every = m_ref[...].astype(BF16)
    lane = lax.broadcasted_iota(jnp.int32, own_ref.shape, 1)
    for p in range(2):
        own = own_ref[...] if p == 0 else pltpu.roll(own_ref[...], GAP, 1)
        keep = jnp.where((lane >= p * GAP) & (lane < p * GAP + s), own, 0.0).astype(BF16)
        present = jnp.where(lane == p * GAP + s, own, 0.0).astype(BF16)
        f_ref[p] = dot(every, present, NT) / jnp.maximum(dot(every, keep, NT), 1.0)

    hi, lo = split(weights(w_ref, w))
    wcat[:w] = hi
    wcat[w : 2 * w] = hi
    wcat[2 * w :] = lo
    for g in range(steps):
        left = residues(l_ref, r, s, g * ib, ib)
        hi = left.astype(BF16).astype(F32)
        hi, lo = split(dot(jnp.concatenate([hi, left - hi, hi], axis=1).astype(BF16), wcat[...]))
        for i in range(ib):
            q = g * ib + i
            for b in range(w):
                rows, lanes = slice(i * s, (i + 1) * s), slice(b * k, (b + 1) * k)
                thi_ref[b * s : (b + 1) * s, q * k : (q + 1) * k] = hi[rows, lanes]
                tlo_ref[b * s : (b + 1) * s, q * k : (q + 1) * k] = lo[rows, lanes]
    copy.wait()

    def scale(p, ghi, glo, g):
        for o in range(per):
            src = pl.multiple_of((me ^ offs[p * per + o]) * rb, rb)
            for q in range(g * ib, (g + 1) * ib):
                hi, lo = split(dv_ref[q, pl.ds(src, rb), :] * f_ref[p, o * rb : (o + 1) * rb, q : q + 1])
                ghi[o * rb : (o + 1) * rb, q * k : (q + 1) * k] = hi
                glo[o * rb : (o + 1) * rb, q * k : (q + 1) * k] = lo

    work = [(p, halves, g) for p, halves in ((1, (ob_ref, bhi, blo)), (0, (oa_ref, ahi, alo))) for g in range(steps)]

    def prepare(p, halves, g):
        scale(p, halves[1], halves[2], g)

    prepare(*work[0])
    for t, (p, (out_ref, ghi, glo), g) in enumerate(work):
        if t + 1 < len(work):
            prepare(*work[t + 1])
        lanes = slice(g * ib * k, (g + 1) * ib * k)
        hi, lo = ghi[:, lanes], glo[:, lanes]
        rows = hi.shape[0]
        x = dot(jnp.concatenate([hi, lo], axis=0), thi_ref[:, lanes], NT)
        x = x[:rows] + x[rows:] + dot(hi, tlo_ref[:, lanes], NT)
        out_ref[...] = x if g == 0 else out_ref[...] + x


def b_call(me, d, masks, own, left, w, offs, rb, ib, s):
    r, total, k = d.shape
    ws = left.shape[1] * s
    rows = total // 2
    return call(
        functools.partial(b_kernel, ib=ib, offs=offs, rb=rb, s=s),
        "right_grad",
        11.0,
        30,
        in_specs=[SM, ANY, VM, VM, VM, VM],
        out_specs=[VM] * 6,
        out_shape=[pltpu.VMEM((rows, ws), F32)] * 2 + [pltpu.VMEM((rows, r * k), BF16)] * 4,
        scratch_shapes=[pltpu.VMEM((ws, r * k), BF16)] * 2
        + [
            pltpu.VMEM(d.shape, F32),
            pltpu.VMEM((2, rows, r), F32),
            pltpu.VMEM((3 * left.shape[1], left.shape[1] * k), BF16),
            pltpu.SemaphoreType.DMA,
        ],
    )(me, pltpu.with_memory_space_constraint(d, pltpu.HBM), masks, own, left, w)


def c_kernel(*refs, ib, s, k, steps, blocks, part, parts):
    g_refs = refs[: 2 * blocks]
    me_ref, ra_ref, rb_ref, w_ref, l_ref, lg_ref, keep_ref, send_ref, rr, xhi, xlo, acc, lt_ref, turned, wsplit = refs[2 * blocks :]
    w = l_ref.shape[1]
    wk = w * k // parts
    ws = w * s // parts
    rows = g_refs[0].shape[0]
    hi, lo = split(weights(w_ref, w, part * w // parts, w // parts))
    wsplit[:w] = hi
    wsplit[w:] = lo
    turned[...] = residues(l_ref, l_ref.shape[0] // s, s, 0, l_ref.shape[0] // s).T
    quarter = w // 4
    for t, place in enumerate(PLACES):
        at = pl.multiple_of(((me_ref[0] & 3) ^ place) * quarter, quarter)
        hi, lo = split(turned[pl.ds(at, quarter), :])
        lt_ref[t * quarter : (t + 1) * quarter] = hi.astype(F32)
        lt_ref[w + t * quarter : w + (t + 1) * quarter] = lo.astype(F32)
    for p, half in enumerate((ra_ref, rb_ref)):
        hi, lo = split(half[:, part * ws : (part + 1) * ws].T)
        rr[:ws, p * rows : (p + 1) * rows] = hi
        rr[ws:, p * rows : (p + 1) * rows] = lo

    def first(g):
        lanes = slice(g * ib * k, (g + 1) * ib * k)
        c1 = 0.0
        for p in range(blocks):
            js = slice(p * rows, (p + 1) * rows)
            x = dot(rr[:, js], g_refs[2 * p][:, lanes])
            c1 = c1 + x[:ws] + x[ws:] + dot(rr[:ws, js], g_refs[2 * p + 1][:, lanes])
        hi, lo = split(c1)
        for i in range(ib):
            q = g * ib + i
            for b in range(ws // s):
                xhi[q * s : (q + 1) * s, b * k : (b + 1) * k] = hi[b * s : (b + 1) * s, i * k : (i + 1) * k]
                xlo[q * s : (q + 1) * s, b * k : (b + 1) * k] = lo[b * s : (b + 1) * s, i * k : (i + 1) * k]

    def second(q0, q1):
        at = slice(q0 * ib * s, q1 * ib * s)
        xh, xl = xhi[at], xlo[at]
        x = dot(xh, wsplit[...], NT)
        lg_ref[at] = x[:, :w] + x[:, w:] + dot(xl, wsplit[:w], NT)
        lt = lt_ref[:, at].astype(BF16)
        x = dot(lt, xh)
        x = x[:w] + x[w:] + dot(lt[:w], xl)
        x = x if q0 == 0 else acc[...] + x
        if q1 < steps:
            acc[...] = x
        else:
            for b in range(ws // s):
                lanes = slice(b * k, (b + 1) * k)
                keep_ref[:, b, :] = x[: w // 2, lanes]
                send_ref[:, b, :] = x[w // 2 :, lanes]

    span = min(2, steps)
    for g in range(steps):
        first(g)
        if g >= span and g % span == 0:
            second(g - span, g)
    second(steps - span, steps)


def c_call(gs, me, rights, w2, left, ib, s, part, parts):
    blocks = len(gs) // 2
    total = 2 * rights[0].shape[0]
    w = left.shape[1]
    ws = w * s // parts
    k = w2.shape[1]
    r = gs[0].shape[1] // k
    wk = w * k // parts
    return call(
        functools.partial(c_kernel, ib=ib, s=s, k=k, steps=r // ib, blocks=blocks, part=part, parts=parts),
        f"left_and_weight_grad_{part}",
        5.6,
        20,
        in_specs=[VM] * (2 * blocks) + [SM, VM, VM, VM, VM],
        out_specs=[VM] * 3,
        out_shape=[pltpu.VMEM((r * s, w), F32)] + [pltpu.VMEM((w // 2, ws // s, k), F32)] * 2,
        scratch_shapes=[pltpu.VMEM((2 * ws, total), BF16)]
        + [pltpu.VMEM((r * s, wk), BF16)] * 2
        + [pltpu.VMEM((w, wk), F32), pltpu.VMEM((2 * w, r * s), F32), pltpu.VMEM((w, r * s), F32)]
        + [pltpu.VMEM((2 * w, wk), BF16)],
    )(*gs, me, *rights, w2, left)


def swap(x, bit, n):
    return lax.ppermute(x, "row", [(i, i ^ bit) for i in range(n)])


def gather_relative(x, bits, n):
    for bit in bits:
        x = jnp.concatenate([x, swap(x, bit, n)], axis=0)
    return x


def relative_order(bits):
    offs = [0]
    for bit in bits:
        offs = offs + [o ^ bit for o in offs]
    return tuple(offs)


def pick(x, index):
    return x.at[index].get(mode="promise_in_bounds")


def after(x, *others):
    return lax.optimization_barrier((x, *others))[0]


def local(n, activation, valid, flags, w1, w2, wf, delta):
    s, r, m = activation.shape
    total, k = delta.shape[1:]
    w = w1.shape[1]
    ib = min(8, r)
    parts = 2
    me = lax.axis_index("row").astype(jnp.int32)
    bits = [1 << e for e in reversed(range(n.bit_length() - 1))]
    offs = relative_order(bits)

    here = me.reshape(1)
    keep = valid.astype(F32)
    both = jnp.einsum("sim,mc->sic", activation, jnp.concatenate([w1, w2], axis=1), precision=EXACT)
    both = both * keep[:, :, None]
    left, right = both[:, :, :w].reshape(s * r, w), both[:, :, w:]
    ws = w * s
    own = jnp.concatenate([keep.T, flags.astype(F32)[:, None], jnp.zeros((r, GAP - 1 - s), F32)], axis=1)
    own = jnp.concatenate([own, swap(own, 1, n), jnp.zeros((r, k - 2 * GAP), F32)], axis=1)
    load = jnp.concatenate([right.transpose(1, 2, 0).reshape(r, ws), own], axis=1)
    for bit in bits[:-2]:
        other = swap(load, bit, n)
        masks = jnp.concatenate([load[:, ws:], other[:, ws:]], axis=0)
        load = jnp.concatenate([load, other], axis=0)
    masks = jnp.concatenate([masks, swap(masks, 2, n)], axis=0)
    load = after(load[:, :ws], masks)

    if r % 16 == 0:
        where, rb, blocks = here, r, offs
    else:
        order = me ^ jnp.array(offs, jnp.int32)
        delta = jnp.take(delta.reshape(r, n, r, k), order, axis=1).reshape(r, total, k)
        rb = total // 4
        where, blocks = jnp.zeros((1,), jnp.int32), tuple(range(4))

    near, far, *gs = b_call(where, delta, masks, own, left, wf, blocks, rb, ib, s)
    load = jnp.concatenate([load, after(swap(load, 2, n), near)], axis=0)
    rights = (load, swap(load, 1, n))

    def halves(x, y, rows):
        return x[:rows] + y[:rows], x[rows:] + y[rows:]

    later = list(reversed(bits[:-1]))
    rows = near.shape[0] // 2
    grad, send = halves(near, swap(far, 1, n), rows)
    left_a, ow_a, send_a = c_call(gs, after(here, grad, send), rights, wf, left, ib, s, 0, parts)
    other_a = swap(send_a, 1, n)
    rows = rows // 2
    grad, send = halves(grad, after(swap(send, later[0], n), left_a), rows)
    left_b, ow_b, send_b = c_call(gs, after(here, grad, send), rights, wf, left, ib, s, 1, parts)

    quarter = w // 4
    ow_b = ow_b + swap(send_b, 1, n)
    ow_a = ow_a + after(other_a, left_b)
    ow = jnp.concatenate([ow_a[:quarter], ow_b[:quarter]], axis=1)
    ow_send = jnp.concatenate([ow_a[quarter:], ow_b[quarter:]], axis=1)
    for bit in later[1:]:
        rows = rows // 2
        other = after(swap(send, bit, n), left_b)
        if bit == later[-1]:
            grad = grad + other
        else:
            grad, send = halves(grad, other, rows)
            send = after(send, ow_send)

    left_grad = (left_a + left_b).reshape(r, s, w).transpose(1, 0, 2) * keep[:, :, None]
    right_grad = grad.reshape(r, w, s).transpose(2, 0, 1) * keep[:, :, None]
    grads = jnp.concatenate([left_grad, right_grad], axis=2)
    alignment = jnp.einsum("sic,mc->sim", grads, jnp.concatenate([w1, w2], axis=1), precision=EXACT)
    small = jnp.einsum("sim,sic->cm", activation, grads, precision=EXACT)
    small = jnp.concatenate([small[:, i : i + k] for i in range(0, m, k)], axis=0).reshape(-1, w, k)
    ow = ow + swap(ow_send, 2, n)
    size = small.shape[0]
    ow = jnp.concatenate([small, ow], axis=0)
    for bit in reversed(bits[:-2]):
        ow = ow + swap(ow, bit, n)
    for bit in (2, 1):
        other = swap(ow, bit, n)
        ow = jnp.concatenate([ow[:size] + other[:size], ow[size:], other[size:]], axis=0)
    small = ow[:size].reshape(m // k, 2 * w, k).transpose(1, 0, 2).reshape(2 * w, m)

    back = pick(jnp.array(PLACES, jnp.int32), (me & 3) ^ jnp.arange(4, dtype=jnp.int32))
    out_grad = ow[size:].reshape(4, quarter, w, k)
    out_grad = pick(out_grad, back).reshape(w * w, k)
    return alignment, small[:w].T, small[w:].T, out_grad


def solution(mesh):
    in_specs = (
        P("groups", "row", None),
        P("groups", "row"),
        P(("groups", "row")),
        P(),
        P(),
        P(),
        P(("groups", "row"), None, None),
    )
    out_specs = (P("groups", "row", None), P("groups", None), P("groups", None), P("groups", None))
    body = functools.partial(local, mesh.shape["row"])
    return jax.shard_map(body, mesh=mesh, in_specs=in_specs, out_specs=out_specs, check_vma=False)
```

time: 98.2 us -> 92.9 us (0.946)
  waiting for transfers between devices: 27.7 us -> 41.1 us
  starting transfers between devices: 28.2 us -> 17.1 us
  local copies, waits for them, and re-layouts: 7.9 us -> 3.82 us
  other arithmetic: 5.31 us -> 2.11 us
    ppermute x28 -> x17, waiting for transfers between devices: 27.7 us -> 41.1 us  [swap(): return lax.ppermute(x, 'row', [(i, i ^ bit) for i in range(n)])]
    ppermute x28 -> x17, starting transfers between devices: 28.2 us -> 17.1 us  [swap(): return lax.ppermute(x, 'row', [(i, i ^ bit) for i in range(n)])]
    concatenate x14 -> x11, other arithmetic: 3.37 us -> 0.22 us  [the longest x1 0.08 us: local(): jnp.concatenate([keep.T, flags.astype(F32)[:, None], jnp.zeros((r, GAP -...]
    reshape x4 -> x1, local copies, waits for them, and re-layouts: 2.23 us -> 0.1 us  [local(): right.transpose(1, 2, 0).reshape(r, ws)]
    ppermute x1 -> x0, local copies, waits for them, and re-layouts: 1.05 us -> none  [swap(): return lax.ppermute(x, 'row', [(i, i ^ bit) for i in range(n)])]
    dot_general x2 -> x1, matrix products: 2.17 us -> 1.34 us  [local(): jnp.einsum('sim,mc->sic', activation, jnp.concatenate([w1, w2], axis=1),...]
    gather x3 -> x2, local copies, waits for them, and re-layouts: 2.58 us -> 2.01 us  [pick(): return x.at[index].get(mode='promise_in_bounds')]
    pallas_call x3 -> x1, Pallas kernels: 11.8 us -> 12.2 us  [b_call(): call(functools.partial(b_kernel, ib=ib, offs=offs, rb=rb, s=s), 'right_gr...]
  transfers between devices with their start and end apart: 28 -> 17, of which waited for: 15 -> 13; matrix products, arithmetic and copies ran while one was open for 13% -> 6% of each run, Pallas kernels for 15% -> 26%
where the time goes in v3:
time: 92.9 us; the launch traced here: 92.6 us
  waiting for transfers between devices  41.1 us (44%)
  Pallas kernels  24 us (26%)
  starting transfers between devices  17.1 us (18%)
  local copies, waits for them, and re-layouts  3.82 us (4%)
  matrix products  3.44 us (4%)
  other arithmetic  2.11 us (2%)
  between operations  1.02 us (1%)
    ppermute x17, waiting for transfers between devices, swap(): return lax.ppermute(x, 'row', [(i, i ^ bit) for i in range(n)])  41.1 us
    ppermute x17, starting transfers between devices, swap(): return lax.ppermute(x, 'row', [(i, i ^ bit) for i in range(n)])  17.1 us
    pallas_call x1, Pallas kernels, b_call(): call(functools.partial(b_kernel, ib=ib, offs=offs, rb=rb, s=s), 'right_gr...  12.2 us
    pallas_call x2, Pallas kernels, c_call(): call(functools.partial(c_kernel, ib=ib, s=s, k=k, steps=r // ib, blocks=b...  11.8 us
    gather x2, local copies, waits for them, and re-layouts, pick(): return x.at[index].get(mode='promise_in_bounds')  2.01 us
  transfers between devices with their start and end apart: 17, of which 13 were waited for; matrix products, arithmetic and copies ran while one was open for 6% of the time, Pallas kernels for 26%

profile of v3, /device:TPU:0, one launch (start us, length us, event | category | flops | bytes accessed | tf_op | source)
XLA Modules:
  0.0 92.6 jit_solution(6750222883499030299)
XLA Ops:
  0.6 0.8 convert_element_type.6
  1.5 0.7 convert_bitcast_fusion
  2.8 1.3 %fusion = f32[16,32,64]{2,1,0:T(8,128)S(1)} fusion(f32[16,32,256]{2,1,0:T(8,128)S(1)} %copy-done, f32[16,32]{1,0:T(8,128)S(1)} %convert_element_type.6, f32[256,32]{0,1:T(8,128)} %param.12, f32[256,32]{0,1:T(8,128)} %param.11), kind=kOutput, calls=%fused_computation.3 | convolution fusion | flops 100712448 | bytes 722944 | tf_op jit(solution)/shard_map/sim,mc->sic/dot_general | solution.py:256
  4.7 3.7 %collective-permute-start.1 = (f32[32,640]{1,0:T(8,128)S(1)}, f32[32,640]{1,0:T(8,128)S(1)}, u32[]{:S(2)}, u32[]{:S(2)}) collective-permute-start(f32[32,640]{1,0:T(8,128)S(1)} %concatenate.57), channel_id=1, source_target_pairs={{0,8},{1,9},{2,10},{3,11},{4,12},{5,13},{6,14},{7,15},{8,0},{9,1},... | collective-permute-start | bytes 245768 | tf_op jit(solution)/shard_map/ppermute | solution.py:220
  8.3 4.9 %collective-permute-done.1 = f32[32,640]{1,0:T(8,128)S(1)} collective-permute-done((f32[32,640]{1,0:T(8,128)S(1)}, f32[32,640]{1,0:T(8,128)S(1)}, u32[]{:S(2)}, u32[]{:S(2)}) %collective-permute-start.1) | collective-permute-done | bytes 81952 | tf_op jit(solution)/shard_map/ppermute | solution.py:220
  13.2 0.8 collective-permute-start.2
  14.1 5.2 %collective-permute-done.2 = f32[64,640]{1,0:T(8,128)S(1)} collective-permute-done((f32[64,640]{1,0:T(8,128)S(1)}, f32[64,640]{1,0:T(8,128)S(1)}, u32[]{:S(2)}, u32[]{:S(2)}) %collective-permute-start.2) | collective-permute-done | bytes 163872 | tf_op jit(solution)/shard_map/ppermute | solution.py:220
  19.3 1.4 %collective-permute-start.3 = (f32[128,128]{1,0:T(8,128)S(1)}, f32[128,128]{1,0:T(8,128)S(1)}, u32[]{:S(2)}, u32[]{:S(2)}) collective-permute-start(f32[128,128]{1,0:T(8,128)S(1)} %pad_maximum_fusion.11), channel_id=1, source_target_pairs={{0,2},{1,3},{2,0},{3,1},{4,6},{5,7},{6,4},{7,5},{8,10},{9,11},{10,... | collective-permute-start | bytes 196616 | tf_op jit(solution)/shard_map/ppermute | solution.py:220
  20.7 2.9 %collective-permute-done.3 = f32[128,128]{1,0:T(8,128)S(1)} collective-permute-done((f32[128,128]{1,0:T(8,128)S(1)}, f32[128,128]{1,0:T(8,128)S(1)}, u32[]{:S(2)}, u32[]{:S(2)}) %collective-permute-start.3) | collective-permute-done | bytes 65568 | tf_op jit(solution)/shard_map/ppermute | solution.py:220
  23.6 1.4 %collective-permute-start.5 = (f32[128,512]{1,0:T(8,128)S(1)}, f32[128,512]{1,0:T(8,128)S(1)}, u32[]{:S(2)}, u32[]{:S(2)}) collective-permute-start(f32[128,512]{1,0:T(8,128)S(1)} %pad_maximum_fusion.2), channel_id=1, source_target_pairs={{0,2},{1,3},{2,0},{3,1},{4,6},{5,7},{6,4},{7,5},{8,10},{9,11},{10,... | collective-permute-start | bytes 786440 | tf_op jit(solution)/shard_map/ppermute | solution.py:220
  25.0 12.2 %right_grad.1 = (f32[256,512]{1,0:T(8,128)S(1)}, f32[256,512]{1,0:T(8,128)S(1)}, bf16[256,4096]{1,0:T(8,128)(2,1)S(1)}, bf16[256,4096]{1,0:T(8,128)(2,1)S(1)}, b...) custom-call(s32[1]{0:T(128)} %bitcast.me_ref.refs_4_, f32[32,512,128]{2,1,0:T(8,128)} %d_ref.1, ...), custom_call_target="tpu_custom_call" | custom-call | flops 11000000512 | tf_op jit(solution)/shard_map/right_grad/pallas_call | solution.py:117
  38.0 1.3 %collective-permute-done.4 = f32[256,512]{1,0:T(8,128)S(1)} collective-permute-done((f32[256,512]{1,0:T(8,128)S(1)}, f32[256,512]{1,0:T(8,128)S(1)}, u32[]{:S(2)}, u32[]{:S(2)}) %collective-permute-start.4) | collective-permute-done | bytes 524320 | tf_op jit(solution)/shard_map/ppermute | solution.py:220
  39.3 0.8 collective-permute-start.7
  40.1 6.0 %left_and_weight_grad_0.1 = (f32[512,32]{1,0:T(8,128)S(1)}, f32[16,16,128]{2,1,0:T(8,128)S(1)}, f32[16,16,128]{2,1,0:T(8,128)S(1)}) custom-call(bf16[256,4096]{1,0:T(8,128)(2,1)S(1)} %get-tuple-element.25.refs_0_, bf16[256,4096]{1,0:T(8,128)(2,1)S(1)} %get-tuple-element.26.refs_1_, bf16[256,4096]{1,0:T(8,128)(2,1)S(1)} %get-tuple-element.27.refs_2_, ...), custom_call_target="tpu_custom_call" | custom-call | flops 5600000000 | tf_op jit(solution)/shard_map/left_and_weight_grad_0/pallas_call | solution.py:204
  46.1 1.7 %collective-permute-done.7 = f32[128,512]{1,0:T(8,128)S(1)} collective-permute-done((f32[128,512]{1,0:T(8,128)S(1)}, f32[128,512]{1,0:T(8,128)S(1)}, u32[]{:S(2)}, u32[]{:S(2)}) %collective-permute-start.7) | collective-permute-done | bytes 262176 | tf_op jit(solution)/shard_map/ppermute | solution.py:220
  47.8 1.1 %collective-permute-start.8 = (f32[64,512]{1,0:T(8,128)S(1)}, f32[64,512]{1,0:T(8,128)S(1)}, u32[]{:S(2)}, u32[]{:S(2)}) collective-permute-start(f32[64,512]{1,0:T(8,128)S(1)} %get-tuple-element.48), channel_id=1, source_target_pairs={{0,4},{1,5},{2,6},{3,7},{4,0},{5,1},{6,2},{7,3},{8,12},{9,13},{10,... | collective-permute-start | bytes 393224 | tf_op jit(solution)/shard_map/ppermute | solution.py:220
  48.9 5.8 %left_and_weight_grad_1.1 = (f32[512,32]{1,0:T(8,128)S(1)}, f32[16,16,128]{2,1,0:T(8,128)S(1)}, f32[16,16,128]{2,1,0:T(8,128)S(1)}) custom-call(bf16[256,4096]{1,0:T(8,128)(2,1)S(1)} %get-tuple-element.25.refs_0_, bf16[256,4096]{1,0:T(8,128)(2,1)S(1)} %get-tuple-element.26.refs_1_, bf16[256,4096]{1,0:T(8,128)(2,1)S(1)} %get-tuple-element.27.refs_2_, ...), custom_call_target="tpu_custom_call" | custom-call | flops 5600000000 | tf_op jit(solution)/shard_map/left_and_weight_grad_1/pallas_call | solution.py:204
  55.3 0.8 collective-permute-done.10
  56.3 3.4 %collective-permute-start.11 = (f32[32,512]{1,0:T(8,128)S(1)}, f32[32,512]{1,0:T(8,128)S(1)}, u32[]{:S(2)}, u32[]{:S(2)}) collective-permute-start(f32[32,512]{1,0:T(8,128)S(1)} %slice_add_fusion.6), channel_id=1, source_target_pairs={{0,8},{1,9},{2,10},{3,11},{4,12},{5,13},{6,14},{7,15},{8,0},{9,1},... | collective-permute-start | bytes 196616 | tf_op jit(solution)/shard_map/ppermute | solution.py:220
  59.8 0.6 collective-permute-start.12
  60.4 3.1 %collective-permute-done.11 = f32[32,512]{1,0:T(8,128)S(1)} collective-permute-done((f32[32,512]{1,0:T(8,128)S(1)}, f32[32,512]{1,0:T(8,128)S(1)}, u32[]{:S(2)}, u32[]{:S(2)}) %collective-permute-start.11) | collective-permute-done | bytes 65568 | tf_op jit(solution)/shard_map/ppermute | solution.py:220
  64.0 0.7 convolution_bitcast_fusion
  64.7 0.6 collective-permute-done.12
  65.7 6.0 %collective-permute-done.13 = f32[12,32,128]{2,1,0:T(8,128)S(1)} collective-permute-done((f32[12,32,128]{2,1,0:T(8,128)S(1)}, f32[12,32,128]{2,1,0:T(8,128)S(1)}, u32[]{:S(2)}, u32[]{:S(2)}) %collective-permute-start.13) | collective-permute-done | bytes 196640 | tf_op jit(solution)/shard_map/ppermute | solution.py:220
  71.7 1.0 %collective-permute-start.14 = (f32[12,32,128]{2,1,0:T(8,128)S(1)}, f32[12,32,128]{2,1,0:T(8,128)S(1)}, u32[]{:S(2)}, u32[]{:S(2)}) collective-permute-start(f32[12,32,128]{2,1,0:T(8,128)S(1)} %fusion.9), channel_id=1, source_target_pairs={{0,8},{1,9},{2,10},{3,11},{4,12},{5,13},{6,14},{7,15},{8,0},{9,1},... | collective-permute-start | bytes 589832 | tf_op jit(solution)/shard_map/ppermute | solution.py:220
  72.8 9.2 %collective-permute-done.14 = f32[12,32,128]{2,1,0:T(8,128)S(1)} collective-permute-done((f32[12,32,128]{2,1,0:T(8,128)S(1)}, f32[12,32,128]{2,1,0:T(8,128)S(1)}, u32[]{:S(2)}, u32[]{:S(2)}) %collective-permute-start.14) | collective-permute-done | bytes 196640 | tf_op jit(solution)/shard_map/ppermute | solution.py:220
  82.1 0.9 collective-permute-start.15
  82.9 0.6 gather_fusion
  83.6 5.2 %collective-permute-done.15 = f32[12,32,128]{2,1,0:T(8,128)S(1)} collective-permute-done((f32[12,32,128]{2,1,0:T(8,128)S(1)}, f32[12,32,128]{2,1,0:T(8,128)S(1)}, u32[]{:S(2)}, u32[]{:S(2)}) %collective-permute-start.15) | collective-permute-done | bytes 196640 | tf_op jit(solution)/shard_map/ppermute | solution.py:220
  88.9 1.4 %fusion.1 = f32[16,32,256]{2,1,0:T(8,128)} fusion(f32[16,32,32]{2,1,0:T(8,128)S(1)} %get-tuple-element.61, f32[16,32,32]{2,1,0:T(8,128)S(1)} %get-tuple-element.60, f32[256,32]{0,1:T(8,128)S(1)} %copy-done.3, f32[256,32]{0,1:T(8,128)S(1)} %copy-done.4), kind=kOutput, calls=%fused_computation.24 | convolution fusion | flops 100712448 | bytes 720896 | tf_op jit(solution)/shard_map/sic,mc->sim/dot_general | solution.py:311
  90.6 0.6 bitcast_bitcast_fusion
  91.2 1.4 %gather_fusion.1 = f32[4,8,32,128]{3,2,1,0:T(8,128)} fusion(f32[4,8,32,128]{3,2,1,0:T(8,128)S(1)} %bitcast.51, s32[1024]{0:T(1024)S(1)} %pad_clamp_fusion), kind=kCustom, calls=%fused_computation.1 | custom fusion | bytes 1048592 | tf_op jit(solution)/shard_map/gather | solution.py:237
  (72 shorter events, 4.3 us)
Async XLA Ops:
  0.6 2.1 %copy-start = (f32[16,32,256]{2,1,0:T(8,128)S(1)}, f32[16,32,256]{2,1,0:T(8,128)}, u32[]{:S(2)}) copy-start(f32[16,32,256]{2,1,0:T(8,128)} %param.8) | copy-start | bytes 1572868
  2.3 2.2 %collective-permute-start = (f32[32,32]{1,0:T(8,128)S(1)}, f32[32,32]{1,0:T(8,128)S(1)}, u32[]{:S(2)}, u32[]{:S(2)}) collective-permute-start(f32[32,32]{1,0:T(8,128)S(1)} %pad_maximum_fusion.13), channel_id=1, source_target_pairs={{0,1},{1,0},{2,3},{3,2},{4,5},{5,4},{6,7},{7,6},{8,9},{9,8},{10,11... | collective-permute-start | bytes 12296 | tf_op jit(solution)/shard_map/ppermute | solution.py:220
  4.1 20.9 %copy-start.1 = (f32[1024,128]{1,0:T(8,128)S(1)}, f32[1024,128]{1,0:T(8,128)}, u32[]{:S(2)}) copy-start(f32[1024,128]{1,0:T(8,128)} %refs_7_.3) | copy-start | bytes 1572868
  4.7 8.5 %collective-permute-start.1 = (f32[32,640]{1,0:T(8,128)S(1)}, f32[32,640]{1,0:T(8,128)S(1)}, u32[]{:S(2)}, u32[]{:S(2)}) collective-permute-start(f32[32,640]{1,0:T(8,128)S(1)} %concatenate.57), channel_id=1, source_target_pairs={{0,8},{1,9},{2,10},{3,11},{4,12},{5,13},{6,14},{7,15},{8,0},{9,1},... | collective-permute-start | bytes 245768 | tf_op jit(solution)/shard_map/ppermute | solution.py:220
  13.2 6.1 %collective-permute-start.2 = (f32[64,640]{1,0:T(8,128)S(1)}, f32[64,640]{1,0:T(8,128)S(1)}, u32[]{:S(2)}, u32[]{:S(2)}) collective-permute-start(f32[64,640]{1,0:T(8,128)S(1)} %pad_maximum_fusion.6), channel_id=1, source_target_pairs={{0,4},{1,5},{2,6},{3,7},{4,0},{5,1},{6,2},{7,3},{8,12},{9,13},{10,... | collective-permute-start | bytes 491528 | tf_op jit(solution)/shard_map/ppermute | solution.py:220
  19.3 4.3 %collective-permute-start.3 = (f32[128,128]{1,0:T(8,128)S(1)}, f32[128,128]{1,0:T(8,128)S(1)}, u32[]{:S(2)}, u32[]{:S(2)}) collective-permute-start(f32[128,128]{1,0:T(8,128)S(1)} %pad_maximum_fusion.11), channel_id=1, source_target_pairs={{0,2},{1,3},{2,0},{3,1},{4,6},{5,7},{6,4},{7,5},{8,10},{9,11},{10,... | collective-permute-start | bytes 196616 | tf_op jit(solution)/shard_map/ppermute | solution.py:220
  23.6 13.7 %collective-permute-start.5 = (f32[128,512]{1,0:T(8,128)S(1)}, f32[128,512]{1,0:T(8,128)S(1)}, u32[]{:S(2)}, u32[]{:S(2)}) collective-permute-start(f32[128,512]{1,0:T(8,128)S(1)} %pad_maximum_fusion.2), channel_id=1, source_target_pairs={{0,2},{1,3},{2,0},{3,1},{4,6},{5,7},{6,4},{7,5},{8,10},{9,11},{10,... | collective-permute-start | bytes 786440 | tf_op jit(solution)/shard_map/ppermute | solution.py:220
  37.3 2.0 %collective-permute-start.4 = (f32[256,512]{1,0:T(8,128)S(1)}, f32[256,512]{1,0:T(8,128)S(1)}, u32[]{:S(2)}, u32[]{:S(2)}) collective-permute-start(f32[256,512]{1,0:T(8,128)S(1)} %get-tuple-element.30), channel_id=1, source_target_pairs={{0,1},{1,0},{2,3},{3,2},{4,5},{5,4},{6,7},{7,6},{8,9},{9,8},{10,11... | collective-permute-start | bytes 1572872 | tf_op jit(solution)/shard_map/ppermute | solution.py:220
  37.4 2.7 %collective-permute-start.6 = (f32[256,512]{1,0:T(8,128)S(1)}, f32[256,512]{1,0:T(8,128)S(1)}, u32[]{:S(2)}, u32[]{:S(2)}) collective-permute-start(f32[256,512]{1,0:T(8,128)S(1)} %constant_dynamic-update-slice_fusion.refs_5_), channel_id=1, source_target_pairs={{0,1},{1,0},{2,3},{3,2},{4,5},{5,4},{6,7},{7,6},{8,9},{9,8},{10,11... | collective-permute-start | bytes 1572872 | tf_op jit(solution)/shard_map/ppermute | solution.py:220
  39.3 8.4 %collective-permute-start.7 = (f32[128,512]{1,0:T(8,128)S(1)}, f32[128,512]{1,0:T(8,128)S(1)}, u32[]{:S(2)}, u32[]{:S(2)}) collective-permute-start(f32[128,512]{1,0:T(8,128)S(1)} %get-tuple-element.46), channel_id=1, source_target_pairs={{0,2},{1,3},{2,0},{3,1},{4,6},{5,7},{6,4},{7,5},{8,10},{9,11},{10,... | collective-permute-start | bytes 786440 | tf_op jit(solution)/shard_map/ppermute | solution.py:220
  47.8 7.5 %collective-permute-start.8 = (f32[64,512]{1,0:T(8,128)S(1)}, f32[64,512]{1,0:T(8,128)S(1)}, u32[]{:S(2)}, u32[]{:S(2)}) collective-permute-start(f32[64,512]{1,0:T(8,128)S(1)} %get-tuple-element.48), channel_id=1, source_target_pairs={{0,4},{1,5},{2,6},{3,7},{4,0},{5,1},{6,2},{7,3},{8,12},{9,13},{10,... | collective-permute-start | bytes 393224 | tf_op jit(solution)/shard_map/ppermute | solution.py:220
  54.7 1.4 %collective-permute-start.10 = (f32[16,16,128]{2,1,0:T(8,128)S(1)}, f32[16,16,128]{2,1,0:T(8,128)S(1)}, u32[]{:S(2)}, u32[]{:S(2)}) collective-permute-start(f32[16,16,128]{2,1,0:T(8,128)S(1)} %get-tuple-element.43), channel_id=1, source_target_pairs={{0,1},{1,0},{2,3},{3,2},{4,5},{5,4},{6,7},{7,6},{8,9},{9,8},{10,11... | collective-permute-start | bytes 393224 | tf_op jit(solution)/shard_map/ppermute | solution.py:220
  54.7 1.5 %collective-permute-start.9 = (f32[16,16,128]{2,1,0:T(8,128)S(1)}, f32[16,16,128]{2,1,0:T(8,128)S(1)}, u32[]{:S(2)}, u32[]{:S(2)}) collective-permute-start(f32[16,16,128]{2,1,0:T(8,128)S(1)} %get-tuple-element.40), channel_id=1, source_target_pairs={{0,1},{1,0},{2,3},{3,2},{4,5},{5,4},{6,7},{7,6},{8,9},{9,8},{10,11... | collective-permute-start | bytes 393224 | tf_op jit(solution)/shard_map/ppermute | solution.py:220
  56.3 7.1 %collective-permute-start.11 = (f32[32,512]{1,0:T(8,128)S(1)}, f32[32,512]{1,0:T(8,128)S(1)}, u32[]{:S(2)}, u32[]{:S(2)}) collective-permute-start(f32[32,512]{1,0:T(8,128)S(1)} %slice_add_fusion.6), channel_id=1, source_target_pairs={{0,8},{1,9},{2,10},{3,11},{4,12},{5,13},{6,14},{7,15},{8,0},{9,1},... | collective-permute-start | bytes 196616 | tf_op jit(solution)/shard_map/ppermute | solution.py:220
  59.8 5.5 %collective-permute-start.12 = (f32[8,32,128]{2,1,0:T(8,128)S(1)}, f32[8,32,128]{2,1,0:T(8,128)S(1)}, u32[]{:S(2)}, u32[]{:S(2)}) collective-permute-start(f32[8,32,128]{2,1,0:T(8,128)S(1)} %pad_maximum_fusion.8), channel_id=1, source_target_pairs={{0,2},{1,3},{2,0},{3,1},{4,6},{5,7},{6,4},{7,5},{8,10},{9,11},{10,... | collective-permute-start | bytes 393224 | tf_op jit(solution)/shard_map/ppermute | solution.py:220
  63.8 19.1 %copy-start.2 = (s32[4]{0:T(128)S(1)}, s32[4]{0:T(128)}, u32[]{:S(2)}) copy-start(s32[4]{0:T(128)} %constant.5.clone) | copy-start | bytes 52
  64.6 24.3 %copy-start.3 = (f32[256,32]{0,1:T(8,128)S(1)}, f32[256,32]{0,1:T(8,128)}, u32[]{:S(2)}) copy-start(f32[256,32]{0,1:T(8,128)} %param.12) | copy-start | bytes 98308
  64.7 24.3 %copy-start.4 = (f32[256,32]{0,1:T(8,128)S(1)}, f32[256,32]{0,1:T(8,128)}, u32[]{:S(2)}) copy-start(f32[256,32]{0,1:T(8,128)} %param.11) | copy-start | bytes 98308
  65.4 6.4 %collective-permute-start.13 = (f32[12,32,128]{2,1,0:T(8,128)S(1)}, f32[12,32,128]{2,1,0:T(8,128)S(1)}, u32[]{:S(2)}, u32[]{:S(2)}) collective-permute-start(f32[12,32,128]{2,1,0:T(8,128)S(1)} %pad_maximum_fusion.5), channel_id=1, source_target_pairs={{0,4},{1,5},{2,6},{3,7},{4,0},{5,1},{6,2},{7,3},{8,12},{9,13},{10,... | collective-permute-start | bytes 589832 | tf_op jit(solution)/shard_map/ppermute | solution.py:220
  71.7 10.3 %collective-permute-start.14 = (f32[12,32,128]{2,1,0:T(8,128)S(1)}, f32[12,32,128]{2,1,0:T(8,128)S(1)}, u32[]{:S(2)}, u32[]{:S(2)}) collective-permute-start(f32[12,32,128]{2,1,0:T(8,128)S(1)} %fusion.9), channel_id=1, source_target_pairs={{0,8},{1,9},{2,10},{3,11},{4,12},{5,13},{6,14},{7,15},{8,0},{9,1},... | collective-permute-start | bytes 589832 | tf_op jit(solution)/shard_map/ppermute | solution.py:220
  82.1 6.7 %collective-permute-start.15 = (f32[12,32,128]{2,1,0:T(8,128)S(1)}, f32[12,32,128]{2,1,0:T(8,128)S(1)}, u32[]{:S(2)}, u32[]{:S(2)}) collective-permute-start(f32[12,32,128]{2,1,0:T(8,128)S(1)} %add.77), channel_id=1, source_target_pairs={{0,2},{1,3},{2,0},{3,1},{4,6},{5,7},{6,4},{7,5},{8,10},{9,11},{10,... | collective-permute-start | bytes 589832 | tf_op jit(solution)/shard_map/ppermute | solution.py:220
  88.8 1.7 %collective-permute-start.16 = (f32[20,32,128]{2,1,0:T(8,128)S(1)}, f32[20,32,128]{2,1,0:T(8,128)S(1)}, u32[]{:S(2)}, u32[]{:S(2)}) collective-permute-start(f32[20,32,128]{2,1,0:T(8,128)S(1)} %pad_maximum_fusion.1), channel_id=1, source_target_pairs={{0,1},{1,0},{2,3},{3,2},{4,5},{5,4},{6,7},{7,6},{8,9},{9,8},{10,11... | collective-permute-start | bytes 983048 | tf_op jit(solution)/shard_map/ppermute | solution.py:220

commit v4 on v3

--- a/solution.py
+++ b/solution.py
@@ -50,30 +50,16 @@
     )
 
 
-def b_kernel(
-    me_ref, d_ref, m_ref, own_ref, l_ref, w_ref, oa_ref, ob_ref, ahi, alo, bhi, blo, thi_ref, tlo_ref, dv_ref, f_ref, wcat, sem, *, ib, offs, rb, s
-):
+def t_kernel(l_ref, w_ref, d_ref, thi_ref, tlo_ref, dv_ref, wcat, sem, *, ib, s):
     r, total, k = d_ref.shape
     w = l_ref.shape[1]
-    steps = r // ib
-    per = len(offs) // 2
     copy = pltpu.make_async_copy(d_ref, dv_ref, sem)
     copy.start()
-    me = me_ref[0]
-
-    every = m_ref[...].astype(BF16)
-    lane = lax.broadcasted_iota(jnp.int32, own_ref.shape, 1)
-    for p in range(2):
-        own = own_ref[...] if p == 0 else pltpu.roll(own_ref[...], GAP, 1)
-        keep = jnp.where((lane >= p * GAP) & (lane < p * GAP + s), own, 0.0).astype(BF16)
-        present = jnp.where(lane == p * GAP + s, own, 0.0).astype(BF16)
-        f_ref[p] = dot(every, present, NT) / jnp.maximum(dot(every, keep, NT), 1.0)
-
     hi, lo = split(weights(w_ref, w))
     wcat[:w] = hi
     wcat[w : 2 * w] = hi
     wcat[2 * w :] = lo
-    for g in range(steps):
+    for g in range(r // ib):
         left = residues(l_ref, r, s, g * ib, ib)
         hi = left.astype(BF16).astype(F32)
         hi, lo = split(dot(jnp.concatenate([hi, left - hi, hi], axis=1).astype(BF16), wcat[...]))
@@ -85,23 +71,51 @@
                 tlo_ref[b * s : (b + 1) * s, q * k : (q + 1) * k] = lo[rows, lanes]
     copy.wait()
 
-    def scale(p, ghi, glo, g):
+
+def t_call(d, left, wf, ib, s):
+    r, total, k = d.shape
+    w = left.shape[1]
+    return call(
+        functools.partial(t_kernel, ib=ib, s=s),
+        "left_by_weights",
+        4.0,
+        12,
+        in_specs=[VM, VM, ANY],
+        out_specs=[VM] * 3,
+        out_shape=[pltpu.VMEM((w * s, r * k), BF16)] * 2 + [pltpu.VMEM(d.shape, F32)],
+        scratch_shapes=[pltpu.VMEM((3 * w, w * k), BF16), pltpu.SemaphoreType.DMA],
+    )(left, wf, pltpu.with_memory_space_constraint(d, pltpu.HBM))
+
+
+def b_kernel(me_ref, dv, thi_ref, tlo_ref, m_ref, own_ref, out_ref, ghi, glo, f_ref, *, ib, offs, rb, s, part):
+    r, total, k = dv.shape
+    per = len(offs) // 2
+    steps = r // ib
+    me = me_ref[0]
+
+    every = m_ref[...].astype(BF16)
+    lane = lax.broadcasted_iota(jnp.int32, own_ref.shape, 1)
+    p = part
+    size = every.shape[0]
+    for h in range(2):
+        start = (2 * h + p) * GAP
+        own = pltpu.roll(own_ref[...], start, 1) if start else own_ref[...]
+        keep = jnp.where((lane >= start) & (lane < start + s), own, 0.0).astype(BF16)
+        present = jnp.where(lane == start + s, own, 0.0).astype(BF16)
+        f_ref[h * size : (h + 1) * size] = dot(every, present, NT) / jnp.maximum(dot(every, keep, NT), 1.0)
+
+    def prepare(g):
         for o in range(per):
             src = pl.multiple_of((me ^ offs[p * per + o]) * rb, rb)
             for q in range(g * ib, (g + 1) * ib):
-                hi, lo = split(dv_ref[q, pl.ds(src, rb), :] * f_ref[p, o * rb : (o + 1) * rb, q : q + 1])
+                hi, lo = split(dv[q, pl.ds(src, rb), :] * f_ref[o * rb : (o + 1) * rb, q : q + 1])
                 ghi[o * rb : (o + 1) * rb, q * k : (q + 1) * k] = hi
                 glo[o * rb : (o + 1) * rb, q * k : (q + 1) * k] = lo
 
-    work = [(p, halves, g) for p, halves in ((1, (ob_ref, bhi, blo)), (0, (oa_ref, ahi, alo))) for g in range(steps)]
-
-    def prepare(p, halves, g):
-        scale(p, halves[1], halves[2], g)
-
-    prepare(*work[0])
-    for t, (p, (out_ref, ghi, glo), g) in enumerate(work):
-        if t + 1 < len(work):
-            prepare(*work[t + 1])
+    prepare(0)
+    for g in range(steps):
+        if g + 1 < steps:
+            prepare(g + 1)
         lanes = slice(g * ib * k, (g + 1) * ib * k)
         hi, lo = ghi[:, lanes], glo[:, lanes]
         rows = hi.shape[0]
@@ -110,26 +124,21 @@
         out_ref[...] = x if g == 0 else out_ref[...] + x
 
 
-def b_call(me, d, masks, own, left, w, offs, rb, ib, s):
+def b_call(me, d, thi, tlo, masks, own, offs, rb, ib, s, part):
     r, total, k = d.shape
-    ws = left.shape[1] * s
+    ws = thi.shape[0]
     rows = total // 2
+    held = [pltpu.with_memory_space_constraint(x, pltpu.VMEM) for x in (d, thi, tlo)]
     return call(
-        functools.partial(b_kernel, ib=ib, offs=offs, rb=rb, s=s),
-        "right_grad",
-        11.0,
-        30,
-        in_specs=[SM, ANY, VM, VM, VM, VM],
-        out_specs=[VM] * 6,
-        out_shape=[pltpu.VMEM((rows, ws), F32)] * 2 + [pltpu.VMEM((rows, r * k), BF16)] * 4,
-        scratch_shapes=[pltpu.VMEM((ws, r * k), BF16)] * 2
-        + [
-            pltpu.VMEM(d.shape, F32),
-            pltpu.VMEM((2, rows, r), F32),
-            pltpu.VMEM((3 * left.shape[1], left.shape[1] * k), BF16),
-            pltpu.SemaphoreType.DMA,
-        ],
-    )(me, pltpu.with_memory_space_constraint(d, pltpu.HBM), masks, own, left, w)
+        functools.partial(b_kernel, ib=ib, offs=offs, rb=rb, s=s, part=part),
+        f"right_grad_{part}",
+        3.7,
+        6,
+        in_specs=[SM] + [VM] * 5,
+        out_specs=[VM] * 3,
+        out_shape=[pltpu.VMEM((rows, ws), F32)] + [pltpu.VMEM((rows, r * k), BF16)] * 2,
+        scratch_shapes=[pltpu.VMEM((rows, r), F32)],
+    )(me, *held, masks, own)
 
 
 def c_kernel(*refs, ib, s, k, steps, blocks, part, parts):
@@ -257,15 +266,16 @@
     both = both * keep[:, :, None]
     left, right = both[:, :, :w].reshape(s * r, w), both[:, :, w:]
     ws = w * s
-    own = jnp.concatenate([keep.T, flags.astype(F32)[:, None], jnp.zeros((r, GAP - 1 - s), F32)], axis=1)
-    own = jnp.concatenate([own, swap(own, 1, n), jnp.zeros((r, k - 2 * GAP), F32)], axis=1)
+    own = jnp.concatenate([valid, flags[None], jnp.zeros((GAP - 1 - s, r), jnp.int32)], axis=0)
+    for bit in (1, 2):
+        own = jnp.concatenate([own, swap(own, bit, n)], axis=0)
+    own = own.T.astype(F32)
+    masks = own
     load = jnp.concatenate([right.transpose(1, 2, 0).reshape(r, ws), own], axis=1)
     for bit in bits[:-2]:
         other = swap(load, bit, n)
-        masks = jnp.concatenate([load[:, ws:], other[:, ws:]], axis=0)
-        load = jnp.concatenate([load, other], axis=0)
-    masks = jnp.concatenate([masks, swap(masks, 2, n)], axis=0)
-    load = after(load[:, :ws], masks)
+        masks = jnp.concatenate([masks, other[:, ws:]], axis=0)
+        load = jnp.concatenate([load[:, :ws], other[:, :ws]] if bit == bits[-3] else [load, other], axis=0)
 
     if r % 16 == 0:
         where, rb, blocks = here, r, offs
@@ -275,27 +285,29 @@
         rb = total // 4
         where, blocks = jnp.zeros((1,), jnp.int32), tuple(range(4))
 
-    near, far, *gs = b_call(where, delta, masks, own, left, wf, blocks, rb, ib, s)
-    load = jnp.concatenate([load, after(swap(load, 2, n), near)], axis=0)
-    rights = (load, swap(load, 1, n))
+    thi, tlo, delta = t_call(delta, after(left, masks), wf, ib, s)
+    far, fhi, flo = b_call(where, delta, thi, tlo, masks, own, blocks, rb, ib, s, 1)
+    load = jnp.concatenate([load, after(swap(load, 2, n), far)], axis=0)
+    near, nhi, nlo = b_call(after(where, load), delta, thi, tlo, masks, own, blocks, rb, ib, s, 0)
+    gs = (nhi, nlo, fhi, flo)
+    rights = (load, after(swap(load, 1, n), near))
 
     def halves(x, y, rows):
         return x[:rows] + y[:rows], x[rows:] + y[rows:]
 
     later = list(reversed(bits[:-1]))
+    quarter = w // 4
     rows = near.shape[0] // 2
-    grad, send = halves(near, swap(far, 1, n), rows)
+    grad, send = halves(near, after(swap(far, 1, n), near), rows)
     left_a, ow_a, send_a = c_call(gs, after(here, grad, send), rights, wf, left, ib, s, 0, parts)
     other_a = swap(send_a, 1, n)
     rows = rows // 2
     grad, send = halves(grad, after(swap(send, later[0], n), left_a), rows)
-    left_b, ow_b, send_b = c_call(gs, after(here, grad, send), rights, wf, left, ib, s, 1, parts)
-
-    quarter = w // 4
-    ow_b = ow_b + swap(send_b, 1, n)
-    ow_a = ow_a + after(other_a, left_b)
-    ow = jnp.concatenate([ow_a[:quarter], ow_b[:quarter]], axis=1)
-    ow_send = jnp.concatenate([ow_a[quarter:], ow_b[quarter:]], axis=1)
+    ow_a, send_a = halves(ow_a, other_a, quarter)
+    left_b, ow_b, send_b = c_call(gs, after(here, grad, send, ow_a, send_a), rights, wf, left, ib, s, 1, parts)
+
+    ow_a = ow_a + after(swap(send_a, 2, n), left_b)
+    ow_b, send_b = halves(ow_b, swap(send_b, 1, n), quarter)
     for bit in later[1:]:
         rows = rows // 2
         other = after(swap(send, bit, n), left_b)
@@ -303,26 +315,28 @@
             grad = grad + other
         else:
             grad, send = halves(grad, other, rows)
-            send = after(send, ow_send)
+    ow_b = ow_b + swap(send_b, 2, n)
 
     left_grad = (left_a + left_b).reshape(r, s, w).transpose(1, 0, 2) * keep[:, :, None]
     right_grad = grad.reshape(r, w, s).transpose(2, 0, 1) * keep[:, :, None]
     grads = jnp.concatenate([left_grad, right_grad], axis=2)
     alignment = jnp.einsum("sic,mc->sim", grads, jnp.concatenate([w1, w2], axis=1), precision=EXACT)
     small = jnp.einsum("sim,sic->cm", activation, grads, precision=EXACT)
-    small = jnp.concatenate([small[:, i : i + k] for i in range(0, m, k)], axis=0).reshape(-1, w, k)
-    ow = ow + swap(ow_send, 2, n)
-    size = small.shape[0]
-    ow = jnp.concatenate([small, ow], axis=0)
-    for bit in reversed(bits[:-2]):
-        ow = ow + swap(ow, bit, n)
-    for bit in (2, 1):
-        other = swap(ow, bit, n)
-        ow = jnp.concatenate([ow[:size] + other[:size], ow[size:], other[size:]], axis=0)
-    small = ow[:size].reshape(m // k, 2 * w, k).transpose(1, 0, 2).reshape(2 * w, m)
-
-    back = pick(jnp.array(PLACES, jnp.int32), (me & 3) ^ jnp.arange(4, dtype=jnp.int32))
-    out_grad = ow[size:].reshape(4, quarter, w, k)
+
+    def finish(x):
+        for bit in reversed(bits[:-2]):
+            x = x + swap(x, bit, n)
+        for bit in (2, 1):
+            x = jnp.concatenate([x, swap(x, bit, n)], axis=0)
+        return x
+
+    ow = jnp.concatenate([finish(ow_a), finish(ow_b)], axis=1)
+    for bit in reversed(bits):
+        small = small + swap(small, bit, n)
+
+    back = (me & 3) ^ jnp.arange(4, dtype=jnp.int32)
+    back = ((back & 1) << 1) | (back >> 1)
+    out_grad = ow.reshape(4, quarter, w, k)
     out_grad = pick(out_grad, back).reshape(w * w, k)
     return alignment, small[:w].T, small[w:].T, out_grad
 

time: 92.9 us -> 81.3 us (0.88)
  waiting for transfers between devices: 41.1 us -> 20.3 us
  starting transfers between devices: 17.1 us -> 27.4 us
  Pallas kernels: 24 us -> 22.9 us
    ppermute x17 -> x26, waiting for transfers between devices: 41.1 us -> 20.3 us  [swap(): return lax.ppermute(x, 'row', [(i, i ^ bit) for i in range(n)])]
    ppermute x17 -> x26, starting transfers between devices: 17.1 us -> 27.4 us  [swap(): return lax.ppermute(x, 'row', [(i, i ^ bit) for i in range(n)])]
    pallas_call x1 -> x3, Pallas kernels: 12.2 us -> 11.1 us  [the longest x2 7.7 us: b_call(): call(functools.partial(b_kernel, ib=ib, offs=offs, rb=rb, s=s, part=part)...]
    gather x2 -> x1, local copies, waits for them, and re-layouts: 2.01 us -> 1.38 us  [pick(): return x.at[index].get(mode='promise_in_bounds')]
  transfers between devices with their start and end apart: 17 -> 26, of which waited for: 13 -> 10; matrix products, arithmetic and copies ran while one was open for 6% -> 7% of each run, Pallas kernels for 26% -> 28%
where the time goes in v4:
time: 81.3 us; the launch traced here: 81 us
  starting transfers between devices  27.4 us (34%)
  Pallas kernels  22.9 us (28%)
  waiting for transfers between devices  20.3 us (25%)
  local copies, waits for them, and re-layouts  4.43 us (5%)
  matrix products  3.43 us (4%)
  other arithmetic  1.5 us (2%)
  between operations  1.03 us (1%)
    ppermute x26, starting transfers between devices, swap(): return lax.ppermute(x, 'row', [(i, i ^ bit) for i in range(n)])  27.4 us
    ppermute x26, waiting for transfers between devices, swap(): return lax.ppermute(x, 'row', [(i, i ^ bit) for i in range(n)])  20.3 us
    pallas_call x2, Pallas kernels, c_call(): call(functools.partial(c_kernel, ib=ib, s=s, k=k, steps=r // ib, blocks=b...  11.8 us
    pallas_call x2, Pallas kernels, b_call(): call(functools.partial(b_kernel, ib=ib, offs=offs, rb=rb, s=s, part=part)...  7.7 us
    pallas_call x1, Pallas kernels, t_call(): call(functools.partial(t_kernel, ib=ib, s=s), 'left_by_weights', 4.0, 12,...  3.44 us
  transfers between devices with their start and end apart: 26, of which 10 were waited for; matrix products, arithmetic and copies ran while one was open for 7% of the time, Pallas kernels for 28%

profile of v4, /device:TPU:0, one launch (start us, length us, event | category | flops | bytes accessed | tf_op | source)
XLA Modules:
  0.0 81.0 jit_solution(11889832401685069375)
XLA Ops:
  0.7 0.9 %copy.25 = s32[16,32]{0,1:T(8,128)S(1)} copy(s32[16,32]{1,0:T(8,128)} %param.8) | data formatting | bytes 4096 | tf_op args[1]
  1.5 0.7 copy.26
  2.8 0.7 convert_element_type.8
  3.5 1.3 %fusion = f32[16,32,64]{2,1,0:T(8,128)S(1)} fusion(f32[16,32,256]{2,1,0:T(8,128)S(1)} %copy-done, f32[16,32]{1,0:T(8,128)S(1)} %convert_element_type.8, f32[256,32]{0,1:T(8,128)} %param.11, f32[256,32]{0,1:T(8,128)} %param.10), kind=kOutput, calls=%fused_computation.2 | convolution fusion | flops 100712448 | bytes 722944 | tf_op jit(solution)/shard_map/sim,mc->sic/dot_general | solution.py:265
  4.9 2.5 %collective-permute-start.1 = (s32[64,32]{0,1:T(8,128)S(1)}, s32[64,32]{0,1:T(8,128)S(1)}, u32[]{:S(2)}, u32[]{:S(2)}) collective-permute-start(s32[64,32]{0,1:T(8,128)S(1)} %pad_add_fusion.1), channel_id=1, source_target_pairs={{0,2},{1,3},{2,0},{3,1},{4,6},{5,7},{6,4},{7,5},{8,10},{9,11},{10,... | collective-permute-start | bytes 24584 | tf_op jit(solution)/shard_map/ppermute | solution.py:229
  7.9 1.3 %collective-permute-done.1 = s32[64,32]{0,1:T(8,128)S(1)} collective-permute-done((s32[64,32]{0,1:T(8,128)S(1)}, s32[64,32]{0,1:T(8,128)S(1)}, u32[]{:S(2)}, u32[]{:S(2)}) %collective-permute-start.1) | collective-permute-done | bytes 8224 | tf_op jit(solution)/shard_map/ppermute | solution.py:229
  9.3 3.2 %collective-permute-start.2 = (f32[32,640]{1,0:T(8,128)S(1)}, f32[32,640]{1,0:T(8,128)S(1)}, u32[]{:S(2)}, u32[]{:S(2)}) collective-permute-start(f32[32,640]{1,0:T(8,128)S(1)} %pad_maximum_fusion.8), channel_id=1, source_target_pairs={{0,8},{1,9},{2,10},{3,11},{4,12},{5,13},{6,14},{7,15},{8,0},{9,1},... | collective-permute-start | bytes 245768 | tf_op jit(solution)/shard_map/ppermute | solution.py:229
  12.5 4.0 %collective-permute-done.2 = f32[32,640]{1,0:T(8,128)S(1)} collective-permute-done((f32[32,640]{1,0:T(8,128)S(1)}, f32[32,640]{1,0:T(8,128)S(1)}, u32[]{:S(2)}, u32[]{:S(2)}) %collective-permute-start.2) | collective-permute-done | bytes 81952 | tf_op jit(solution)/shard_map/ppermute | solution.py:229
  17.0 4.9 %collective-permute-done.3 = f32[64,640]{1,0:T(8,128)S(1)} collective-permute-done((f32[64,640]{1,0:T(8,128)S(1)}, f32[64,640]{1,0:T(8,128)S(1)}, u32[]{:S(2)}, u32[]{:S(2)}) %collective-permute-start.3) | collective-permute-done | bytes 163872 | tf_op jit(solution)/shard_map/ppermute | solution.py:229
  21.9 1.6 %collective-permute-start.4 = (f32[128,512]{1,0:T(8,128)S(1)}, f32[128,512]{1,0:T(8,128)S(1)}, u32[]{:S(2)}, u32[]{:S(2)}) collective-permute-start(f32[128,512]{1,0:T(8,128)S(1)} %pad_maximum_fusion.1), channel_id=1, source_target_pairs={{0,2},{1,3},{2,0},{3,1},{4,6},{5,7},{6,4},{7,5},{8,10},{9,11},{10,... | collective-permute-start | bytes 786440 | tf_op jit(solution)/shard_map/ppermute | solution.py:229
  23.5 3.4 %left_by_weights.1 = (bf16[512,4096]{1,0:T(8,128)(2,1)S(1)}, bf16[512,4096]{1,0:T(8,128)(2,1)S(1)}, f32[32,512,128]{2,1,0:T(8,128)S(1)}) custom-call(f32[512,32]{1,0:T(8,128)S(1)} %bitcast.32, f32[1024,128]{1,0:T(8,128)S(1)} %copy-done.1, f32[32,512,128]{2,1,0:T(8,128)} %d_ref.1), custom_call_target="tpu_custom_call" | custom-call | flops 4000000000 | tf_op jit(solution)/shard_map/left_by_weights/pallas_call | solution.py:78
  26.9 3.9 %right_grad_1.1 = (f32[256,512]{1,0:T(8,128)S(1)}, bf16[256,4096]{1,0:T(8,128)(2,1)S(1)}, bf16[256,4096]{1,0:T(8,128)(2,1)S(1)}) custom-call(s32[1]{0:T(128)} %bitcast.me_ref.refs_4_, f32[32,512,128]{2,1,0:T(8,128)S(1)} %get-tuple-element.31.dv, bf16[512,4096]{1,0:T(8,128)(2,1)S(1)} %get-tuple-element.32.thi_ref, ...), custom_call_target="tpu_custom_call" | custom-call | flops 3700000000 | tf_op jit(solution)/shard_map/right_grad_1/pallas_call | solution.py:132
  31.5 3.8 %right_grad_0.1 = (f32[256,512]{1,0:T(8,128)S(1)}, bf16[256,4096]{1,0:T(8,128)(2,1)S(1)}, bf16[256,4096]{1,0:T(8,128)(2,1)S(1)}) custom-call(s32[1]{0:T(128)} %bitcast.me_ref.refs_4_, f32[32,512,128]{2,1,0:T(8,128)S(1)} %get-tuple-element.31.dv, bf16[512,4096]{1,0:T(8,128)(2,1)S(1)} %get-tuple-element.32.thi_ref, ...), custom_call_target="tpu_custom_call" | custom-call | flops 3700000000 | tf_op jit(solution)/shard_map/right_grad_0/pallas_call | solution.py:132
  36.0 6.0 %left_and_weight_grad_0.1 = (f32[512,32]{1,0:T(8,128)S(1)}, f32[16,16,128]{2,1,0:T(8,128)S(1)}, f32[16,16,128]{2,1,0:T(8,128)S(1)}) custom-call(bf16[256,4096]{1,0:T(8,128)(2,1)S(1)} %get-tuple-element.37.refs_0_, bf16[256,4096]{1,0:T(8,128)(2,1)S(1)} %get-tuple-element.38.refs_1_, bf16[256,4096]{1,0:T(8,128)(2,1)S(1)} %get-tuple-element.39.refs_2_, ...), custom_call_target="tpu_custom_call" | custom-call | flops 5600000000 | tf_op jit(solution)/shard_map/left_and_weight_grad_0/pallas_call | solution.py:213
  42.1 1.6 %collective-permute-done.7 = f32[128,512]{1,0:T(8,128)S(1)} collective-permute-done((f32[128,512]{1,0:T(8,128)S(1)}, f32[128,512]{1,0:T(8,128)S(1)}, u32[]{:S(2)}, u32[]{:S(2)}) %collective-permute-start.7) | collective-permute-done | bytes 262176 | tf_op jit(solution)/shard_map/ppermute | solution.py:229
  44.3 0.7 collective-permute-start.15
  45.0 5.8 %left_and_weight_grad_1.1 = (f32[512,32]{1,0:T(8,128)S(1)}, f32[16,16,128]{2,1,0:T(8,128)S(1)}, f32[16,16,128]{2,1,0:T(8,128)S(1)}) custom-call(bf16[256,4096]{1,0:T(8,128)(2,1)S(1)} %get-tuple-element.37.refs_0_, bf16[256,4096]{1,0:T(8,128)(2,1)S(1)} %get-tuple-element.38.refs_1_, bf16[256,4096]{1,0:T(8,128)(2,1)S(1)} %get-tuple-element.39.refs_2_, ...), custom_call_target="tpu_custom_call" | custom-call | flops 5600000000 | tf_op jit(solution)/shard_map/left_and_weight_grad_1/pallas_call | solution.py:213
  50.9 3.3 %collective-permute-start.10 = (f32[32,512]{1,0:T(8,128)S(1)}, f32[32,512]{1,0:T(8,128)S(1)}, u32[]{:S(2)}, u32[]{:S(2)}) collective-permute-start(f32[32,512]{1,0:T(8,128)S(1)} %slice_add_fusion.6), channel_id=1, source_target_pairs={{0,8},{1,9},{2,10},{3,11},{4,12},{5,13},{6,14},{7,15},{8,0},{9,1},... | collective-permute-start | bytes 196616 | tf_op jit(solution)/shard_map/ppermute | solution.py:229
  54.3 0.6 collective-permute-start.16
  55.0 2.2 %collective-permute-done.10 = f32[32,512]{1,0:T(8,128)S(1)} collective-permute-done((f32[32,512]{1,0:T(8,128)S(1)}, f32[32,512]{1,0:T(8,128)S(1)}, u32[]{:S(2)}, u32[]{:S(2)}) %collective-permute-start.10) | collective-permute-done | bytes 65568 | tf_op jit(solution)/shard_map/ppermute | solution.py:229
  57.6 0.7 convolution_bitcast_fusion
  58.4 1.5 %collective-permute-start.21 = (f32[8,16,128]{2,1,0:T(8,128)S(1)}, f32[8,16,128]{2,1,0:T(8,128)S(1)}, u32[]{:S(2)}, u32[]{:S(2)}) collective-permute-start(f32[8,16,128]{2,1,0:T(8,128)S(1)} %slice_add_fusion.4), channel_id=1, source_target_pairs={{0,2},{1,3},{2,0},{3,1},{4,6},{5,7},{6,4},{7,5},{8,10},{9,11},{10,... | collective-permute-start | bytes 196616 | tf_op jit(solution)/shard_map/ppermute | solution.py:229
  60.0 3.0 %collective-permute-start.17 = (f32[8,16,128]{2,1,0:T(8,128)S(1)}, f32[8,16,128]{2,1,0:T(8,128)S(1)}, u32[]{:S(2)}, u32[]{:S(2)}) collective-permute-start(f32[8,16,128]{2,1,0:T(8,128)S(1)} %add.91), channel_id=1, source_target_pairs={{0,8},{1,9},{2,10},{3,11},{4,12},{5,13},{6,14},{7,15},{8,0},{9,1},... | collective-permute-start | bytes 196616 | tf_op jit(solution)/shard_map/ppermute | solution.py:229
  63.3 1.0 %collective-permute-start.22 = (f32[8,16,128]{2,1,0:T(8,128)S(1)}, f32[8,16,128]{2,1,0:T(8,128)S(1)}, u32[]{:S(2)}, u32[]{:S(2)}) collective-permute-start(f32[8,16,128]{2,1,0:T(8,128)S(1)} %fusion.2), channel_id=1, source_target_pairs={{0,4},{1,5},{2,6},{3,7},{4,0},{5,1},{6,2},{7,3},{8,12},{9,13},{10,... | collective-permute-start | bytes 196616 | tf_op jit(solution)/shard_map/ppermute | solution.py:229
  64.3 2.4 %collective-permute-done.17 = f32[8,16,128]{2,1,0:T(8,128)S(1)} collective-permute-done((f32[8,16,128]{2,1,0:T(8,128)S(1)}, f32[8,16,128]{2,1,0:T(8,128)S(1)}, u32[]{:S(2)}, u32[]{:S(2)}) %collective-permute-start.17) | collective-permute-done | bytes 65568 | tf_op jit(solution)/shard_map/ppermute | solution.py:229
  68.0 3.0 %collective-permute-start.23 = (f32[8,16,128]{2,1,0:T(8,128)S(1)}, f32[8,16,128]{2,1,0:T(8,128)S(1)}, u32[]{:S(2)}, u32[]{:S(2)}) collective-permute-start(f32[8,16,128]{2,1,0:T(8,128)S(1)} %add.96), channel_id=1, source_target_pairs={{0,8},{1,9},{2,10},{3,11},{4,12},{5,13},{6,14},{7,15},{8,0},{9,1},... | collective-permute-start | bytes 196616 | tf_op jit(solution)/shard_map/ppermute | solution.py:229
  70.9 1.4 %fusion.1 = f32[16,32,256]{2,1,0:T(8,128)} fusion(f32[16,32,32]{2,1,0:T(8,128)S(1)} %get-tuple-element.67, f32[16,32,32]{2,1,0:T(8,128)S(1)} %get-tuple-element.66, f32[256,32]{0,1:T(8,128)S(1)} %copy-done.2, f32[256,32]{0,1:T(8,128)S(1)} %copy-done.3), kind=kOutput, calls=%fused_computation.18 | convolution fusion | flops 100712448 | bytes 720896 | tf_op jit(solution)/shard_map/sic,mc->sim/dot_general | solution.py:323
  72.4 1.2 %collective-permute-start.14 = (f32[64,256]{1,0:T(8,128)S(1)}, f32[64,256]{1,0:T(8,128)S(1)}, u32[]{:S(2)}, u32[]{:S(2)}) collective-permute-start(f32[64,256]{1,0:T(8,128)S(1)} %add.88), channel_id=1, source_target_pairs={{0,8},{1,9},{2,10},{3,11},{4,12},{5,13},{6,14},{7,15},{8,0},{9,1},... | collective-permute-start | bytes 196616 | tf_op jit(solution)/shard_map/ppermute | solution.py:229
  73.6 1.8 %collective-permute-start.24 = (f32[8,16,128]{2,1,0:T(8,128)S(1)}, f32[8,16,128]{2,1,0:T(8,128)S(1)}, u32[]{:S(2)}, u32[]{:S(2)}) collective-permute-start(f32[8,16,128]{2,1,0:T(8,128)S(1)} %add.97), channel_id=1, source_target_pairs={{0,2},{1,3},{2,0},{3,1},{4,6},{5,7},{6,4},{7,5},{8,10},{9,11},{10,... | collective-permute-start | bytes 196616 | tf_op jit(solution)/shard_map/ppermute | solution.py:229
  75.5 2.6 %collective-permute-done.14 = f32[64,256]{1,0:T(8,128)S(1)} collective-permute-done((f32[64,256]{1,0:T(8,128)S(1)}, f32[64,256]{1,0:T(8,128)S(1)}, u32[]{:S(2)}, u32[]{:S(2)}) %collective-permute-start.14) | collective-permute-done | bytes 65568 | tf_op jit(solution)/shard_map/ppermute | solution.py:229
  78.9 0.7 collective-permute-done.25
  79.6 1.4 %gather_fusion = f32[4,8,32,128]{3,2,1,0:T(8,128)} fusion(f32[4,8,32,128]{3,2,1,0:T(8,128)S(1)} %bitcast.35, s32[1024]{0:T(1024)S(1)} %pad_clamp_fusion), kind=kCustom, calls=%fused_computation | custom fusion | bytes 1048592 | tf_op jit(solution)/shard_map/gather | solution.py:246
  (83 shorter events, 6.9 us)
Async XLA Ops:
  0.6 2.9 %copy-start = (f32[16,32,256]{2,1,0:T(8,128)S(1)}, f32[16,32,256]{2,1,0:T(8,128)}, u32[]{:S(2)}) copy-start(f32[16,32,256]{2,1,0:T(8,128)} %param.7) | copy-start | bytes 1572868
  0.6 22.8 %copy-start.1 = (f32[1024,128]{1,0:T(8,128)S(1)}, f32[1024,128]{1,0:T(8,128)}, u32[]{:S(2)}) copy-start(f32[1024,128]{1,0:T(8,128)} %refs_7_.3) | copy-start | bytes 1572868
  2.3 2.5 %collective-permute-start = (s32[32,32]{0,1:T(8,128)S(1)}, s32[32,32]{0,1:T(8,128)S(1)}, u32[]{:S(2)}, u32[]{:S(2)}) collective-permute-start(s32[32,32]{0,1:T(8,128)S(1)} %pad_add_fusion), channel_id=1, source_target_pairs={{0,1},{1,0},{2,3},{3,2},{4,5},{5,4},{6,7},{7,6},{8,9},{9,8},{10,11... | collective-permute-start | bytes 12296 | tf_op jit(solution)/shard_map/ppermute | solution.py:229
  4.9 4.2 %collective-permute-start.1 = (s32[64,32]{0,1:T(8,128)S(1)}, s32[64,32]{0,1:T(8,128)S(1)}, u32[]{:S(2)}, u32[]{:S(2)}) collective-permute-start(s32[64,32]{0,1:T(8,128)S(1)} %pad_add_fusion.1), channel_id=1, source_target_pairs={{0,2},{1,3},{2,0},{3,1},{4,6},{5,7},{6,4},{7,5},{8,10},{9,11},{10,... | collective-permute-start | bytes 24584 | tf_op jit(solution)/shard_map/ppermute | solution.py:229
  9.3 7.2 %collective-permute-start.2 = (f32[32,640]{1,0:T(8,128)S(1)}, f32[32,640]{1,0:T(8,128)S(1)}, u32[]{:S(2)}, u32[]{:S(2)}) collective-permute-start(f32[32,640]{1,0:T(8,128)S(1)} %pad_maximum_fusion.8), channel_id=1, source_target_pairs={{0,8},{1,9},{2,10},{3,11},{4,12},{5,13},{6,14},{7,15},{8,0},{9,1},... | collective-permute-start | bytes 245768 | tf_op jit(solution)/shard_map/ppermute | solution.py:229
  16.5 5.4 %collective-permute-start.3 = (f32[64,640]{1,0:T(8,128)S(1)}, f32[64,640]{1,0:T(8,128)S(1)}, u32[]{:S(2)}, u32[]{:S(2)}) collective-permute-start(f32[64,640]{1,0:T(8,128)S(1)} %pad_maximum_fusion.3), channel_id=1, source_target_pairs={{0,4},{1,5},{2,6},{3,7},{4,0},{5,1},{6,2},{7,3},{8,12},{9,13},{10,... | collective-permute-start | bytes 491528 | tf_op jit(solution)/shard_map/ppermute | solution.py:229
  21.9 9.0 %collective-permute-start.4 = (f32[128,512]{1,0:T(8,128)S(1)}, f32[128,512]{1,0:T(8,128)S(1)}, u32[]{:S(2)}, u32[]{:S(2)}) collective-permute-start(f32[128,512]{1,0:T(8,128)S(1)} %pad_maximum_fusion.1), channel_id=1, source_target_pairs={{0,2},{1,3},{2,0},{3,1},{4,6},{5,7},{6,4},{7,5},{8,10},{9,11},{10,... | collective-permute-start | bytes 786440 | tf_op jit(solution)/shard_map/ppermute | solution.py:229
  30.8 4.5 %collective-permute-start.5 = (f32[256,512]{1,0:T(8,128)S(1)}, f32[256,512]{1,0:T(8,128)S(1)}, u32[]{:S(2)}, u32[]{:S(2)}) collective-permute-start(f32[256,512]{1,0:T(8,128)S(1)} %get-tuple-element.34), channel_id=1, source_target_pairs={{0,1},{1,0},{2,3},{3,2},{4,5},{5,4},{6,7},{7,6},{8,9},{9,8},{10,11... | collective-permute-start | bytes 1572872 | tf_op jit(solution)/shard_map/ppermute | solution.py:229
  30.9 5.1 %collective-permute-start.6 = (f32[256,512]{1,0:T(8,128)S(1)}, f32[256,512]{1,0:T(8,128)S(1)}, u32[]{:S(2)}, u32[]{:S(2)}) collective-permute-start(f32[256,512]{1,0:T(8,128)S(1)} %pad_maximum_fusion.refs_5_), channel_id=1, source_target_pairs={{0,1},{1,0},{2,3},{3,2},{4,5},{5,4},{6,7},{7,6},{8,9},{9,8},{10,11... | collective-permute-start | bytes 1572872 | tf_op jit(solution)/shard_map/ppermute | solution.py:229
  35.4 8.3 %collective-permute-start.7 = (f32[128,512]{1,0:T(8,128)S(1)}, f32[128,512]{1,0:T(8,128)S(1)}, u32[]{:S(2)}, u32[]{:S(2)}) collective-permute-start(f32[128,512]{1,0:T(8,128)S(1)} %get-tuple-element.56), channel_id=1, source_target_pairs={{0,2},{1,3},{2,0},{3,1},{4,6},{5,7},{6,4},{7,5},{8,10},{9,11},{10,... | collective-permute-start | bytes 786440 | tf_op jit(solution)/shard_map/ppermute | solution.py:229
  42.0 2.2 %collective-permute-start.8 = (f32[16,16,128]{2,1,0:T(8,128)S(1)}, f32[16,16,128]{2,1,0:T(8,128)S(1)}, u32[]{:S(2)}, u32[]{:S(2)}) collective-permute-start(f32[16,16,128]{2,1,0:T(8,128)S(1)} %get-tuple-element.48), channel_id=1, source_target_pairs={{0,1},{1,0},{2,3},{3,2},{4,5},{5,4},{6,7},{7,6},{8,9},{9,8},{10,11... | collective-permute-start | bytes 393224 | tf_op jit(solution)/shard_map/ppermute | solution.py:229
  43.8 7.1 %collective-permute-start.9 = (f32[64,512]{1,0:T(8,128)S(1)}, f32[64,512]{1,0:T(8,128)S(1)}, u32[]{:S(2)}, u32[]{:S(2)}) collective-permute-start(f32[64,512]{1,0:T(8,128)S(1)} %get-tuple-element.58), channel_id=1, source_target_pairs={{0,4},{1,5},{2,6},{3,7},{4,0},{5,1},{6,2},{7,3},{8,12},{9,13},{10,... | collective-permute-start | bytes 393224 | tf_op jit(solution)/shard_map/ppermute | solution.py:229
  44.3 10.0 %collective-permute-start.15 = (f32[8,16,128]{2,1,0:T(8,128)S(1)}, f32[8,16,128]{2,1,0:T(8,128)S(1)}, u32[]{:S(2)}, u32[]{:S(2)}) collective-permute-start(f32[8,16,128]{2,1,0:T(8,128)S(1)} %get-tuple-element.60), channel_id=1, source_target_pairs={{0,2},{1,3},{2,0},{3,1},{4,6},{5,7},{6,4},{7,5},{8,10},{9,11},{10,... | collective-permute-start | bytes 196616 | tf_op jit(solution)/shard_map/ppermute | solution.py:229
  50.8 20.1 %copy-start.2 = (f32[256,32]{0,1:T(8,128)S(1)}, f32[256,32]{0,1:T(8,128)}, u32[]{:S(2)}) copy-start(f32[256,32]{0,1:T(8,128)} %param.11) | copy-start | bytes 98308
  50.8 20.1 %copy-start.3 = (f32[256,32]{0,1:T(8,128)S(1)}, f32[256,32]{0,1:T(8,128)}, u32[]{:S(2)}) copy-start(f32[256,32]{0,1:T(8,128)} %param.10) | copy-start | bytes 98308
  50.9 6.3 %collective-permute-start.10 = (f32[32,512]{1,0:T(8,128)S(1)}, f32[32,512]{1,0:T(8,128)S(1)}, u32[]{:S(2)}, u32[]{:S(2)}) collective-permute-start(f32[32,512]{1,0:T(8,128)S(1)} %slice_add_fusion.6), channel_id=1, source_target_pairs={{0,8},{1,9},{2,10},{3,11},{4,12},{5,13},{6,14},{7,15},{8,0},{9,1},... | collective-permute-start | bytes 196616 | tf_op jit(solution)/shard_map/ppermute | solution.py:229
  54.2 4.2 %collective-permute-start.20 = (f32[16,16,128]{2,1,0:T(8,128)S(1)}, f32[16,16,128]{2,1,0:T(8,128)S(1)}, u32[]{:S(2)}, u32[]{:S(2)}) collective-permute-start(f32[16,16,128]{2,1,0:T(8,128)S(1)} %get-tuple-element.55), channel_id=1, source_target_pairs={{0,1},{1,0},{2,3},{3,2},{4,5},{5,4},{6,7},{7,6},{8,9},{9,8},{10,11... | collective-permute-start | bytes 393224 | tf_op jit(solution)/shard_map/ppermute | solution.py:229
  54.3 5.7 %collective-permute-start.16 = (f32[8,16,128]{2,1,0:T(8,128)S(1)}, f32[8,16,128]{2,1,0:T(8,128)S(1)}, u32[]{:S(2)}, u32[]{:S(2)}) collective-permute-start(f32[8,16,128]{2,1,0:T(8,128)S(1)} %add.90), channel_id=1, source_target_pairs={{0,4},{1,5},{2,6},{3,7},{4,0},{5,1},{6,2},{7,3},{8,12},{9,13},{10,... | collective-permute-start | bytes 196616 | tf_op jit(solution)/shard_map/ppermute | solution.py:229
  58.3 4.7 %collective-permute-start.11 = (f32[64,256]{1,0:T(8,128)S(1)}, f32[64,256]{1,0:T(8,128)S(1)}, u32[]{:S(2)}, u32[]{:S(2)}) collective-permute-start(f32[64,256]{1,0:T(8,128)S(1)} %convolution_bitcast_fusion), channel_id=1, source_target_pairs={{0,1},{1,0},{2,3},{3,2},{4,5},{5,4},{6,7},{7,6},{8,9},{9,8},{10,11... | collective-permute-start | bytes 196616 | tf_op jit(solution)/shard_map/ppermute | solution.py:229
  58.4 4.9 %collective-permute-start.21 = (f32[8,16,128]{2,1,0:T(8,128)S(1)}, f32[8,16,128]{2,1,0:T(8,128)S(1)}, u32[]{:S(2)}, u32[]{:S(2)}) collective-permute-start(f32[8,16,128]{2,1,0:T(8,128)S(1)} %slice_add_fusion.4), channel_id=1, source_target_pairs={{0,2},{1,3},{2,0},{3,1},{4,6},{5,7},{6,4},{7,5},{8,10},{9,11},{10,... | collective-permute-start | bytes 196616 | tf_op jit(solution)/shard_map/ppermute | solution.py:229
  60.0 6.7 %collective-permute-start.17 = (f32[8,16,128]{2,1,0:T(8,128)S(1)}, f32[8,16,128]{2,1,0:T(8,128)S(1)}, u32[]{:S(2)}, u32[]{:S(2)}) collective-permute-start(f32[8,16,128]{2,1,0:T(8,128)S(1)} %add.91), channel_id=1, source_target_pairs={{0,8},{1,9},{2,10},{3,11},{4,12},{5,13},{6,14},{7,15},{8,0},{9,1},... | collective-permute-start | bytes 196616 | tf_op jit(solution)/shard_map/ppermute | solution.py:229
  63.0 4.3 %collective-permute-start.12 = (f32[64,256]{1,0:T(8,128)S(1)}, f32[64,256]{1,0:T(8,128)S(1)}, u32[]{:S(2)}, u32[]{:S(2)}) collective-permute-start(f32[64,256]{1,0:T(8,128)S(1)} %add.86), channel_id=1, source_target_pairs={{0,2},{1,3},{2,0},{3,1},{4,6},{5,7},{6,4},{7,5},{8,10},{9,11},{10,... | collective-permute-start | bytes 196616 | tf_op jit(solution)/shard_map/ppermute | solution.py:229
  63.3 4.7 %collective-permute-start.22 = (f32[8,16,128]{2,1,0:T(8,128)S(1)}, f32[8,16,128]{2,1,0:T(8,128)S(1)}, u32[]{:S(2)}, u32[]{:S(2)}) collective-permute-start(f32[8,16,128]{2,1,0:T(8,128)S(1)} %fusion.2), channel_id=1, source_target_pairs={{0,4},{1,5},{2,6},{3,7},{4,0},{5,1},{6,2},{7,3},{8,12},{9,13},{10,... | collective-permute-start | bytes 196616 | tf_op jit(solution)/shard_map/ppermute | solution.py:229
  66.7 8.8 %collective-permute-start.18 = (f32[8,16,128]{2,1,0:T(8,128)S(1)}, f32[8,16,128]{2,1,0:T(8,128)S(1)}, u32[]{:S(2)}, u32[]{:S(2)}) collective-permute-start(f32[8,16,128]{2,1,0:T(8,128)S(1)} %add.92), channel_id=1, source_target_pairs={{0,2},{1,3},{2,0},{3,1},{4,6},{5,7},{6,4},{7,5},{8,10},{9,11},{10,... | collective-permute-start | bytes 196616 | tf_op jit(solution)/shard_map/ppermute | solution.py:229
  67.3 5.0 %collective-permute-start.13 = (f32[64,256]{1,0:T(8,128)S(1)}, f32[64,256]{1,0:T(8,128)S(1)}, u32[]{:S(2)}, u32[]{:S(2)}) collective-permute-start(f32[64,256]{1,0:T(8,128)S(1)} %add.87), channel_id=1, source_target_pairs={{0,4},{1,5},{2,6},{3,7},{4,0},{5,1},{6,2},{7,3},{8,12},{9,13},{10,... | collective-permute-start | bytes 196616 | tf_op jit(solution)/shard_map/ppermute | solution.py:229
  68.0 5.6 %collective-permute-start.23 = (f32[8,16,128]{2,1,0:T(8,128)S(1)}, f32[8,16,128]{2,1,0:T(8,128)S(1)}, u32[]{:S(2)}, u32[]{:S(2)}) collective-permute-start(f32[8,16,128]{2,1,0:T(8,128)S(1)} %add.96), channel_id=1, source_target_pairs={{0,8},{1,9},{2,10},{3,11},{4,12},{5,13},{6,14},{7,15},{8,0},{9,1},... | collective-permute-start | bytes 196616 | tf_op jit(solution)/shard_map/ppermute | solution.py:229
  72.4 5.7 %collective-permute-start.14 = (f32[64,256]{1,0:T(8,128)S(1)}, f32[64,256]{1,0:T(8,128)S(1)}, u32[]{:S(2)}, u32[]{:S(2)}) collective-permute-start(f32[64,256]{1,0:T(8,128)S(1)} %add.88), channel_id=1, source_target_pairs={{0,8},{1,9},{2,10},{3,11},{4,12},{5,13},{6,14},{7,15},{8,0},{9,1},... | collective-permute-start | bytes 196616 | tf_op jit(solution)/shard_map/ppermute | solution.py:229
  73.6 4.5 %collective-permute-start.24 = (f32[8,16,128]{2,1,0:T(8,128)S(1)}, f32[8,16,128]{2,1,0:T(8,128)S(1)}, u32[]{:S(2)}, u32[]{:S(2)}) collective-permute-start(f32[8,16,128]{2,1,0:T(8,128)S(1)} %add.97), channel_id=1, source_target_pairs={{0,2},{1,3},{2,0},{3,1},{4,6},{5,7},{6,4},{7,5},{8,10},{9,11},{10,... | collective-permute-start | bytes 196616 | tf_op jit(solution)/shard_map/ppermute | solution.py:229
  75.5 3.4 %collective-permute-start.19 = (f32[16,16,128]{2,1,0:T(8,128)S(1)}, f32[16,16,128]{2,1,0:T(8,128)S(1)}, u32[]{:S(2)}, u32[]{:S(2)}) collective-permute-start(f32[16,16,128]{2,1,0:T(8,128)S(1)} %pad_maximum_fusion.4), channel_id=1, source_target_pairs={{0,1},{1,0},{2,3},{3,2},{4,5},{5,4},{6,7},{7,6},{8,9},{9,8},{10,11... | collective-permute-start | bytes 393224 | tf_op jit(solution)/shard_map/ppermute | solution.py:229
  78.2 1.4 %collective-permute-start.25 = (f32[16,16,128]{2,1,0:T(8,128)S(1)}, f32[16,16,128]{2,1,0:T(8,128)S(1)}, u32[]{:S(2)}, u32[]{:S(2)}) collective-permute-start(f32[16,16,128]{2,1,0:T(8,128)S(1)} %pad_maximum_fusion.5), channel_id=1, source_target_pairs={{0,1},{1,0},{2,3},{3,2},{4,5},{5,4},{6,7},{7,6},{8,9},{9,8},{10,11... | collective-permute-start | bytes 393224 | tf_op jit(solution)/shard_map/ppermute | solution.py:229

commit v5 on v4

--- a/solution.py
+++ b/solution.py
@@ -5,6 +5,7 @@
 from jax import lax
 from jax.experimental import pallas as pl
 from jax.experimental.pallas import tpu as pltpu
+from jax.experimental.layout import Layout, with_layout_constraint
 from jax.sharding import PartitionSpec as P
 
 EXACT = lax.Precision.HIGHEST
@@ -225,6 +226,38 @@
     )(*gs, me, *rights, w2, left)
 
 
+def place_kernel(me_ref, *refs, parts):
+    sources, (out_ref, sems) = refs[: 2 * parts], refs[2 * parts :]
+    rows, wide = sources[0].shape[:2]
+    quarter = rows // 2
+    copies = []
+    for part in range(parts):
+        for q, place in enumerate(PLACES):
+            source = sources[2 * part + q // 2].at[pl.ds((q % 2) * quarter, quarter)]
+            at = pl.multiple_of(((me_ref[0] & 3) ^ place) * quarter, quarter)
+            target = out_ref.at[pl.ds(at, quarter), pl.ds(part * wide, wide)]
+            copies.append(pltpu.make_async_copy(source, target, sems.at[4 * part + q]))
+    for copy in copies:
+        copy.start()
+    for copy in copies:
+        copy.wait()
+
+
+def place_call(me, sources):
+    parts = len(sources) // 2
+    rows, wide, k = sources[0].shape
+    return call(
+        functools.partial(place_kernel, parts=parts),
+        "place_weight_grad",
+        0.8,
+        4,
+        in_specs=[SM] + [VM] * len(sources),
+        out_specs=ANY,
+        out_shape=jax.ShapeDtypeStruct((2 * rows, parts * wide, k), F32),
+        scratch_shapes=[pltpu.SemaphoreType.DMA((4 * parts,))],
+    )(me, *sources)
+
+
 def swap(x, bit, n):
     return lax.ppermute(x, "row", [(i, i ^ bit) for i in range(n)])
 
@@ -240,10 +273,6 @@
     for bit in bits:
         offs = offs + [o ^ bit for o in offs]
     return tuple(offs)
-
-
-def pick(x, index):
-    return x.at[index].get(mode="promise_in_bounds")
 
 
 def after(x, *others):
@@ -267,6 +296,7 @@
     left, right = both[:, :, :w].reshape(s * r, w), both[:, :, w:]
     ws = w * s
     own = jnp.concatenate([valid, flags[None], jnp.zeros((GAP - 1 - s, r), jnp.int32)], axis=0)
+    own = with_layout_constraint(own, Layout(major_to_minor=(0, 1)))
     for bit in (1, 2):
         own = jnp.concatenate([own, swap(own, bit, n)], axis=0)
     own = own.T.astype(F32)
@@ -320,24 +350,25 @@
     left_grad = (left_a + left_b).reshape(r, s, w).transpose(1, 0, 2) * keep[:, :, None]
     right_grad = grad.reshape(r, w, s).transpose(2, 0, 1) * keep[:, :, None]
     grads = jnp.concatenate([left_grad, right_grad], axis=2)
-    alignment = jnp.einsum("sic,mc->sim", grads, jnp.concatenate([w1, w2], axis=1), precision=EXACT)
     small = jnp.einsum("sim,sic->cm", activation, grads, precision=EXACT)
 
     def finish(x):
         for bit in reversed(bits[:-2]):
             x = x + swap(x, bit, n)
-        for bit in (2, 1):
-            x = jnp.concatenate([x, swap(x, bit, n)], axis=0)
         return x
 
-    ow = jnp.concatenate([finish(ow_a), finish(ow_b)], axis=1)
+    def spread(x):
+        x = jnp.concatenate([x, swap(x, 2, n)], axis=0)
+        return [x, swap(x, 1, n)]
+
+    ow_a = spread(finish(ow_a))
+    ow_b = finish(ow_b)
+    grads = after(grads, ow_b)
+    alignment = jnp.einsum("sic,mc->sim", grads, jnp.concatenate([w1, w2], axis=1), precision=EXACT)
     for bit in reversed(bits):
         small = small + swap(small, bit, n)
 
-    back = (me & 3) ^ jnp.arange(4, dtype=jnp.int32)
-    back = ((back & 1) << 1) | (back >> 1)
-    out_grad = ow.reshape(4, quarter, w, k)
-    out_grad = pick(out_grad, back).reshape(w * w, k)
+    out_grad = place_call(here, ow_a + spread(ow_b)).reshape(w * w, k)
     return alignment, small[:w].T, small[w:].T, out_grad
 
 

time: 81.3 us -> 80 us (0.984)
  local copies, waits for them, and re-layouts: 4.43 us -> 1.52 us
  Pallas kernels: 22.9 us -> 23.8 us
  other arithmetic: 1.5 us -> 2.39 us
    gather x1 -> x0, local copies, waits for them, and re-layouts: 1.38 us -> none  [pick(): return x.at[index].get(mode='promise_in_bounds')]
    unnamed x9 -> x8, local copies, waits for them, and re-layouts: 0.88 us -> 0.03 us
    pallas_call x0 -> x1, Pallas kernels: none -> 0.85 us  [place_call(): call(functools.partial(place_kernel, parts=parts), 'place_weight_grad', 0...]
  transfers between devices with their start and end apart: 26 -> 26, of which waited for: 10 -> 13; matrix products, arithmetic and copies ran while one was open for 7% -> 7% of each run, Pallas kernels for 28% -> 29%
where the time goes in v5:
time: 80 us; the launch traced here: 79.7 us
  starting transfers between devices  27.6 us (34%)
  Pallas kernels  23.8 us (30%)
  waiting for transfers between devices  20 us (25%)
  matrix products  3.26 us (4%)
  other arithmetic  2.39 us (3%)
  local copies, waits for them, and re-layouts  1.52 us (2%)
  between operations  1.18 us (1%)
    ppermute x26, starting transfers between devices, swap(): return lax.ppermute(x, 'row', [(i, i ^ bit) for i in range(n)])  27.6 us
    ppermute x26, waiting for transfers between devices, swap(): return lax.ppermute(x, 'row', [(i, i ^ bit) for i in range(n)])  20 us
    pallas_call x2, Pallas kernels, c_call(): call(functools.partial(c_kernel, ib=ib, s=s, k=k, steps=r // ib, blocks=b...  11.8 us
    pallas_call x2, Pallas kernels, b_call(): call(functools.partial(b_kernel, ib=ib, offs=offs, rb=rb, s=s, part=part)...  7.71 us
    pallas_call x1, Pallas kernels, t_call(): call(functools.partial(t_kernel, ib=ib, s=s), 'left_by_weights', 4.0, 12,...  3.44 us
  transfers between devices with their start and end apart: 26, of which 13 were waited for; matrix products, arithmetic and copies ran while one was open for 7% of the time, Pallas kernels for 29%

profile of v5, /device:TPU:0, one launch (start us, length us, event | category | flops | bytes accessed | tf_op | source)
XLA Modules:
  0.0 79.7 jit_solution(13036520183614737225)
XLA Ops:
  0.7 0.9 %add_add_fusion = s32[32,32]{1,0:T(8,128)S(1)} fusion(s32[1,32]{1,0:T(1,128)} %bitcast.37, s32[16,32]{1,0:T(8,128)} %param.8, s32[32]{0:T(128)S(1)} %pad.26.clone), kind=kLoop, calls=%fused_computation.30 | loop fusion | flops 2048 | bytes 6400 | tf_op jit(solution)/shard_map/concatenate | solution.py:298
  2.1 0.7 convert_element_type.8
  2.8 1.3 %fusion = f32[16,32,64]{2,1,0:T(8,128)S(1)} fusion(f32[16,32,256]{2,1,0:T(8,128)S(1)} %copy-done, f32[16,32]{1,0:T(8,128)S(1)} %convert_element_type.8, f32[256,32]{0,1:T(8,128)} %param.11, f32[256,32]{0,1:T(8,128)} %param.10), kind=kOutput, calls=%fused_computation.1 | convolution fusion | flops 100712448 | bytes 722944 | tf_op jit(solution)/shard_map/sim,mc->sic/dot_general | solution.py:294
  4.3 2.5 %collective-permute-start.1 = (s32[64,32]{0,1:T(8,128)S(1)}, s32[64,32]{0,1:T(8,128)S(1)}, u32[]{:S(2)}, u32[]{:S(2)}) collective-permute-start(s32[64,32]{0,1:T(8,128)S(1)} %pad_add_fusion), channel_id=1, source_target_pairs={{0,2},{1,3},{2,0},{3,1},{4,6},{5,7},{6,4},{7,5},{8,10},{9,11},{10,... | collective-permute-start | bytes 24584 | tf_op jit(solution)/shard_map/ppermute | solution.py:262
  7.2 1.3 %collective-permute-done.1 = s32[64,32]{0,1:T(8,128)S(1)} collective-permute-done((s32[64,32]{0,1:T(8,128)S(1)}, s32[64,32]{0,1:T(8,128)S(1)}, u32[]{:S(2)}, u32[]{:S(2)}) %collective-permute-start.1) | collective-permute-done | bytes 8224 | tf_op jit(solution)/shard_map/ppermute | solution.py:262
  8.6 3.2 %collective-permute-start.2 = (f32[32,640]{1,0:T(8,128)S(1)}, f32[32,640]{1,0:T(8,128)S(1)}, u32[]{:S(2)}, u32[]{:S(2)}) collective-permute-start(f32[32,640]{1,0:T(8,128)S(1)} %pad_maximum_fusion.6), channel_id=1, source_target_pairs={{0,8},{1,9},{2,10},{3,11},{4,12},{5,13},{6,14},{7,15},{8,0},{9,1},... | collective-permute-start | bytes 245768 | tf_op jit(solution)/shard_map/ppermute | solution.py:262
  11.8 4.0 %collective-permute-done.2 = f32[32,640]{1,0:T(8,128)S(1)} collective-permute-done((f32[32,640]{1,0:T(8,128)S(1)}, f32[32,640]{1,0:T(8,128)S(1)}, u32[]{:S(2)}, u32[]{:S(2)}) %collective-permute-start.2) | collective-permute-done | bytes 81952 | tf_op jit(solution)/shard_map/ppermute | solution.py:262
  16.3 4.9 %collective-permute-done.3 = f32[64,640]{1,0:T(8,128)S(1)} collective-permute-done((f32[64,640]{1,0:T(8,128)S(1)}, f32[64,640]{1,0:T(8,128)S(1)}, u32[]{:S(2)}, u32[]{:S(2)}) %collective-permute-start.3) | collective-permute-done | bytes 163872 | tf_op jit(solution)/shard_map/ppermute | solution.py:262
  21.2 1.6 %collective-permute-start.4 = (f32[128,512]{1,0:T(8,128)S(1)}, f32[128,512]{1,0:T(8,128)S(1)}, u32[]{:S(2)}, u32[]{:S(2)}) collective-permute-start(f32[128,512]{1,0:T(8,128)S(1)} %pad_maximum_fusion.1), channel_id=1, source_target_pairs={{0,2},{1,3},{2,0},{3,1},{4,6},{5,7},{6,4},{7,5},{8,10},{9,11},{10,... | collective-permute-start | bytes 786440 | tf_op jit(solution)/shard_map/ppermute | solution.py:262
  22.8 3.4 %left_by_weights.1 = (bf16[512,4096]{1,0:T(8,128)(2,1)S(1)}, bf16[512,4096]{1,0:T(8,128)(2,1)S(1)}, f32[32,512,128]{2,1,0:T(8,128)S(1)}) custom-call(f32[512,32]{1,0:T(8,128)S(1)} %bitcast.31, f32[1024,128]{1,0:T(8,128)S(1)} %copy-done.1, f32[32,512,128]{2,1,0:T(8,128)} %d_ref.1), custom_call_target="tpu_custom_call" | custom-call | flops 4000000000 | tf_op jit(solution)/shard_map/left_by_weights/pallas_call | solution.py:79
  26.2 3.9 %right_grad_1.1 = (f32[256,512]{1,0:T(8,128)S(1)}, bf16[256,4096]{1,0:T(8,128)(2,1)S(1)}, bf16[256,4096]{1,0:T(8,128)(2,1)S(1)}) custom-call(s32[1]{0:T(128)} %bitcast.me_ref.refs_4_, f32[32,512,128]{2,1,0:T(8,128)S(1)} %get-tuple-element.32.dv, bf16[512,4096]{1,0:T(8,128)(2,1)S(1)} %get-tuple-element.33.thi_ref, ...), custom_call_target="tpu_custom_call" | custom-call | flops 3700000000 | tf_op jit(solution)/shard_map/right_grad_1/pallas_call | solution.py:133
  30.8 3.8 %right_grad_0.1 = (f32[256,512]{1,0:T(8,128)S(1)}, bf16[256,4096]{1,0:T(8,128)(2,1)S(1)}, bf16[256,4096]{1,0:T(8,128)(2,1)S(1)}) custom-call(s32[1]{0:T(128)} %bitcast.me_ref.refs_4_, f32[32,512,128]{2,1,0:T(8,128)S(1)} %get-tuple-element.32.dv, bf16[512,4096]{1,0:T(8,128)(2,1)S(1)} %get-tuple-element.33.thi_ref, ...), custom_call_target="tpu_custom_call" | custom-call | flops 3700000000 | tf_op jit(solution)/shard_map/right_grad_0/pallas_call | solution.py:133
  35.3 6.0 %left_and_weight_grad_0.1 = (f32[512,32]{1,0:T(8,128)S(1)}, f32[16,16,128]{2,1,0:T(8,128)S(1)}, f32[16,16,128]{2,1,0:T(8,128)S(1)}) custom-call(bf16[256,4096]{1,0:T(8,128)(2,1)S(1)} %get-tuple-element.38.refs_0_, bf16[256,4096]{1,0:T(8,128)(2,1)S(1)} %get-tuple-element.39.refs_1_, bf16[256,4096]{1,0:T(8,128)(2,1)S(1)} %get-tuple-element.40.refs_2_, ...), custom_call_target="tpu_custom_call" | custom-call | flops 5600000000 | tf_op jit(solution)/shard_map/left_and_weight_grad_0/pallas_call | solution.py:214
  41.4 1.6 %collective-permute-done.7 = f32[128,512]{1,0:T(8,128)S(1)} collective-permute-done((f32[128,512]{1,0:T(8,128)S(1)}, f32[128,512]{1,0:T(8,128)S(1)}, u32[]{:S(2)}, u32[]{:S(2)}) %collective-permute-start.7) | collective-permute-done | bytes 262176 | tf_op jit(solution)/shard_map/ppermute | solution.py:262
  43.6 0.7 collective-permute-start.19
  44.3 5.8 %left_and_weight_grad_1.1 = (f32[512,32]{1,0:T(8,128)S(1)}, f32[16,16,128]{2,1,0:T(8,128)S(1)}, f32[16,16,128]{2,1,0:T(8,128)S(1)}) custom-call(bf16[256,4096]{1,0:T(8,128)(2,1)S(1)} %get-tuple-element.38.refs_0_, bf16[256,4096]{1,0:T(8,128)(2,1)S(1)} %get-tuple-element.39.refs_1_, bf16[256,4096]{1,0:T(8,128)(2,1)S(1)} %get-tuple-element.40.refs_2_, ...), custom_call_target="tpu_custom_call" | custom-call | flops 5600000000 | tf_op jit(solution)/shard_map/left_and_weight_grad_1/pallas_call | solution.py:214
  50.2 3.3 %collective-permute-start.10 = (f32[32,512]{1,0:T(8,128)S(1)}, f32[32,512]{1,0:T(8,128)S(1)}, u32[]{:S(2)}, u32[]{:S(2)}) collective-permute-start(f32[32,512]{1,0:T(8,128)S(1)} %slice_add_fusion.6), channel_id=1, source_target_pairs={{0,8},{1,9},{2,10},{3,11},{4,12},{5,13},{6,14},{7,15},{8,0},{9,1},... | collective-permute-start | bytes 196616 | tf_op jit(solution)/shard_map/ppermute | solution.py:262
  53.6 0.6 collective-permute-start.20
  54.3 2.2 %collective-permute-done.10 = f32[32,512]{1,0:T(8,128)S(1)} collective-permute-done((f32[32,512]{1,0:T(8,128)S(1)}, f32[32,512]{1,0:T(8,128)S(1)}, u32[]{:S(2)}, u32[]{:S(2)}) %collective-permute-start.10) | collective-permute-done | bytes 65568 | tf_op jit(solution)/shard_map/ppermute | solution.py:262
  57.7 1.6 %collective-permute-start.12 = (f32[8,16,128]{2,1,0:T(8,128)S(1)}, f32[8,16,128]{2,1,0:T(8,128)S(1)}, u32[]{:S(2)}, u32[]{:S(2)}) collective-permute-start(f32[8,16,128]{2,1,0:T(8,128)S(1)} %slice_add_fusion.4), channel_id=1, source_target_pairs={{0,2},{1,3},{2,0},{3,1},{4,6},{5,7},{6,4},{7,5},{8,10},{9,11},{10,... | collective-permute-start | bytes 196616 | tf_op jit(solution)/shard_map/ppermute | solution.py:262
  59.3 3.0 %collective-permute-start.21 = (f32[8,16,128]{2,1,0:T(8,128)S(1)}, f32[8,16,128]{2,1,0:T(8,128)S(1)}, u32[]{:S(2)}, u32[]{:S(2)}) collective-permute-start(f32[8,16,128]{2,1,0:T(8,128)S(1)} %add.86), channel_id=1, source_target_pairs={{0,8},{1,9},{2,10},{3,11},{4,12},{5,13},{6,14},{7,15},{8,0},{9,1},... | collective-permute-start | bytes 196616 | tf_op jit(solution)/shard_map/ppermute | solution.py:262
  62.6 1.0 %collective-permute-start.13 = (f32[8,16,128]{2,1,0:T(8,128)S(1)}, f32[8,16,128]{2,1,0:T(8,128)S(1)}, u32[]{:S(2)}, u32[]{:S(2)}) collective-permute-start(f32[8,16,128]{2,1,0:T(8,128)S(1)} %fusion.1), channel_id=1, source_target_pairs={{0,4},{1,5},{2,6},{3,7},{4,0},{5,1},{6,2},{7,3},{8,12},{9,13},{10,... | collective-permute-start | bytes 196616 | tf_op jit(solution)/shard_map/ppermute | solution.py:262
  63.6 2.4 %collective-permute-done.21 = f32[8,16,128]{2,1,0:T(8,128)S(1)} collective-permute-done((f32[8,16,128]{2,1,0:T(8,128)S(1)}, f32[8,16,128]{2,1,0:T(8,128)S(1)}, u32[]{:S(2)}, u32[]{:S(2)}) %collective-permute-start.21) | collective-permute-done | bytes 65568 | tf_op jit(solution)/shard_map/ppermute | solution.py:262
  67.3 2.9 %collective-permute-start.14 = (f32[8,16,128]{2,1,0:T(8,128)S(1)}, f32[8,16,128]{2,1,0:T(8,128)S(1)}, u32[]{:S(2)}, u32[]{:S(2)}) collective-permute-start(f32[8,16,128]{2,1,0:T(8,128)S(1)} %add.79), channel_id=1, source_target_pairs={{0,8},{1,9},{2,10},{3,11},{4,12},{5,13},{6,14},{7,15},{8,0},{9,1},... | collective-permute-start | bytes 196616 | tf_op jit(solution)/shard_map/ppermute | solution.py:262
  70.4 1.0 %collective-permute-done.17 = f32[64,256]{1,0:T(8,128)S(1)} collective-permute-done((f32[64,256]{1,0:T(8,128)S(1)}, f32[64,256]{1,0:T(8,128)S(1)}, u32[]{:S(2)}, u32[]{:S(2)}) %collective-permute-start.17) | collective-permute-done | bytes 65568 | tf_op jit(solution)/shard_map/ppermute | solution.py:262
  71.4 1.5 %collective-permute-start.18 = (f32[64,256]{1,0:T(8,128)S(1)}, f32[64,256]{1,0:T(8,128)S(1)}, u32[]{:S(2)}, u32[]{:S(2)}) collective-permute-start(f32[64,256]{1,0:T(8,128)S(1)} %add.83), channel_id=1, source_target_pairs={{0,8},{1,9},{2,10},{3,11},{4,12},{5,13},{6,14},{7,15},{8,0},{9,1},... | collective-permute-start | bytes 196616 | tf_op jit(solution)/shard_map/ppermute | solution.py:262
  73.0 1.8 %collective-permute-start.24 = (f32[8,16,128]{2,1,0:T(8,128)S(1)}, f32[8,16,128]{2,1,0:T(8,128)S(1)}, u32[]{:S(2)}, u32[]{:S(2)}) collective-permute-start(f32[8,16,128]{2,1,0:T(8,128)S(1)} %add.80), channel_id=1, source_target_pairs={{0,2},{1,3},{2,0},{3,1},{4,6},{5,7},{6,4},{7,5},{8,10},{9,11},{10,... | collective-permute-start | bytes 196616 | tf_op jit(solution)/shard_map/ppermute | solution.py:262
  74.8 1.3 %fusion.3 = f32[16,32,256]{2,1,0:T(8,128)} fusion(f32[16,32,64]{2,1,0:T(8,128)S(1)} %pad_maximum_fusion.2, f32[256,32]{0,1:T(8,128)S(1)} %copy-done.2, f32[256,32]{0,1:T(8,128)S(1)} %copy-done.3), kind=kOutput, calls=%fused_computation.27 | convolution fusion | flops 100679680 | bytes 720896 | tf_op jit(solution)/shard_map/sic,mc->sim/dot_general | solution.py:367
  76.1 0.9 %collective-permute-done.18 = f32[64,256]{1,0:T(8,128)S(1)} collective-permute-done((f32[64,256]{1,0:T(8,128)S(1)}, f32[64,256]{1,0:T(8,128)S(1)}, u32[]{:S(2)}, u32[]{:S(2)}) %collective-permute-start.18) | collective-permute-done | bytes 65568 | tf_op jit(solution)/shard_map/ppermute | solution.py:262
  77.4 0.6 slice_bitcast_fusion.1
  78.0 0.7 collective-permute-done.25.refs_3_
  78.7 0.8 %place_weight_grad.1 = f32[32,32,128]{2,1,0:T(8,128)} custom-call(s32[1]{0:T(128)} %bitcast.me_ref.refs_4_, f32[16,16,128]{2,1,0:T(8,128)S(1)} %pad_maximum_fusion.4.refs_0_, f32[16,16,128]{2,1,0:T(8,128)S(1)} %collective-permute-done.23.refs_1_, f32[16,16,128]{2,1,0:T(8,128)S(1)} %pad_maximum_fusion.5.refs_2_, ...), custom_call_target="tpu_custom_call" | custom-call | flops 800000000 | tf_op jit(solution)/shard_map/place_weight_grad/pallas_call | solution.py:249
  (80 shorter events, 7.3 us)
Async XLA Ops:
  0.6 2.2 %copy-start = (f32[16,32,256]{2,1,0:T(8,128)S(1)}, f32[16,32,256]{2,1,0:T(8,128)}, u32[]{:S(2)}) copy-start(f32[16,32,256]{2,1,0:T(8,128)} %param.7) | copy-start | bytes 1572868
  0.6 22.1 %copy-start.1 = (f32[1024,128]{1,0:T(8,128)S(1)}, f32[1024,128]{1,0:T(8,128)}, u32[]{:S(2)}) copy-start(f32[1024,128]{1,0:T(8,128)} %refs_7_.3) | copy-start | bytes 1572868
  1.7 2.5 %collective-permute-start = (s32[32,32]{0,1:T(8,128)S(1)}, s32[32,32]{0,1:T(8,128)S(1)}, u32[]{:S(2)}, u32[]{:S(2)}) collective-permute-start(s32[32,32]{0,1:T(8,128)S(1)} %copy.20), channel_id=1, source_target_pairs={{0,1},{1,0},{2,3},{3,2},{4,5},{5,4},{6,7},{7,6},{8,9},{9,8},{10,11... | collective-permute-start | bytes 12296 | tf_op jit(solution)/shard_map/ppermute | solution.py:262
  4.3 4.2 %collective-permute-start.1 = (s32[64,32]{0,1:T(8,128)S(1)}, s32[64,32]{0,1:T(8,128)S(1)}, u32[]{:S(2)}, u32[]{:S(2)}) collective-permute-start(s32[64,32]{0,1:T(8,128)S(1)} %pad_add_fusion), channel_id=1, source_target_pairs={{0,2},{1,3},{2,0},{3,1},{4,6},{5,7},{6,4},{7,5},{8,10},{9,11},{10,... | collective-permute-start | bytes 24584 | tf_op jit(solution)/shard_map/ppermute | solution.py:262
  8.6 7.2 %collective-permute-start.2 = (f32[32,640]{1,0:T(8,128)S(1)}, f32[32,640]{1,0:T(8,128)S(1)}, u32[]{:S(2)}, u32[]{:S(2)}) collective-permute-start(f32[32,640]{1,0:T(8,128)S(1)} %pad_maximum_fusion.6), channel_id=1, source_target_pairs={{0,8},{1,9},{2,10},{3,11},{4,12},{5,13},{6,14},{7,15},{8,0},{9,1},... | collective-permute-start | bytes 245768 | tf_op jit(solution)/shard_map/ppermute | solution.py:262
  15.8 5.4 %collective-permute-start.3 = (f32[64,640]{1,0:T(8,128)S(1)}, f32[64,640]{1,0:T(8,128)S(1)}, u32[]{:S(2)}, u32[]{:S(2)}) collective-permute-start(f32[64,640]{1,0:T(8,128)S(1)} %pad_maximum_fusion.3), channel_id=1, source_target_pairs={{0,4},{1,5},{2,6},{3,7},{4,0},{5,1},{6,2},{7,3},{8,12},{9,13},{10,... | collective-permute-start | bytes 491528 | tf_op jit(solution)/shard_map/ppermute | solution.py:262
  21.2 9.0 %collective-permute-start.4 = (f32[128,512]{1,0:T(8,128)S(1)}, f32[128,512]{1,0:T(8,128)S(1)}, u32[]{:S(2)}, u32[]{:S(2)}) collective-permute-start(f32[128,512]{1,0:T(8,128)S(1)} %pad_maximum_fusion.1), channel_id=1, source_target_pairs={{0,2},{1,3},{2,0},{3,1},{4,6},{5,7},{6,4},{7,5},{8,10},{9,11},{10,... | collective-permute-start | bytes 786440 | tf_op jit(solution)/shard_map/ppermute | solution.py:262
  30.1 4.5 %collective-permute-start.5 = (f32[256,512]{1,0:T(8,128)S(1)}, f32[256,512]{1,0:T(8,128)S(1)}, u32[]{:S(2)}, u32[]{:S(2)}) collective-permute-start(f32[256,512]{1,0:T(8,128)S(1)} %get-tuple-element.35), channel_id=1, source_target_pairs={{0,1},{1,0},{2,3},{3,2},{4,5},{5,4},{6,7},{7,6},{8,9},{9,8},{10,11... | collective-permute-start | bytes 1572872 | tf_op jit(solution)/shard_map/ppermute | solution.py:262
  30.2 5.1 %collective-permute-start.6 = (f32[256,512]{1,0:T(8,128)S(1)}, f32[256,512]{1,0:T(8,128)S(1)}, u32[]{:S(2)}, u32[]{:S(2)}) collective-permute-start(f32[256,512]{1,0:T(8,128)S(1)} %pad_maximum_fusion.refs_5_), channel_id=1, source_target_pairs={{0,1},{1,0},{2,3},{3,2},{4,5},{5,4},{6,7},{7,6},{8,9},{9,8},{10,11... | collective-permute-start | bytes 1572872 | tf_op jit(solution)/shard_map/ppermute | solution.py:262
  34.7 8.3 %collective-permute-start.7 = (f32[128,512]{1,0:T(8,128)S(1)}, f32[128,512]{1,0:T(8,128)S(1)}, u32[]{:S(2)}, u32[]{:S(2)}) collective-permute-start(f32[128,512]{1,0:T(8,128)S(1)} %get-tuple-element.58), channel_id=1, source_target_pairs={{0,2},{1,3},{2,0},{3,1},{4,6},{5,7},{6,4},{7,5},{8,10},{9,11},{10,... | collective-permute-start | bytes 786440 | tf_op jit(solution)/shard_map/ppermute | solution.py:262
  41.3 2.2 %collective-permute-start.8 = (f32[16,16,128]{2,1,0:T(8,128)S(1)}, f32[16,16,128]{2,1,0:T(8,128)S(1)}, u32[]{:S(2)}, u32[]{:S(2)}) collective-permute-start(f32[16,16,128]{2,1,0:T(8,128)S(1)} %get-tuple-element.49), channel_id=1, source_target_pairs={{0,1},{1,0},{2,3},{3,2},{4,5},{5,4},{6,7},{7,6},{8,9},{9,8},{10,11... | collective-permute-start | bytes 393224 | tf_op jit(solution)/shard_map/ppermute | solution.py:262
  43.1 7.1 %collective-permute-start.9 = (f32[64,512]{1,0:T(8,128)S(1)}, f32[64,512]{1,0:T(8,128)S(1)}, u32[]{:S(2)}, u32[]{:S(2)}) collective-permute-start(f32[64,512]{1,0:T(8,128)S(1)} %get-tuple-element.60), channel_id=1, source_target_pairs={{0,4},{1,5},{2,6},{3,7},{4,0},{5,1},{6,2},{7,3},{8,12},{9,13},{10,... | collective-permute-start | bytes 393224 | tf_op jit(solution)/shard_map/ppermute | solution.py:262
  43.6 10.0 %collective-permute-start.19 = (f32[8,16,128]{2,1,0:T(8,128)S(1)}, f32[8,16,128]{2,1,0:T(8,128)S(1)}, u32[]{:S(2)}, u32[]{:S(2)}) collective-permute-start(f32[8,16,128]{2,1,0:T(8,128)S(1)} %get-tuple-element.62), channel_id=1, source_target_pairs={{0,2},{1,3},{2,0},{3,1},{4,6},{5,7},{6,4},{7,5},{8,10},{9,11},{10,... | collective-permute-start | bytes 196616 | tf_op jit(solution)/shard_map/ppermute | solution.py:262
  50.1 24.6 %copy-start.2 = (f32[256,32]{0,1:T(8,128)S(1)}, f32[256,32]{0,1:T(8,128)}, u32[]{:S(2)}) copy-start(f32[256,32]{0,1:T(8,128)} %param.11) | copy-start | bytes 98308
  50.1 24.6 %copy-start.3 = (f32[256,32]{0,1:T(8,128)S(1)}, f32[256,32]{0,1:T(8,128)}, u32[]{:S(2)}) copy-start(f32[256,32]{0,1:T(8,128)} %param.10) | copy-start | bytes 98308
  50.2 6.3 %collective-permute-start.10 = (f32[32,512]{1,0:T(8,128)S(1)}, f32[32,512]{1,0:T(8,128)S(1)}, u32[]{:S(2)}, u32[]{:S(2)}) collective-permute-start(f32[32,512]{1,0:T(8,128)S(1)} %slice_add_fusion.6), channel_id=1, source_target_pairs={{0,8},{1,9},{2,10},{3,11},{4,12},{5,13},{6,14},{7,15},{8,0},{9,1},... | collective-permute-start | bytes 196616 | tf_op jit(solution)/shard_map/ppermute | solution.py:262
  53.5 4.2 %collective-permute-start.11 = (f32[16,16,128]{2,1,0:T(8,128)S(1)}, f32[16,16,128]{2,1,0:T(8,128)S(1)}, u32[]{:S(2)}, u32[]{:S(2)}) collective-permute-start(f32[16,16,128]{2,1,0:T(8,128)S(1)} %get-tuple-element.55), channel_id=1, source_target_pairs={{0,1},{1,0},{2,3},{3,2},{4,5},{5,4},{6,7},{7,6},{8,9},{9,8},{10,11... | collective-permute-start | bytes 393224 | tf_op jit(solution)/shard_map/ppermute | solution.py:262
  53.6 5.7 %collective-permute-start.20 = (f32[8,16,128]{2,1,0:T(8,128)S(1)}, f32[8,16,128]{2,1,0:T(8,128)S(1)}, u32[]{:S(2)}, u32[]{:S(2)}) collective-permute-start(f32[8,16,128]{2,1,0:T(8,128)S(1)} %add.85), channel_id=1, source_target_pairs={{0,4},{1,5},{2,6},{3,7},{4,0},{5,1},{6,2},{7,3},{8,12},{9,13},{10,... | collective-permute-start | bytes 196616 | tf_op jit(solution)/shard_map/ppermute | solution.py:262
  57.6 4.7 %collective-permute-start.15 = (f32[64,256]{1,0:T(8,128)S(1)}, f32[64,256]{1,0:T(8,128)S(1)}, u32[]{:S(2)}, u32[]{:S(2)}) collective-permute-start(f32[64,256]{1,0:T(8,128)S(1)} %convolution_bitcast_fusion), channel_id=1, source_target_pairs={{0,1},{1,0},{2,3},{3,2},{4,5},{5,4},{6,7},{7,6},{8,9},{9,8},{10,11... | collective-permute-start | bytes 196616 | tf_op jit(solution)/shard_map/ppermute | solution.py:262
  57.7 4.9 %collective-permute-start.12 = (f32[8,16,128]{2,1,0:T(8,128)S(1)}, f32[8,16,128]{2,1,0:T(8,128)S(1)}, u32[]{:S(2)}, u32[]{:S(2)}) collective-permute-start(f32[8,16,128]{2,1,0:T(8,128)S(1)} %slice_add_fusion.4), channel_id=1, source_target_pairs={{0,2},{1,3},{2,0},{3,1},{4,6},{5,7},{6,4},{7,5},{8,10},{9,11},{10,... | collective-permute-start | bytes 196616 | tf_op jit(solution)/shard_map/ppermute | solution.py:262
  59.3 6.7 %collective-permute-start.21 = (f32[8,16,128]{2,1,0:T(8,128)S(1)}, f32[8,16,128]{2,1,0:T(8,128)S(1)}, u32[]{:S(2)}, u32[]{:S(2)}) collective-permute-start(f32[8,16,128]{2,1,0:T(8,128)S(1)} %add.86), channel_id=1, source_target_pairs={{0,8},{1,9},{2,10},{3,11},{4,12},{5,13},{6,14},{7,15},{8,0},{9,1},... | collective-permute-start | bytes 196616 | tf_op jit(solution)/shard_map/ppermute | solution.py:262
  62.3 4.3 %collective-permute-start.16 = (f32[64,256]{1,0:T(8,128)S(1)}, f32[64,256]{1,0:T(8,128)S(1)}, u32[]{:S(2)}, u32[]{:S(2)}) collective-permute-start(f32[64,256]{1,0:T(8,128)S(1)} %add.81), channel_id=1, source_target_pairs={{0,2},{1,3},{2,0},{3,1},{4,6},{5,7},{6,4},{7,5},{8,10},{9,11},{10,... | collective-permute-start | bytes 196616 | tf_op jit(solution)/shard_map/ppermute | solution.py:262
  62.6 4.7 %collective-permute-start.13 = (f32[8,16,128]{2,1,0:T(8,128)S(1)}, f32[8,16,128]{2,1,0:T(8,128)S(1)}, u32[]{:S(2)}, u32[]{:S(2)}) collective-permute-start(f32[8,16,128]{2,1,0:T(8,128)S(1)} %fusion.1), channel_id=1, source_target_pairs={{0,4},{1,5},{2,6},{3,7},{4,0},{5,1},{6,2},{7,3},{8,12},{9,13},{10,... | collective-permute-start | bytes 196616 | tf_op jit(solution)/shard_map/ppermute | solution.py:262
  66.0 4.3 %collective-permute-start.22 = (f32[8,16,128]{2,1,0:T(8,128)S(1)}, f32[8,16,128]{2,1,0:T(8,128)S(1)}, u32[]{:S(2)}, u32[]{:S(2)}) collective-permute-start(f32[8,16,128]{2,1,0:T(8,128)S(1)} %add.87), channel_id=1, source_target_pairs={{0,2},{1,3},{2,0},{3,1},{4,6},{5,7},{6,4},{7,5},{8,10},{9,11},{10,... | collective-permute-start | bytes 196616 | tf_op jit(solution)/shard_map/ppermute | solution.py:262
  66.7 4.8 %collective-permute-start.17 = (f32[64,256]{1,0:T(8,128)S(1)}, f32[64,256]{1,0:T(8,128)S(1)}, u32[]{:S(2)}, u32[]{:S(2)}) collective-permute-start(f32[64,256]{1,0:T(8,128)S(1)} %add.82), channel_id=1, source_target_pairs={{0,4},{1,5},{2,6},{3,7},{4,0},{5,1},{6,2},{7,3},{8,12},{9,13},{10,... | collective-permute-start | bytes 196616 | tf_op jit(solution)/shard_map/ppermute | solution.py:262
  67.3 5.6 %collective-permute-start.14 = (f32[8,16,128]{2,1,0:T(8,128)S(1)}, f32[8,16,128]{2,1,0:T(8,128)S(1)}, u32[]{:S(2)}, u32[]{:S(2)}) collective-permute-start(f32[8,16,128]{2,1,0:T(8,128)S(1)} %add.79), channel_id=1, source_target_pairs={{0,8},{1,9},{2,10},{3,11},{4,12},{5,13},{6,14},{7,15},{8,0},{9,1},... | collective-permute-start | bytes 196616 | tf_op jit(solution)/shard_map/ppermute | solution.py:262
  70.3 7.7 %collective-permute-start.23 = (f32[16,16,128]{2,1,0:T(8,128)S(1)}, f32[16,16,128]{2,1,0:T(8,128)S(1)}, u32[]{:S(2)}, u32[]{:S(2)}) collective-permute-start(f32[16,16,128]{2,1,0:T(8,128)S(1)} %pad_maximum_fusion.4.refs_0_), channel_id=1, source_target_pairs={{0,1},{1,0},{2,3},{3,2},{4,5},{5,4},{6,7},{7,6},{8,9},{9,8},{10,11... | collective-permute-start | bytes 393224 | tf_op jit(solution)/shard_map/ppermute | solution.py:262
  71.4 5.6 %collective-permute-start.18 = (f32[64,256]{1,0:T(8,128)S(1)}, f32[64,256]{1,0:T(8,128)S(1)}, u32[]{:S(2)}, u32[]{:S(2)}) collective-permute-start(f32[64,256]{1,0:T(8,128)S(1)} %add.83), channel_id=1, source_target_pairs={{0,8},{1,9},{2,10},{3,11},{4,12},{5,13},{6,14},{7,15},{8,0},{9,1},... | collective-permute-start | bytes 196616 | tf_op jit(solution)/shard_map/ppermute | solution.py:262
  73.0 4.3 %collective-permute-start.24 = (f32[8,16,128]{2,1,0:T(8,128)S(1)}, f32[8,16,128]{2,1,0:T(8,128)S(1)}, u32[]{:S(2)}, u32[]{:S(2)}) collective-permute-start(f32[8,16,128]{2,1,0:T(8,128)S(1)} %add.80), channel_id=1, source_target_pairs={{0,2},{1,3},{2,0},{3,1},{4,6},{5,7},{6,4},{7,5},{8,10},{9,11},{10,... | collective-permute-start | bytes 196616 | tf_op jit(solution)/shard_map/ppermute | solution.py:262
  77.3 1.4 %collective-permute-start.25 = (f32[16,16,128]{2,1,0:T(8,128)S(1)}, f32[16,16,128]{2,1,0:T(8,128)S(1)}, u32[]{:S(2)}, u32[]{:S(2)}) collective-permute-start(f32[16,16,128]{2,1,0:T(8,128)S(1)} %pad_maximum_fusion.5.refs_2_), channel_id=1, source_target_pairs={{0,1},{1,0},{2,3},{3,2},{4,5},{5,4},{6,7},{7,6},{8,9},{9,8},{10,11... | collective-permute-start | bytes 393224 | tf_op jit(solution)/shard_map/ppermute | solution.py:262

commit v6 on v5

--- a/solution.py
+++ b/solution.py
@@ -340,7 +340,7 @@
     ow_b, send_b = halves(ow_b, swap(send_b, 1, n), quarter)
     for bit in later[1:]:
         rows = rows // 2
-        other = after(swap(send, bit, n), left_b)
+        other = after(swap(send, bit, n), left_b, send_b) if bit == later[-1] else after(swap(send, bit, n), left_b)
         if bit == later[-1]:
             grad = grad + other
         else:
@@ -365,7 +365,7 @@
     ow_b = finish(ow_b)
     grads = after(grads, ow_b)
     alignment = jnp.einsum("sic,mc->sim", grads, jnp.concatenate([w1, w2], axis=1), precision=EXACT)
-    for bit in reversed(bits):
+    for bit in (*reversed(bits[:-1]), 1):
         small = small + swap(small, bit, n)
 
     out_grad = place_call(here, ow_a + spread(ow_b)).reshape(w * w, k)

time: 80 us -> 80.4 us (level)
  waiting for transfers between devices: 20 us -> 22.8 us
  starting transfers between devices: 27.6 us -> 25.2 us
    ppermute x26, waiting for transfers between devices: 20 us -> 22.8 us  [swap(): return lax.ppermute(x, 'row', [(i, i ^ bit) for i in range(n)])]
    ppermute x26, starting transfers between devices: 27.6 us -> 25.2 us  [swap(): return lax.ppermute(x, 'row', [(i, i ^ bit) for i in range(n)])]
  transfers between devices with their start and end apart: 26 -> 26, of which waited for: 13 -> 12; matrix products, arithmetic and copies ran while one was open for 7% -> 7% of each run, Pallas kernels for 29% -> 29%
where the time goes in v6:
time: 80.4 us; the launch traced here: 80.1 us
  starting transfers between devices  25.2 us (31%)
  Pallas kernels  23.8 us (30%)
  waiting for transfers between devices  22.8 us (28%)
  matrix products  3.26 us (4%)
  other arithmetic  2.4 us (3%)
  local copies, waits for them, and re-layouts  1.52 us (2%)
  between operations  1.18 us (1%)
    ppermute x26, starting transfers between devices, swap(): return lax.ppermute(x, 'row', [(i, i ^ bit) for i in range(n)])  25.2 us
    ppermute x26, waiting for transfers between devices, swap(): return lax.ppermute(x, 'row', [(i, i ^ bit) for i in range(n)])  22.8 us
    pallas_call x2, Pallas kernels, c_call(): call(functools.partial(c_kernel, ib=ib, s=s, k=k, steps=r // ib, blocks=b...  11.8 us
    pallas_call x2, Pallas kernels, b_call(): call(functools.partial(b_kernel, ib=ib, offs=offs, rb=rb, s=s, part=part)...  7.71 us
    pallas_call x1, Pallas kernels, t_call(): call(functools.partial(t_kernel, ib=ib, s=s), 'left_by_weights', 4.0, 12,...  3.44 us
  transfers between devices with their start and end apart: 26, of which 12 were waited for; matrix products, arithmetic and copies ran while one was open for 7% of the time, Pallas kernels for 29%

profile of v6, /device:TPU:0, one launch (start us, length us, event | category | flops | bytes accessed | tf_op | source)
XLA Modules:
  0.0 80.1 jit_solution(18391536837490691834)
XLA Ops:
  0.7 0.9 %add_add_fusion = s32[32,32]{1,0:T(8,128)S(1)} fusion(s32[1,32]{1,0:T(1,128)} %bitcast.37, s32[16,32]{1,0:T(8,128)} %param.8, s32[32]{0:T(128)S(1)} %pad.26.clone), kind=kLoop, calls=%fused_computation.30 | loop fusion | flops 2048 | bytes 6400 | tf_op jit(solution)/shard_map/concatenate | solution.py:298
  2.1 0.7 convert_element_type.8
  2.8 1.3 %fusion = f32[16,32,64]{2,1,0:T(8,128)S(1)} fusion(f32[16,32,256]{2,1,0:T(8,128)S(1)} %copy-done, f32[16,32]{1,0:T(8,128)S(1)} %convert_element_type.8, f32[256,32]{0,1:T(8,128)} %param.11, f32[256,32]{0,1:T(8,128)} %param.10), kind=kOutput, calls=%fused_computation.1 | convolution fusion | flops 100712448 | bytes 722944 | tf_op jit(solution)/shard_map/sim,mc->sic/dot_general | solution.py:294
  4.3 2.5 %collective-permute-start.1 = (s32[64,32]{0,1:T(8,128)S(1)}, s32[64,32]{0,1:T(8,128)S(1)}, u32[]{:S(2)}, u32[]{:S(2)}) collective-permute-start(s32[64,32]{0,1:T(8,128)S(1)} %pad_add_fusion), channel_id=1, source_target_pairs={{0,2},{1,3},{2,0},{3,1},{4,6},{5,7},{6,4},{7,5},{8,10},{9,11},{10,... | collective-permute-start | bytes 24584 | tf_op jit(solution)/shard_map/ppermute | solution.py:262
  7.2 1.3 %collective-permute-done.1 = s32[64,32]{0,1:T(8,128)S(1)} collective-permute-done((s32[64,32]{0,1:T(8,128)S(1)}, s32[64,32]{0,1:T(8,128)S(1)}, u32[]{:S(2)}, u32[]{:S(2)}) %collective-permute-start.1) | collective-permute-done | bytes 8224 | tf_op jit(solution)/shard_map/ppermute | solution.py:262
  8.6 3.2 %collective-permute-start.2 = (f32[32,640]{1,0:T(8,128)S(1)}, f32[32,640]{1,0:T(8,128)S(1)}, u32[]{:S(2)}, u32[]{:S(2)}) collective-permute-start(f32[32,640]{1,0:T(8,128)S(1)} %pad_maximum_fusion.6), channel_id=1, source_target_pairs={{0,8},{1,9},{2,10},{3,11},{4,12},{5,13},{6,14},{7,15},{8,0},{9,1},... | collective-permute-start | bytes 245768 | tf_op jit(solution)/shard_map/ppermute | solution.py:262
  11.8 4.0 %collective-permute-done.2 = f32[32,640]{1,0:T(8,128)S(1)} collective-permute-done((f32[32,640]{1,0:T(8,128)S(1)}, f32[32,640]{1,0:T(8,128)S(1)}, u32[]{:S(2)}, u32[]{:S(2)}) %collective-permute-start.2) | collective-permute-done | bytes 81952 | tf_op jit(solution)/shard_map/ppermute | solution.py:262
  16.3 4.9 %collective-permute-done.3 = f32[64,640]{1,0:T(8,128)S(1)} collective-permute-done((f32[64,640]{1,0:T(8,128)S(1)}, f32[64,640]{1,0:T(8,128)S(1)}, u32[]{:S(2)}, u32[]{:S(2)}) %collective-permute-start.3) | collective-permute-done | bytes 163872 | tf_op jit(solution)/shard_map/ppermute | solution.py:262
  21.2 1.6 %collective-permute-start.4 = (f32[128,512]{1,0:T(8,128)S(1)}, f32[128,512]{1,0:T(8,128)S(1)}, u32[]{:S(2)}, u32[]{:S(2)}) collective-permute-start(f32[128,512]{1,0:T(8,128)S(1)} %pad_maximum_fusion.1), channel_id=1, source_target_pairs={{0,2},{1,3},{2,0},{3,1},{4,6},{5,7},{6,4},{7,5},{8,10},{9,11},{10,... | collective-permute-start | bytes 786440 | tf_op jit(solution)/shard_map/ppermute | solution.py:262
  22.8 3.4 %left_by_weights.1 = (bf16[512,4096]{1,0:T(8,128)(2,1)S(1)}, bf16[512,4096]{1,0:T(8,128)(2,1)S(1)}, f32[32,512,128]{2,1,0:T(8,128)S(1)}) custom-call(f32[512,32]{1,0:T(8,128)S(1)} %bitcast.31, f32[1024,128]{1,0:T(8,128)S(1)} %copy-done.1, f32[32,512,128]{2,1,0:T(8,128)} %d_ref.1), custom_call_target="tpu_custom_call" | custom-call | flops 4000000000 | tf_op jit(solution)/shard_map/left_by_weights/pallas_call | solution.py:79
  26.2 3.9 %right_grad_1.1 = (f32[256,512]{1,0:T(8,128)S(1)}, bf16[256,4096]{1,0:T(8,128)(2,1)S(1)}, bf16[256,4096]{1,0:T(8,128)(2,1)S(1)}) custom-call(s32[1]{0:T(128)} %bitcast.me_ref.refs_4_, f32[32,512,128]{2,1,0:T(8,128)S(1)} %get-tuple-element.32.dv, bf16[512,4096]{1,0:T(8,128)(2,1)S(1)} %get-tuple-element.33.thi_ref, ...), custom_call_target="tpu_custom_call" | custom-call | flops 3700000000 | tf_op jit(solution)/shard_map/right_grad_1/pallas_call | solution.py:133
  30.8 3.8 %right_grad_0.1 = (f32[256,512]{1,0:T(8,128)S(1)}, bf16[256,4096]{1,0:T(8,128)(2,1)S(1)}, bf16[256,4096]{1,0:T(8,128)(2,1)S(1)}) custom-call(s32[1]{0:T(128)} %bitcast.me_ref.refs_4_, f32[32,512,128]{2,1,0:T(8,128)S(1)} %get-tuple-element.32.dv, bf16[512,4096]{1,0:T(8,128)(2,1)S(1)} %get-tuple-element.33.thi_ref, ...), custom_call_target="tpu_custom_call" | custom-call | flops 3700000000 | tf_op jit(solution)/shard_map/right_grad_0/pallas_call | solution.py:133
  35.3 6.0 %left_and_weight_grad_0.1 = (f32[512,32]{1,0:T(8,128)S(1)}, f32[16,16,128]{2,1,0:T(8,128)S(1)}, f32[16,16,128]{2,1,0:T(8,128)S(1)}) custom-call(bf16[256,4096]{1,0:T(8,128)(2,1)S(1)} %get-tuple-element.38.refs_0_, bf16[256,4096]{1,0:T(8,128)(2,1)S(1)} %get-tuple-element.39.refs_1_, bf16[256,4096]{1,0:T(8,128)(2,1)S(1)} %get-tuple-element.40.refs_2_, ...), custom_call_target="tpu_custom_call" | custom-call | flops 5600000000 | tf_op jit(solution)/shard_map/left_and_weight_grad_0/pallas_call | solution.py:214
  41.4 1.6 %collective-permute-done.7 = f32[128,512]{1,0:T(8,128)S(1)} collective-permute-done((f32[128,512]{1,0:T(8,128)S(1)}, f32[128,512]{1,0:T(8,128)S(1)}, u32[]{:S(2)}, u32[]{:S(2)}) %collective-permute-start.7) | collective-permute-done | bytes 262176 | tf_op jit(solution)/shard_map/ppermute | solution.py:262
  43.6 0.7 collective-permute-start.19
  44.3 5.8 %left_and_weight_grad_1.1 = (f32[512,32]{1,0:T(8,128)S(1)}, f32[16,16,128]{2,1,0:T(8,128)S(1)}, f32[16,16,128]{2,1,0:T(8,128)S(1)}) custom-call(bf16[256,4096]{1,0:T(8,128)(2,1)S(1)} %get-tuple-element.38.refs_0_, bf16[256,4096]{1,0:T(8,128)(2,1)S(1)} %get-tuple-element.39.refs_1_, bf16[256,4096]{1,0:T(8,128)(2,1)S(1)} %get-tuple-element.40.refs_2_, ...), custom_call_target="tpu_custom_call" | custom-call | flops 5600000000 | tf_op jit(solution)/shard_map/left_and_weight_grad_1/pallas_call | solution.py:214
  50.3 3.3 %collective-permute-start.10 = (f32[32,512]{1,0:T(8,128)S(1)}, f32[32,512]{1,0:T(8,128)S(1)}, u32[]{:S(2)}, u32[]{:S(2)}) collective-permute-start(f32[32,512]{1,0:T(8,128)S(1)} %slice_add_fusion.6), channel_id=1, source_target_pairs={{0,8},{1,9},{2,10},{3,11},{4,12},{5,13},{6,14},{7,15},{8,0},{9,1},... | collective-permute-start | bytes 196616 | tf_op jit(solution)/shard_map/ppermute | solution.py:262
  54.3 1.0 %collective-permute-start.12 = (f32[8,16,128]{2,1,0:T(8,128)S(1)}, f32[8,16,128]{2,1,0:T(8,128)S(1)}, u32[]{:S(2)}, u32[]{:S(2)}) collective-permute-start(f32[8,16,128]{2,1,0:T(8,128)S(1)} %slice_add_fusion.5), channel_id=1, source_target_pairs={{0,2},{1,3},{2,0},{3,1},{4,6},{5,7},{6,4},{7,5},{8,10},{9,11},{10,... | collective-permute-start | bytes 196616 | tf_op jit(solution)/shard_map/ppermute | solution.py:262
  55.3 2.6 %collective-permute-done.10 = f32[32,512]{1,0:T(8,128)S(1)} collective-permute-done((f32[32,512]{1,0:T(8,128)S(1)}, f32[32,512]{1,0:T(8,128)S(1)}, u32[]{:S(2)}, u32[]{:S(2)}) %collective-permute-start.10) | collective-permute-done | bytes 65568 | tf_op jit(solution)/shard_map/ppermute | solution.py:262
  59.1 1.6 %collective-permute-start.15 = (f32[64,256]{1,0:T(8,128)S(1)}, f32[64,256]{1,0:T(8,128)S(1)}, u32[]{:S(2)}, u32[]{:S(2)}) collective-permute-start(f32[64,256]{1,0:T(8,128)S(1)} %convolution_bitcast_fusion), channel_id=1, source_target_pairs={{0,2},{1,3},{2,0},{3,1},{4,6},{5,7},{6,4},{7,5},{8,10},{9,11},{10,... | collective-permute-start | bytes 196616 | tf_op jit(solution)/shard_map/ppermute | solution.py:262
  60.6 1.6 %collective-permute-start.21 = (f32[8,16,128]{2,1,0:T(8,128)S(1)}, f32[8,16,128]{2,1,0:T(8,128)S(1)}, u32[]{:S(2)}, u32[]{:S(2)}) collective-permute-start(f32[8,16,128]{2,1,0:T(8,128)S(1)} %add.86), channel_id=1, source_target_pairs={{0,8},{1,9},{2,10},{3,11},{4,12},{5,13},{6,14},{7,15},{8,0},{9,1},... | collective-permute-start | bytes 196616 | tf_op jit(solution)/shard_map/ppermute | solution.py:262
  62.4 1.0 %collective-permute-done.15 = f32[64,256]{1,0:T(8,128)S(1)} collective-permute-done((f32[64,256]{1,0:T(8,128)S(1)}, f32[64,256]{1,0:T(8,128)S(1)}, u32[]{:S(2)}, u32[]{:S(2)}) %collective-permute-start.15) | collective-permute-done | bytes 65568 | tf_op jit(solution)/shard_map/ppermute | solution.py:262
  63.4 1.0 %collective-permute-start.16 = (f32[64,256]{1,0:T(8,128)S(1)}, f32[64,256]{1,0:T(8,128)S(1)}, u32[]{:S(2)}, u32[]{:S(2)}) collective-permute-start(f32[64,256]{1,0:T(8,128)S(1)} %add.81), channel_id=1, source_target_pairs={{0,4},{1,5},{2,6},{3,7},{4,0},{5,1},{6,2},{7,3},{8,12},{9,13},{10,... | collective-permute-start | bytes 196616 | tf_op jit(solution)/shard_map/ppermute | solution.py:262
  64.4 1.6 %collective-permute-done.21 = f32[8,16,128]{2,1,0:T(8,128)S(1)} collective-permute-done((f32[8,16,128]{2,1,0:T(8,128)S(1)}, f32[8,16,128]{2,1,0:T(8,128)S(1)}, u32[]{:S(2)}, u32[]{:S(2)}) %collective-permute-start.21) | collective-permute-done | bytes 65568 | tf_op jit(solution)/shard_map/ppermute | solution.py:262
  66.0 1.0 %collective-permute-start.22 = (f32[8,16,128]{2,1,0:T(8,128)S(1)}, f32[8,16,128]{2,1,0:T(8,128)S(1)}, u32[]{:S(2)}, u32[]{:S(2)}) collective-permute-start(f32[8,16,128]{2,1,0:T(8,128)S(1)} %add.87), channel_id=1, source_target_pairs={{0,2},{1,3},{2,0},{3,1},{4,6},{5,7},{6,4},{7,5},{8,10},{9,11},{10,... | collective-permute-start | bytes 196616 | tf_op jit(solution)/shard_map/ppermute | solution.py:262
  67.2 1.6 %collective-permute-start.14 = (f32[8,16,128]{2,1,0:T(8,128)S(1)}, f32[8,16,128]{2,1,0:T(8,128)S(1)}, u32[]{:S(2)}, u32[]{:S(2)}) collective-permute-start(f32[8,16,128]{2,1,0:T(8,128)S(1)} %add.79), channel_id=1, source_target_pairs={{0,8},{1,9},{2,10},{3,11},{4,12},{5,13},{6,14},{7,15},{8,0},{9,1},... | collective-permute-start | bytes 196616 | tf_op jit(solution)/shard_map/ppermute | solution.py:262
  68.8 1.5 %collective-permute-start.17 = (f32[64,256]{1,0:T(8,128)S(1)}, f32[64,256]{1,0:T(8,128)S(1)}, u32[]{:S(2)}, u32[]{:S(2)}) collective-permute-start(f32[64,256]{1,0:T(8,128)S(1)} %add.82), channel_id=1, source_target_pairs={{0,8},{1,9},{2,10},{3,11},{4,12},{5,13},{6,14},{7,15},{8,0},{9,1},... | collective-permute-start | bytes 196616 | tf_op jit(solution)/shard_map/ppermute | solution.py:262
  70.5 2.9 %collective-permute-done.14 = f32[8,16,128]{2,1,0:T(8,128)S(1)} collective-permute-done((f32[8,16,128]{2,1,0:T(8,128)S(1)}, f32[8,16,128]{2,1,0:T(8,128)S(1)}, u32[]{:S(2)}, u32[]{:S(2)}) %collective-permute-start.14) | collective-permute-done | bytes 65568 | tf_op jit(solution)/shard_map/ppermute | solution.py:262
  73.3 0.8 %collective-permute-start.24 = (f32[8,16,128]{2,1,0:T(8,128)S(1)}, f32[8,16,128]{2,1,0:T(8,128)S(1)}, u32[]{:S(2)}, u32[]{:S(2)}) collective-permute-start(f32[8,16,128]{2,1,0:T(8,128)S(1)} %add.80), channel_id=1, source_target_pairs={{0,2},{1,3},{2,0},{3,1},{4,6},{5,7},{6,4},{7,5},{8,10},{9,11},{10,... | collective-permute-start | bytes 196616 | tf_op jit(solution)/shard_map/ppermute | solution.py:262
  74.3 1.3 %fusion.3 = f32[16,32,256]{2,1,0:T(8,128)} fusion(f32[16,32,64]{2,1,0:T(8,128)S(1)} %pad_maximum_fusion.2, f32[256,32]{0,1:T(8,128)S(1)} %copy-done.2, f32[256,32]{0,1:T(8,128)S(1)} %copy-done.3), kind=kOutput, calls=%fused_computation.27 | convolution fusion | flops 100679680 | bytes 720896 | tf_op jit(solution)/shard_map/sic,mc->sim/dot_general | solution.py:367
  75.6 2.1 %collective-permute-done.24 = f32[8,16,128]{2,1,0:T(8,128)S(1)} collective-permute-done((f32[8,16,128]{2,1,0:T(8,128)S(1)}, f32[8,16,128]{2,1,0:T(8,128)S(1)}, u32[]{:S(2)}, u32[]{:S(2)}) %collective-permute-start.24) | collective-permute-done | bytes 65568 | tf_op jit(solution)/shard_map/ppermute | solution.py:262
  79.1 0.8 %place_weight_grad.1 = f32[32,32,128]{2,1,0:T(8,128)} custom-call(s32[1]{0:T(128)} %bitcast.me_ref.refs_4_, f32[16,16,128]{2,1,0:T(8,128)S(1)} %pad_maximum_fusion.4.refs_0_, f32[16,16,128]{2,1,0:T(8,128)S(1)} %collective-permute-done.23.refs_1_, f32[16,16,128]{2,1,0:T(8,128)S(1)} %pad_maximum_fusion.5.refs_2_, ...), custom_call_target="tpu_custom_call" | custom-call | flops 800000000 | tf_op jit(solution)/shard_map/place_weight_grad/pallas_call | solution.py:249
  (80 shorter events, 7.8 us)
Async XLA Ops:
  0.6 2.2 %copy-start = (f32[16,32,256]{2,1,0:T(8,128)S(1)}, f32[16,32,256]{2,1,0:T(8,128)}, u32[]{:S(2)}) copy-start(f32[16,32,256]{2,1,0:T(8,128)} %param.7) | copy-start | bytes 1572868
  0.6 22.1 %copy-start.1 = (f32[1024,128]{1,0:T(8,128)S(1)}, f32[1024,128]{1,0:T(8,128)}, u32[]{:S(2)}) copy-start(f32[1024,128]{1,0:T(8,128)} %refs_7_.3) | copy-start | bytes 1572868
  1.7 2.5 %collective-permute-start = (s32[32,32]{0,1:T(8,128)S(1)}, s32[32,32]{0,1:T(8,128)S(1)}, u32[]{:S(2)}, u32[]{:S(2)}) collective-permute-start(s32[32,32]{0,1:T(8,128)S(1)} %copy.20), channel_id=1, source_target_pairs={{0,1},{1,0},{2,3},{3,2},{4,5},{5,4},{6,7},{7,6},{8,9},{9,8},{10,11... | collective-permute-start | bytes 12296 | tf_op jit(solution)/shard_map/ppermute | solution.py:262
  4.3 4.2 %collective-permute-start.1 = (s32[64,32]{0,1:T(8,128)S(1)}, s32[64,32]{0,1:T(8,128)S(1)}, u32[]{:S(2)}, u32[]{:S(2)}) collective-permute-start(s32[64,32]{0,1:T(8,128)S(1)} %pad_add_fusion), channel_id=1, source_target_pairs={{0,2},{1,3},{2,0},{3,1},{4,6},{5,7},{6,4},{7,5},{8,10},{9,11},{10,... | collective-permute-start | bytes 24584 | tf_op jit(solution)/shard_map/ppermute | solution.py:262
  8.6 7.2 %collective-permute-start.2 = (f32[32,640]{1,0:T(8,128)S(1)}, f32[32,640]{1,0:T(8,128)S(1)}, u32[]{:S(2)}, u32[]{:S(2)}) collective-permute-start(f32[32,640]{1,0:T(8,128)S(1)} %pad_maximum_fusion.6), channel_id=1, source_target_pairs={{0,8},{1,9},{2,10},{3,11},{4,12},{5,13},{6,14},{7,15},{8,0},{9,1},... | collective-permute-start | bytes 245768 | tf_op jit(solution)/shard_map/ppermute | solution.py:262
  15.8 5.4 %collective-permute-start.3 = (f32[64,640]{1,0:T(8,128)S(1)}, f32[64,640]{1,0:T(8,128)S(1)}, u32[]{:S(2)}, u32[]{:S(2)}) collective-permute-start(f32[64,640]{1,0:T(8,128)S(1)} %pad_maximum_fusion.3), channel_id=1, source_target_pairs={{0,4},{1,5},{2,6},{3,7},{4,0},{5,1},{6,2},{7,3},{8,12},{9,13},{10,... | collective-permute-start | bytes 491528 | tf_op jit(solution)/shard_map/ppermute | solution.py:262
  21.2 9.0 %collective-permute-start.4 = (f32[128,512]{1,0:T(8,128)S(1)}, f32[128,512]{1,0:T(8,128)S(1)}, u32[]{:S(2)}, u32[]{:S(2)}) collective-permute-start(f32[128,512]{1,0:T(8,128)S(1)} %pad_maximum_fusion.1), channel_id=1, source_target_pairs={{0,2},{1,3},{2,0},{3,1},{4,6},{5,7},{6,4},{7,5},{8,10},{9,11},{10,... | collective-permute-start | bytes 786440 | tf_op jit(solution)/shard_map/ppermute | solution.py:262
  30.1 4.5 %collective-permute-start.5 = (f32[256,512]{1,0:T(8,128)S(1)}, f32[256,512]{1,0:T(8,128)S(1)}, u32[]{:S(2)}, u32[]{:S(2)}) collective-permute-start(f32[256,512]{1,0:T(8,128)S(1)} %get-tuple-element.35), channel_id=1, source_target_pairs={{0,1},{1,0},{2,3},{3,2},{4,5},{5,4},{6,7},{7,6},{8,9},{9,8},{10,11... | collective-permute-start | bytes 1572872 | tf_op jit(solution)/shard_map/ppermute | solution.py:262
  30.2 5.1 %collective-permute-start.6 = (f32[256,512]{1,0:T(8,128)S(1)}, f32[256,512]{1,0:T(8,128)S(1)}, u32[]{:S(2)}, u32[]{:S(2)}) collective-permute-start(f32[256,512]{1,0:T(8,128)S(1)} %pad_maximum_fusion.refs_5_), channel_id=1, source_target_pairs={{0,1},{1,0},{2,3},{3,2},{4,5},{5,4},{6,7},{7,6},{8,9},{9,8},{10,11... | collective-permute-start | bytes 1572872 | tf_op jit(solution)/shard_map/ppermute | solution.py:262
  34.7 8.3 %collective-permute-start.7 = (f32[128,512]{1,0:T(8,128)S(1)}, f32[128,512]{1,0:T(8,128)S(1)}, u32[]{:S(2)}, u32[]{:S(2)}) collective-permute-start(f32[128,512]{1,0:T(8,128)S(1)} %get-tuple-element.58), channel_id=1, source_target_pairs={{0,2},{1,3},{2,0},{3,1},{4,6},{5,7},{6,4},{7,5},{8,10},{9,11},{10,... | collective-permute-start | bytes 786440 | tf_op jit(solution)/shard_map/ppermute | solution.py:262
  41.3 2.2 %collective-permute-start.8 = (f32[16,16,128]{2,1,0:T(8,128)S(1)}, f32[16,16,128]{2,1,0:T(8,128)S(1)}, u32[]{:S(2)}, u32[]{:S(2)}) collective-permute-start(f32[16,16,128]{2,1,0:T(8,128)S(1)} %get-tuple-element.49), channel_id=1, source_target_pairs={{0,1},{1,0},{2,3},{3,2},{4,5},{5,4},{6,7},{7,6},{8,9},{9,8},{10,11... | collective-permute-start | bytes 393224 | tf_op jit(solution)/shard_map/ppermute | solution.py:262
  43.1 7.2 %collective-permute-start.9 = (f32[64,512]{1,0:T(8,128)S(1)}, f32[64,512]{1,0:T(8,128)S(1)}, u32[]{:S(2)}, u32[]{:S(2)}) collective-permute-start(f32[64,512]{1,0:T(8,128)S(1)} %get-tuple-element.60), channel_id=1, source_target_pairs={{0,4},{1,5},{2,6},{3,7},{4,0},{5,1},{6,2},{7,3},{8,12},{9,13},{10,... | collective-permute-start | bytes 393224 | tf_op jit(solution)/shard_map/ppermute | solution.py:262
  43.6 10.0 %collective-permute-start.19 = (f32[8,16,128]{2,1,0:T(8,128)S(1)}, f32[8,16,128]{2,1,0:T(8,128)S(1)}, u32[]{:S(2)}, u32[]{:S(2)}) collective-permute-start(f32[8,16,128]{2,1,0:T(8,128)S(1)} %get-tuple-element.62), channel_id=1, source_target_pairs={{0,2},{1,3},{2,0},{3,1},{4,6},{5,7},{6,4},{7,5},{8,10},{9,11},{10,... | collective-permute-start | bytes 196616 | tf_op jit(solution)/shard_map/ppermute | solution.py:262
  50.1 24.1 %copy-start.2 = (f32[256,32]{0,1:T(8,128)S(1)}, f32[256,32]{0,1:T(8,128)}, u32[]{:S(2)}) copy-start(f32[256,32]{0,1:T(8,128)} %param.11) | copy-start | bytes 98308
  50.1 24.1 %copy-start.3 = (f32[256,32]{0,1:T(8,128)S(1)}, f32[256,32]{0,1:T(8,128)}, u32[]{:S(2)}) copy-start(f32[256,32]{0,1:T(8,128)} %param.10) | copy-start | bytes 98308
  50.2 4.1 %collective-permute-start.11 = (f32[16,16,128]{2,1,0:T(8,128)S(1)}, f32[16,16,128]{2,1,0:T(8,128)S(1)}, u32[]{:S(2)}, u32[]{:S(2)}) collective-permute-start(f32[16,16,128]{2,1,0:T(8,128)S(1)} %get-tuple-element.54), channel_id=1, source_target_pairs={{0,1},{1,0},{2,3},{3,2},{4,5},{5,4},{6,7},{7,6},{8,9},{9,8},{10,11... | collective-permute-start | bytes 393224 | tf_op jit(solution)/shard_map/ppermute | solution.py:262
  50.3 7.6 %collective-permute-start.10 = (f32[32,512]{1,0:T(8,128)S(1)}, f32[32,512]{1,0:T(8,128)S(1)}, u32[]{:S(2)}, u32[]{:S(2)}) collective-permute-start(f32[32,512]{1,0:T(8,128)S(1)} %slice_add_fusion.6), channel_id=1, source_target_pairs={{0,8},{1,9},{2,10},{3,11},{4,12},{5,13},{6,14},{7,15},{8,0},{9,1},... | collective-permute-start | bytes 196616 | tf_op jit(solution)/shard_map/ppermute | solution.py:262
  53.6 7.0 %collective-permute-start.20 = (f32[8,16,128]{2,1,0:T(8,128)S(1)}, f32[8,16,128]{2,1,0:T(8,128)S(1)}, u32[]{:S(2)}, u32[]{:S(2)}) collective-permute-start(f32[8,16,128]{2,1,0:T(8,128)S(1)} %add.85), channel_id=1, source_target_pairs={{0,4},{1,5},{2,6},{3,7},{4,0},{5,1},{6,2},{7,3},{8,12},{9,13},{10,... | collective-permute-start | bytes 196616 | tf_op jit(solution)/shard_map/ppermute | solution.py:262
  54.3 8.0 %collective-permute-start.12 = (f32[8,16,128]{2,1,0:T(8,128)S(1)}, f32[8,16,128]{2,1,0:T(8,128)S(1)}, u32[]{:S(2)}, u32[]{:S(2)}) collective-permute-start(f32[8,16,128]{2,1,0:T(8,128)S(1)} %slice_add_fusion.5), channel_id=1, source_target_pairs={{0,2},{1,3},{2,0},{3,1},{4,6},{5,7},{6,4},{7,5},{8,10},{9,11},{10,... | collective-permute-start | bytes 196616 | tf_op jit(solution)/shard_map/ppermute | solution.py:262
  59.1 4.3 %collective-permute-start.15 = (f32[64,256]{1,0:T(8,128)S(1)}, f32[64,256]{1,0:T(8,128)S(1)}, u32[]{:S(2)}, u32[]{:S(2)}) collective-permute-start(f32[64,256]{1,0:T(8,128)S(1)} %convolution_bitcast_fusion), channel_id=1, source_target_pairs={{0,2},{1,3},{2,0},{3,1},{4,6},{5,7},{6,4},{7,5},{8,10},{9,11},{10,... | collective-permute-start | bytes 196616 | tf_op jit(solution)/shard_map/ppermute | solution.py:262
  60.6 5.4 %collective-permute-start.21 = (f32[8,16,128]{2,1,0:T(8,128)S(1)}, f32[8,16,128]{2,1,0:T(8,128)S(1)}, u32[]{:S(2)}, u32[]{:S(2)}) collective-permute-start(f32[8,16,128]{2,1,0:T(8,128)S(1)} %add.86), channel_id=1, source_target_pairs={{0,8},{1,9},{2,10},{3,11},{4,12},{5,13},{6,14},{7,15},{8,0},{9,1},... | collective-permute-start | bytes 196616 | tf_op jit(solution)/shard_map/ppermute | solution.py:262
  62.3 4.9 %collective-permute-start.13 = (f32[8,16,128]{2,1,0:T(8,128)S(1)}, f32[8,16,128]{2,1,0:T(8,128)S(1)}, u32[]{:S(2)}, u32[]{:S(2)}) collective-permute-start(f32[8,16,128]{2,1,0:T(8,128)S(1)} %fusion.1), channel_id=1, source_target_pairs={{0,4},{1,5},{2,6},{3,7},{4,0},{5,1},{6,2},{7,3},{8,12},{9,13},{10,... | collective-permute-start | bytes 196616 | tf_op jit(solution)/shard_map/ppermute | solution.py:262
  63.4 5.4 %collective-permute-start.16 = (f32[64,256]{1,0:T(8,128)S(1)}, f32[64,256]{1,0:T(8,128)S(1)}, u32[]{:S(2)}, u32[]{:S(2)}) collective-permute-start(f32[64,256]{1,0:T(8,128)S(1)} %add.81), channel_id=1, source_target_pairs={{0,4},{1,5},{2,6},{3,7},{4,0},{5,1},{6,2},{7,3},{8,12},{9,13},{10,... | collective-permute-start | bytes 196616 | tf_op jit(solution)/shard_map/ppermute | solution.py:262
  66.0 4.3 %collective-permute-start.22 = (f32[8,16,128]{2,1,0:T(8,128)S(1)}, f32[8,16,128]{2,1,0:T(8,128)S(1)}, u32[]{:S(2)}, u32[]{:S(2)}) collective-permute-start(f32[8,16,128]{2,1,0:T(8,128)S(1)} %add.87), channel_id=1, source_target_pairs={{0,2},{1,3},{2,0},{3,1},{4,6},{5,7},{6,4},{7,5},{8,10},{9,11},{10,... | collective-permute-start | bytes 196616 | tf_op jit(solution)/shard_map/ppermute | solution.py:262
  67.2 6.2 %collective-permute-start.14 = (f32[8,16,128]{2,1,0:T(8,128)S(1)}, f32[8,16,128]{2,1,0:T(8,128)S(1)}, u32[]{:S(2)}, u32[]{:S(2)}) collective-permute-start(f32[8,16,128]{2,1,0:T(8,128)S(1)} %add.79), channel_id=1, source_target_pairs={{0,8},{1,9},{2,10},{3,11},{4,12},{5,13},{6,14},{7,15},{8,0},{9,1},... | collective-permute-start | bytes 196616 | tf_op jit(solution)/shard_map/ppermute | solution.py:262
  68.8 5.4 %collective-permute-start.17 = (f32[64,256]{1,0:T(8,128)S(1)}, f32[64,256]{1,0:T(8,128)S(1)}, u32[]{:S(2)}, u32[]{:S(2)}) collective-permute-start(f32[64,256]{1,0:T(8,128)S(1)} %add.82), channel_id=1, source_target_pairs={{0,8},{1,9},{2,10},{3,11},{4,12},{5,13},{6,14},{7,15},{8,0},{9,1},... | collective-permute-start | bytes 196616 | tf_op jit(solution)/shard_map/ppermute | solution.py:262
  70.4 8.1 %collective-permute-start.23 = (f32[16,16,128]{2,1,0:T(8,128)S(1)}, f32[16,16,128]{2,1,0:T(8,128)S(1)}, u32[]{:S(2)}, u32[]{:S(2)}) collective-permute-start(f32[16,16,128]{2,1,0:T(8,128)S(1)} %pad_maximum_fusion.4.refs_0_), channel_id=1, source_target_pairs={{0,1},{1,0},{2,3},{3,2},{4,5},{5,4},{6,7},{7,6},{8,9},{9,8},{10,11... | collective-permute-start | bytes 393224 | tf_op jit(solution)/shard_map/ppermute | solution.py:262
  73.3 4.3 %collective-permute-start.24 = (f32[8,16,128]{2,1,0:T(8,128)S(1)}, f32[8,16,128]{2,1,0:T(8,128)S(1)}, u32[]{:S(2)}, u32[]{:S(2)}) collective-permute-start(f32[8,16,128]{2,1,0:T(8,128)S(1)} %add.80), channel_id=1, source_target_pairs={{0,2},{1,3},{2,0},{3,1},{4,6},{5,7},{6,4},{7,5},{8,10},{9,11},{10,... | collective-permute-start | bytes 196616 | tf_op jit(solution)/shard_map/ppermute | solution.py:262
  74.2 3.6 %collective-permute-start.18 = (f32[64,256]{1,0:T(8,128)S(1)}, f32[64,256]{1,0:T(8,128)S(1)}, u32[]{:S(2)}, u32[]{:S(2)}) collective-permute-start(f32[64,256]{1,0:T(8,128)S(1)} %add.83), channel_id=1, source_target_pairs={{0,1},{1,0},{2,3},{3,2},{4,5},{5,4},{6,7},{7,6},{8,9},{9,8},{10,11... | collective-permute-start | bytes 196616 | tf_op jit(solution)/shard_map/ppermute | solution.py:262
  77.7 1.4 %collective-permute-start.25 = (f32[16,16,128]{2,1,0:T(8,128)S(1)}, f32[16,16,128]{2,1,0:T(8,128)S(1)}, u32[]{:S(2)}, u32[]{:S(2)}) collective-permute-start(f32[16,16,128]{2,1,0:T(8,128)S(1)} %pad_maximum_fusion.5.refs_2_), channel_id=1, source_target_pairs={{0,1},{1,0},{2,3},{3,2},{4,5},{5,4},{6,7},{7,6},{8,9},{9,8},{10,11... | collective-permute-start | bytes 393224 | tf_op jit(solution)/shard_map/ppermute | solution.py:262
